TPU v7x, 128 devices: a whole 4x4x4 slice. The times are simulated.
128 devices in a mesh: group: 4 (over z), shard: 32 (over x, y, core).
Axes of the slice: x: 4, y: 4, z: 4, core: 2. Of those that a mesh axis runs over, the one named last changes fastest.
Arguments:
- embeddings: bfloat16 [49152, 768], P(('group', 'shard')), may hold values from -0.21875 to 0.21875
- members: int32 [49152], P(('group', 'shard')), may hold values from 0 to 8191, as said below
- counts: int32 [4, 32], replicated, may hold values from 96 to 384
Outputs:
- row_potential: float32 [49152], P(('group', 'shard'))
- col_potential: float32 [49152], P(('group', 'shard'))
- coarse_potential: float32 [8192], P(('group', 'shard'))
Inputs may be any that keep to these rules, and one draw needn't show every extreme that they name: `members`: tracklets of shard index s (block b with b % 32 = s) name prototypes (k // (256 // 4)) * 32 * (256 // 4) + s * (256 // 4) + k % (256 // 4) for k below 256; every prototype is named by a tracklet at row r < 256 // 4 of some block.
All inputs are finite; a program needn't handle non-finite values.
Results may differ from a plain program's by a relative error of at most 0.0065.
Values may be sent and summed in bfloat16 or wider, within the bound.
No kernel may reach another device: no remote copies, remote signals or barrier semaphores. Data moves between devices by JAX's collectives and lax.ppermute only.
A program may use at most 128 MiB of HBM per device.

v0:
```python
import math

import jax
import jax.numpy as jnp
from jax import lax
from jax.experimental import pallas as pl
from jax.experimental.pallas import tpu as pltpu
from jax.sharding import Mesh, PartitionSpec as P


PROTO_BLOCK = 256
EPS = 0.01
SC = math.log2(math.e) / EPS
NEG = -1e30
LOW, HIGH, PEAK = 2.0 ** -25, 2.0 ** 120, 2.0 ** 64
STEP = 256
F32 = jnp.float32
BF16 = jnp.bfloat16
MIB = 2 ** 20
X, Y, Z = 4, 4, 4
PAD = 128

VMEM = pl.BlockSpec(memory_space=pltpu.VMEM)
SMEM = pl.BlockSpec(memory_space=pltpu.SMEM)
ANY = pl.BlockSpec(memory_space=pl.ANY)


HBM = pltpu.MemorySpace.HBM
IN_HBM = pl.BlockSpec(memory_space=HBM)


def call(body, out_shape, in_specs, scratch=(), out_specs=None, limit=6, name=None, flops=0, nbytes=0):
    return pl.pallas_call(
        body,
        out_shape=out_shape,
        in_specs=in_specs,
        out_specs=out_specs or jax.tree.map(lambda _: VMEM, out_shape),
        scratch_shapes=list(scratch),
        compiler_params=pltpu.CompilerParams(vmem_limit_bytes=limit * MIB),
        cost_estimate=pl.CostEstimate(flops=flops, bytes_accessed=nbytes, transcendentals=0),
        name=name,
    )


def sds(shape, dtype=F32):
    return jax.ShapeDtypeStruct(shape, dtype)


def iota(shape, dim):
    return lax.broadcasted_iota(jnp.int32, shape, dim)


def to_lanes(col):
    n = col.shape[0]
    eye = iota((128, 128), 0) == iota((128, 128), 1)
    return jnp.concatenate(
        [
            jnp.sum(jnp.where(eye, col[k * 128:(k + 1) * 128], 0.0), axis=0, keepdims=True)
            for k in range(n // 128)
        ],
        axis=0,
    )


def to_rows(vals, out_ref):
    for k in range(vals.shape[0]):
        out_ref[k * 128:(k + 1) * 128, :] = jnp.transpose(
            jnp.broadcast_to(vals[k:k + 1, :], (128, 128))
        )


def lse2(parts):
    top = parts[0]
    for p in parts[1:]:
        top = jnp.maximum(top, p)
    total = jnp.exp2(parts[0] - top)
    for p in parts[1:]:
        total = total + jnp.exp2(p - top)
    return top + jnp.log2(total)


def in_range(total, peak):
    outside = jnp.sum(jnp.where((total > LOW) & (total < HIGH), 0.0, 1.0))
    return (outside == 0.0) & (peak <= PEAK)


def spread(vals, wide_ref):
    for k in range(vals.shape[0]):
        wide_ref[:, k * 128:(k + 1) * 128] = jnp.broadcast_to(vals[k:k + 1, :], (8, 128))


def store_lse(total, shift, peak, out_ref, safe):
    n = total.shape[0]
    good = in_range(total, peak)

    @pl.when(good)
    def _():
        out_ref[0:n, :] = jnp.log2(total) + shift

    @pl.when(jnp.logical_not(good))
    def _():
        safe()


def reduce_columns(tile, h, guard, out_ref, wide_ref, backup, live=None):
    rows, cols = tile.shape
    shift = jnp.max(h)
    spread(jnp.exp2(h - shift), wide_ref)
    lane, sub = iota((8, 128), 1), iota((8, 128), 0)

    def body(r, _):
        acc = jnp.zeros((8, 128), F32)
        for g in range(16):
            s = tile[pl.ds(pl.multiple_of(r * 128 + g * 8, 8), 8), :] * wide_ref[...]
            part = jnp.sum(s, axis=1, keepdims=True)
            acc = acc + jnp.where(lane == sub + 8 * g, part, 0.0)
        out_ref[pl.ds(r, 1), :] = jnp.sum(acc, axis=0, keepdims=True)
        return 0

    lax.fori_loop(0, rows // 128, body, 0, unroll=4)
    total = out_ref[0:rows // 128, :]
    if live is not None:
        total = jnp.where(live[...] > 0.0, total, 1.0)
    store_lse(total, shift, jnp.max(guard[...]), out_ref, lambda: safe_columns(backup, h, out_ref, wide_ref))


def reduce_rows(tile, h, guard, out_ref, tall_ref, backup):
    rows, cols = tile.shape
    shift = jnp.max(h)
    to_rows(jnp.exp2(h - shift), tall_ref)
    width, chunk = 512, 64
    groups = width // 128
    for strip in range(cols // width):
        at = pl.ds(strip * width, width)

        def body(c, acc):
            part = pl.ds(pl.multiple_of(c * chunk, chunk), chunk)
            s = tile[part, at] * jnp.concatenate([tall_ref[part, :]] * groups, axis=1)
            return acc + jnp.sum(s.reshape(chunk // 8, 8, width), axis=0)

        acc = lax.fori_loop(0, rows // chunk, body, jnp.zeros((8, width), F32), unroll=2)
        acc = jnp.sum(acc, axis=0, keepdims=True)
        for k in range(groups):
            row = strip * groups + k
            out_ref[row:row + 1, :] = acc[:, k * 128:(k + 1) * 128]
    store_lse(
        out_ref[0:cols // 128, :], shift, jnp.max(guard[...]), out_ref,
        lambda: safe_rows(backup, h, out_ref, tall_ref),
    )


def block_scores(backup, ci, cj):
    rows_hbm, cols_hbm, own, a_buf, b_buf, sem = backup
    for src, at, buf in ((rows_hbm, ci, a_buf), (cols_hbm, cj, b_buf)):
        copy = pltpu.make_async_copy(src.at[pl.ds(pl.multiple_of(at * STEP, STEP), STEP)], buf, sem)
        copy.start()
        copy.wait()
    s = dot_t(a_buf[...], b_buf[...])
    i, j = iota((STEP, STEP), 0) + ci * STEP, iota((STEP, STEP), 1) + cj * STEP
    return jnp.where((i == j) & (j < own), NEG, s)


def safe_columns(backup, h, out_ref, wide_ref):
    n, m = backup[0].shape[0] // STEP, backup[1].shape[0] // STEP
    spread(h, wide_ref)

    def by_rows(ci, _):
        def by_cols(cj, carry):
            top, total = carry
            s = block_scores(backup, ci, cj)
            s = s + wide_ref[0:1, pl.ds(pl.multiple_of(cj * STEP, STEP), STEP)]
            now = jnp.maximum(top, jnp.max(s, axis=1, keepdims=True))
            return now, total * jnp.exp2(top - now) + jnp.sum(jnp.exp2(s - now), axis=1, keepdims=True)

        top, total = lax.fori_loop(
            0, m, by_cols, (jnp.full((STEP, 1), NEG, F32), jnp.zeros((STEP, 1), F32))
        )
        lanes = to_lanes(jnp.broadcast_to(top + jnp.log2(total), (STEP, 128)))
        for k in range(STEP // 128):
            out_ref[pl.ds(ci * (STEP // 128) + k, 1), :] = lanes[k:k + 1, :]
        return 0

    lax.fori_loop(0, n, by_rows, 0)


def safe_rows(backup, h, out_ref, tall_ref):
    n, m = backup[0].shape[0] // STEP, backup[1].shape[0] // STEP
    to_rows(h, tall_ref)

    def by_cols(cj, _):
        def by_rows(ci, carry):
            top, total = carry
            add = tall_ref[pl.ds(pl.multiple_of(ci * STEP, STEP), STEP), :]
            s = block_scores(backup, ci, cj) + jnp.concatenate([add] * (STEP // 128), axis=1)
            now = jnp.maximum(top, jnp.max(s, axis=0, keepdims=True))
            return now, total * jnp.exp2(top - now) + jnp.sum(jnp.exp2(s - now), axis=0, keepdims=True)

        top, total = lax.fori_loop(
            0, n, by_rows, (jnp.full((1, STEP), NEG, F32), jnp.zeros((1, STEP), F32))
        )
        lse = top + jnp.log2(total)
        for k in range(STEP // 128):
            out_ref[pl.ds(cj * (STEP // 128) + k, 1), :] = lse[:, k * 128:(k + 1) * 128]
        return 0

    lax.fori_loop(0, m, by_cols, 0)


def info_place(info):
    return info[Z, 0], info[Z, 1], info[Z, 2], info[Z, 3]


def count_at(counts, z, x, y, c):
    return counts[z, (x * Y + y) * 2 + c]


def behind(at, c, k, n):
    return lax.rem(at + jnp.where(c == 0, n - k, k), n)


def row_counts(counts, idx):
    z, x, y, c = idx
    return [
        count_at(counts, z, x, behind(y, (c + dc) % 2, k, Y), (c + dc) % 2) for dc in range(2) for k in range(Y)
    ]


def col_counts(counts, idx):
    z, x, y, c = idx
    return [count_at(counts, z, behind(x, c, k, X), y, c) for k in range(X)]


def live_mask(block_counts, per):
    at = iota((per, 128), 0) * 128 + iota((per, 128), 1)
    return jnp.concatenate([jnp.where(at < n, 1.0, 0.0) for n in block_counts], axis=0)


def log2_of(n):
    return jnp.log2(jnp.full((1, 128), n, jnp.int32).astype(F32))


def from_columns(parts, first, per):
    blocks = []
    for j in range(X):
        rows = [first + (j - k) % X * per for k in range(X)]
        blocks.append(lse2([p[r:r + per, :] for p, r in zip(parts, rows)]))
    return jnp.concatenate(blocks, axis=0)


def gather_columns(parts, first, per):
    return jnp.concatenate([p[first:first + per, :] for p in parts], axis=0)


def fold_y(parts, first, per):
    blocks = []
    for dc in range(2):
        for j in range(Y):
            rows = [first + (dc * Y + (j - k if dc == 0 else j + k) % Y) * per for k in range(Y)]
            blocks.append(lse2([p[r:r + per, :] for p, r in zip(parts, rows)]))
    return jnp.concatenate(blocks, axis=0)


def fold_core(mine, other, first, per):
    half = Y * per
    return jnp.concatenate(
        [
            lse2([mine[first:first + half, :], other[first + half:first + 2 * half, :]]),
            lse2([mine[first + half:first + 2 * half, :], other[first:first + half, :]]),
        ],
        axis=0,
    )


def pool_kernel(info, emb, members, keep, send, live_rows, live_cols, seat, logs):
    idx = info_place(info)
    z, x, y, c = idx
    quarter = PROTO_BLOCK // Z
    per = members.shape[0]
    ids = members[...]
    which = lax.shift_right_logical(ids, 11)
    within = jnp.bitwise_and(ids, quarter - 1)
    turn = jnp.bitwise_xor(which, z)
    seat[...] = (turn * quarter + within).astype(F32)
    slot = jnp.where(turn == 0, 0, jnp.where(turn == 3, 1, turn + 1)) * quarter + within
    local = jnp.concatenate([slot[k:k + 1, :] for k in range(per)], axis=1)
    rows, d = emb.shape
    live = iota((1, rows), 1) < count_at(info, z, x, y, c)
    hot = ((iota((PROTO_BLOCK, rows), 0) == local) & live).astype(BF16)
    sums = jnp.dot(hot, emb[...], preferred_element_type=F32)
    sizes = jnp.dot(hot, jnp.ones((rows, PAD), BF16), preferred_element_type=F32)
    half = 2 * quarter
    keep[:, 0:d] = sums[0:half]
    keep[:, d:] = sizes[0:half]
    send[:, 0:d] = sums[half:]
    send[:, d:] = sizes[half:]
    live_rows[...] = live_mask(row_counts(info, idx), per)
    live_cols[...] = live_mask(col_counts(info, idx), per)
    mine, total = 0, 0
    for g in range(Z):
        n = info[g, 0]
        for s in range(1, X * Y * 2):
            n = n + info[g, s]
        mine = mine + jnp.where(g == z, n, 0)
        total = total + n
    logs[...] = jnp.concatenate([log2_of(mine), log2_of(total), jnp.zeros((6, 128), F32)], axis=0)


def code_sizes(sizes):
    high = jnp.floor(sizes * (1.0 / 256.0))
    low = sizes - 256.0 * high
    return jnp.where(iota(sizes.shape, 1) < 64, high, low).astype(BF16)


def read_sizes(block, d):
    coded = block[:, d:].astype(F32)
    return coded[:, 0:1] * 256.0 + coded[:, 64:65]


def pool2_kernel(mine, got, keep, send):
    quarter = mine.shape[0] // 2
    keep[...] = mine[0:quarter, :] + got[0:quarter, :]
    send[...] = mine[quarter:, :] + got[quarter:, :]


def means_kernel(mine, got, out):
    d = mine.shape[1] - PAD
    sums = mine[...] + got[...]
    sizes = sums[:, d:]
    out[:, 0:d] = (sums[:, 0:d] / sizes[:, 0:1]).astype(BF16)
    out[:, d:] = code_sizes(sizes)


def join_kernel(logs, p0, p1, p2, p3, means, plog):
    quarter, width = p0.shape
    d = width - PAD
    sizes = []
    for k, ref in enumerate((p0, p1, p2, p3)):
        block = ref[...]
        means[k * quarter:(k + 1) * quarter, :] = block[:, 0:d]
        sizes.append(jnp.broadcast_to(read_sizes(block, d), (quarter, 128)))
    plog[...] = jnp.zeros(plog.shape, F32)
    plog[0:2, :] = jnp.log2(to_lanes(jnp.concatenate(sizes, axis=0))) - logs[1:2, :]


def fetch(row_blocks, col_blocks, rows_buf, cols_buf, row_sems, col_sems):
    size = row_blocks[0].shape[0]

    def start(blocks, buf, sems, b):
        pltpu.make_async_copy(blocks[b], buf.at[pl.ds(b * size, size)], sems.at[b]).start()

    for b in range(X):
        start(col_blocks, cols_buf, col_sems, b)
    for b in range(2 * Y):
        start(row_blocks, rows_buf, row_sems, b)

    def wait(buf, sems, b):
        into = buf.at[pl.ds(pl.multiple_of(b * size, size), size)]
        pltpu.make_async_copy(into, into, sems.at[b]).wait()

    return lambda b: wait(rows_buf, row_sems, b), lambda b: wait(cols_buf, col_sems, b)


def dot_t(a, b):
    return lax.dot_general(a, b, (((1,), (1,)), ((), ())), preferred_element_type=F32) * SC


def fill_tile(tile, size, waits, rows_buf, cols_buf, rows_out, cols_out, out_sems, acc, live, sums):
    rows, cols = tile.shape
    wait_rows, wait_cols = waits
    step, wide = 2 * size, 512
    for b in range(X):
        wait_cols(b)
    save_cols = pltpu.make_async_copy(cols_buf, cols_out, out_sems.at[1])
    save_cols.start()
    if acc is not None:
        acc[...] = jnp.zeros(acc.shape, F32)

    def body(i, _):
        at = pl.ds(pl.multiple_of(i * step, step), step)
        wait_rows(2 * i)
        wait_rows(2 * i + 1)
        pltpu.make_async_copy(rows_buf.at[at], rows_out.at[at], out_sems.at[0]).start()
        for j in range(cols // wide):
            across = pl.ds(j * wide, wide)
            s = dot_t(rows_buf[at, :], cols_buf[across, :])
            if j == 0:
                col = iota((step, wide), 1)
                s = jnp.where((iota((step, wide), 0) + i * step == col) & (col < size), NEG, s)
            s = jnp.exp2(s)
            if live is not None:
                s = s * jnp.concatenate([live[at, :]] * (wide // 128), axis=1)
            tile[at, across] = s
            if acc is not None:
                acc[:, across] += jnp.sum(s.reshape(step // 8, 8, wide), axis=0)
            if sums is not None:
                part = s[:, 0:128]
                for k in range(1, wide // 128):
                    part = part + s[:, k * 128:(k + 1) * 128]
                sums[at, :] = part if j == 0 else sums[at, :] + part
        return 0

    lax.fori_loop(0, rows // step, body, 0)
    pltpu.make_async_copy(rows_buf, rows_out, out_sems.at[0]).wait()
    save_cols.wait()


def coarse_tile_kernel(own, x1, x2, x3, y1, y2, y3, s0, s1, s2, s3, plog, tile, payload, peak, rows_out, cols_out,
                       rows_buf, cols_buf, row_sems, col_sems, out_sems, sums, wide, a_buf, b_buf, sem):
    n = own.shape[0]
    waits = fetch(
        [own, y1, y2, y3, s0, s1, s2, s3], [own, x1, x2, x3], rows_buf, cols_buf, row_sems, col_sems
    )
    fill_tile(tile, n, waits, rows_buf, cols_buf, rows_out, cols_out, out_sems, None, None, sums)
    rows, cols = tile.shape
    payload[...] = jnp.zeros(payload.shape, F32)
    lane, sub = iota((8, 128), 1), iota((8, 128), 0)

    def body(r, _):
        acc = jnp.zeros((8, 128), F32)
        for g in range(16):
            s = sums[pl.ds(pl.multiple_of(r * 128 + g * 8, 8), 8), :]
            acc = acc + jnp.where(lane == sub + 8 * g, jnp.sum(s, axis=1, keepdims=True), 0.0)
        payload[pl.ds(r, 1), :] = jnp.sum(acc, axis=0, keepdims=True)
        return 0

    lax.fori_loop(0, rows // 128, body, 0, unroll=4)
    total = payload[0:rows // 128, :]
    most = jnp.max(total)
    peak[...] = jnp.full(peak.shape, most, F32)
    store_lse(
        total, 0.0, most, payload,
        lambda: safe_columns(
            (rows_out, cols_out, n, a_buf, b_buf, sem), jnp.zeros((cols // 128, 128), F32), payload, wide
        ),
    )
    payload[rows // 128:rows // 128 + 2, :] = plog[0:2, :]


def fine_tile_kernel(info, live_rows, own, x1, x2, x3, y1, y2, y3, s0, s1, s2, s3, tile, part, peak, rows_out,
                     cols_out, rows_buf, cols_buf, row_sems, col_sems, out_sems, tall, acc, a_buf, b_buf, sem):
    n = own.shape[0]
    waits = fetch(
        [own, y1, y2, y3, s0, s1, s2, s3], [own, x1, x2, x3], rows_buf, cols_buf, row_sems, col_sems
    )
    for b, count in enumerate(row_counts(info, info_place(info))):
        tall[b * n:(b + 1) * n, :] = jnp.where(iota((n, 128), 0) < count, 1.0, 0.0)
    fill_tile(tile, n, waits, rows_buf, cols_buf, rows_out, cols_out, out_sems, acc, tall, None)
    rows, cols = tile.shape
    total = jnp.sum(acc[...], axis=0, keepdims=True)
    for k in range(cols // 128):
        part[k:k + 1, :] = total[:, k * 128:(k + 1) * 128]
    h = jnp.where(live_rows[...] > 0.0, 0.0, NEG)
    most = jnp.max(total)
    peak[...] = jnp.full(peak.shape, most, F32)
    store_lse(
        part[...], 0.0, most, part,
        lambda: safe_rows((rows_out, cols_out, n, a_buf, b_buf, sem), h, part, tall),
    )


def fold_y_kernel(plan, *refs):
    parts, out = refs[0:Y], refs[Y]
    out[...] = jnp.zeros(out.shape, F32)
    for first, per in plan["lse"]:
        n = 2 * Y * per
        out[first:first + n, :] = fold_y(parts, first, per)
    if plan["plog"] is not None:
        first, into = plan["plog"]
        out[into:into + 2 * Y, :] = jnp.concatenate(
            [p[first:first + 2, :] for p in parts], axis=0
        )


def coarse2_kernel(mine, other, part, plog, seat, tile, peak, rows_hbm, cols_hbm, payload, plog_rows, tall, *bufs):
    plog_rows[0:8, :] = mine[16:24, :]
    plog_rows[8:16, :] = other[16:24, :]
    h = plog_rows[...] + SC - fold_core(mine, other, 0, 2)
    payload[...] = jnp.zeros(payload.shape, F32)
    reduce_rows(tile, h, peak, payload, tall, (rows_hbm, cols_hbm, PROTO_BLOCK, *bufs))
    payload[8:20, :] = part[...]
    payload[20:22, :] = plog[0:2, :]
    payload[22:25, :] = seat[...]


def fine_h(lse, logs, live, boost=0.0):
    return jnp.where(live[...] > 0.0, SC - logs[0:1, :] - lse + boost, NEG)


def step3_kernel(logs, live_rows, live_cols, p0, p1, p2, p3, ktile, kpeak, krows, kcols, tile, peak, rows_hbm, cols_hbm,
                 payload, plog_cols, seats, wide, kwide, *bufs):
    parts = (p0, p1, p2, p3)
    plog_cols[...] = gather_columns(parts, 20, 2)
    seats[...] = gather_columns(parts, 22, 3)
    payload[...] = jnp.zeros(payload.shape, F32)
    h = fine_h(from_columns(parts, 8, 3), logs, live_cols)
    backup = (rows_hbm, cols_hbm, tile.shape[1] // X, *bufs)
    reduce_columns(tile, h, peak, payload.at[16:40, :], wide, backup, live_rows)
    h = plog_cols[...] + SC - from_columns(parts, 0, 2)
    reduce_columns(ktile, h, kpeak, payload.at[0:16, :], kwide, (krows, kcols, PROTO_BLOCK, *bufs))


def step4_kernel(logs, live_rows, mine, other, plog_rows, ktile, kpeak, krows, kcols, tile, peak, rows_hbm, cols_hbm,
                 payload, tall, ktall, *bufs):
    payload[...] = jnp.zeros(payload.shape, F32)
    h = plog_rows[...] + SC - fold_core(mine, other, 0, 2)
    reduce_rows(ktile, h, kpeak, payload.at[0:8, :], ktall, (krows, kcols, PROTO_BLOCK, *bufs))
    h = fine_h(fold_core(mine, other, 16, 3), logs, live_rows)
    backup = (rows_hbm, cols_hbm, tile.shape[1] // X, *bufs)
    reduce_rows(tile, h, peak, payload.at[8:20, :], tall, backup)


def step5_kernel(logs, live_rows, live_cols, p0, p1, p2, p3, plog_cols, seats, tile, peak, rows_hbm, cols_hbm,
                 payload, coarse, tall, wide, *bufs):
    parts = (p0, p1, p2, p3)
    v = plog_cols[...] + SC - from_columns(parts, 0, 2)
    coarse[...] = v[0:1, :] * (1.0 / SC)
    to_rows(v, tall)
    local = seats[...].astype(jnp.int32)
    boost = []
    for k in range(X * 3):
        vals = tall[(k // 3) * PROTO_BLOCK:(k // 3 + 1) * PROTO_BLOCK, :]
        pick = iota((PROTO_BLOCK, 128), 0) == local[k:k + 1, :]
        boost.append(jnp.sum(jnp.where(pick, vals, 0.0), axis=0, keepdims=True))
    h = fine_h(from_columns(parts, 8, 3), logs, live_cols, jnp.concatenate(boost, axis=0))
    payload[...] = jnp.zeros(payload.shape, F32)
    reduce_columns(tile, h, peak, payload, wide, (rows_hbm, cols_hbm, tile.shape[1] // X, *bufs), live_rows)


def potential(h):
    return jnp.where(h == NEG, 0.0, h)[0:3, :] * (1.0 / SC)


def step6_kernel(logs, live_rows, mine, other, tile, peak, rows_hbm, cols_hbm, payload, out, tall, *bufs):
    h = fine_h(fold_core(mine, other, 0, 3), logs, live_rows)
    out[...] = potential(h)
    payload[...] = jnp.zeros(payload.shape, F32)
    backup = (rows_hbm, cols_hbm, tile.shape[1] // X, *bufs)
    reduce_rows(tile, h, peak, payload, tall, backup)


def last_kernel(logs, live_cols, p0, p1, p2, p3, out):
    out[...] = potential(fine_h(from_columns((p0, p1, p2, p3), 0, 3), logs, live_cols))


def swap(v, axis, bit):
    n = {"z": Z, "c": 2}[axis]
    return lax.ppermute(v, axis, [(i, i ^ bit) for i in range(n)])


def turn(v, axis, k):
    n = {"x": X, "y": Y}[axis]
    return lax.ppermute(
        v, (axis, "c"), [(i * 2 + c, (i + (k if c == 0 else n - k)) % n * 2 + c) for i in range(n) for c in range(2)]
    )


def spread_over(v, axis):
    return [v] + [turn(v, axis, k) for k in (1, 2, 3)]


def vmem(v):
    return pltpu.with_memory_space_constraint(v, pltpu.VMEM)


def held(tile, peak, rows, cols):
    return [vmem(tile), peak, *[pltpu.with_memory_space_constraint(v, HBM) for v in (rows, cols)]]


def local(embeddings, members, counts):
    rows, d = embeddings.shape
    here = jnp.stack([lax.axis_index(a) for a in ("z", "x", "y", "c")]).astype(jnp.int32)
    info = jnp.concatenate([counts, jnp.pad(here[None], ((0, 0), (0, counts.shape[1] - 4)))], axis=0)
    per = rows // 128
    n_rows, n_cols = rows * Y * 2, rows * X
    k_rows, k_cols = PROTO_BLOCK * Y * 2, PROTO_BLOCK * X
    quarter = PROTO_BLOCK // Z
    width = d + PAD

    def first(own):
        return turn(own, "x", 1), turn(own, "x", 3), turn(own, "y", 1), turn(own, "y", 3)

    x1, x3, y1, y3 = first(embeddings)
    keep, send, live_rows, live_cols, seat, logs = call(
        pool_kernel,
        [
            sds((2 * quarter, width)), sds((2 * quarter, width)), sds((n_rows // 128, 128)),
            sds((n_cols // 128, 128)), sds((per, 128)), sds((8, 128)),
        ],
        [SMEM, VMEM, VMEM],
        name="pool",
    )(info, embeddings, members.reshape(per, 128))
    keep, send = call(
        pool2_kernel, [sds((quarter, width)), sds((quarter, width))], [VMEM] * 2, name="pool2"
    )(keep, swap(send, "z", 1))
    got = swap(send, "z", 3)
    x1, x3, y1, y3, got = lax.optimization_barrier((x1, x3, y1, y3, got))
    x2, y2 = turn(x1, "x", 1), turn(y1, "y", 1)
    part = call(means_kernel, sds((quarter, width), BF16), [VMEM] * 2, name="means")(keep, got)
    far = [swap(part, "z", k) for k in (1, 2, 3)]
    x1, y1, y3, x2, y2, embeddings, far = lax.optimization_barrier((x1, y1, y3, x2, y2, embeddings, far))
    means, plog = call(
        join_kernel, [sds((PROTO_BLOCK, d), BF16), sds((8, 128))], [VMEM] * 5, name="join"
    )(logs, part, *far)
    s0, s1, s2, s3 = [swap(v, "c", 1) for v in (embeddings, y1, y2, y3)]
    vectors = [embeddings, x1, x2, x3, y1, y2, y3, s0, s1, s2, s3]

    bufs = [pltpu.VMEM((STEP, d), BF16), pltpu.VMEM((STEP, d), BF16), pltpu.SemaphoreType.DMA]

    def tile_call(body, n, m, part_rows, specs, extra, name):
        out = [pltpu.VMEM((n, m), F32), sds((part_rows, 128)), sds((8, 128)), HBM((n, d), BF16), HBM((m, d), BF16)]
        return call(
            body,
            out,
            specs,
            scratch=[
                pltpu.VMEM((n, d), BF16),
                pltpu.VMEM((m, d), BF16),
                pltpu.SemaphoreType.DMA((2 * Y,)),
                pltpu.SemaphoreType.DMA((X,)),
                pltpu.SemaphoreType.DMA((2,)),
                *extra,
                *bufs,
            ],
            out_specs=[VMEM, VMEM, VMEM, IN_HBM, IN_HBM],
            limit=18,
            name=name,
            flops=2 * n * m * d,
        )

    tall = pltpu.VMEM((n_rows, 128), F32)
    wide = pltpu.VMEM((8, n_cols), F32)
    mx1, mx3, my1, my3 = first(means)
    tile, upart, *back = tile_call(
        fine_tile_kernel, n_rows, n_cols, n_cols // 128, [SMEM, VMEM] + [ANY] * 11, [tall, wide], "fine_tile"
    )(info, live_rows, *vectors)
    upart, means, mx1, mx3, my1, my3 = lax.optimization_barrier((upart, means, mx1, mx3, my1, my3))
    mx2, my2 = turn(mx1, "x", 1), turn(my1, "y", 1)
    t0, t1, t3, t2 = swap(means, "c", 1), swap(my1, "c", 1), swap(my3, "c", 1), swap(my2, "c", 1)
    back = held(tile, *back)

    ktile, part, *kback = tile_call(
        coarse_tile_kernel, k_rows, k_cols, 24, [ANY] * 11 + [VMEM],
        [pltpu.VMEM((k_rows, 128), F32), pltpu.VMEM((8, k_cols), F32)], "coarse_tile"
    )(means, mx1, mx2, mx3, my1, my2, my3, t0, t1, t2, t3, plog)
    kback = held(ktile, *kback)
    kspecs = [VMEM, VMEM, IN_HBM, IN_HBM]
    mine = call(
        lambda *r: fold_y_kernel({"lse": [(0, 2)], "plog": (16, 16)}, *r),
        sds((24, 128)),
        [VMEM] * 4,
        name="fold_y1",
    )(*spread_over(part, "y"))
    other = swap(mine, "c", 1)

    part, plog_rows = call(
        coarse2_kernel,
        [sds((32, 128)), sds((16, 128))],
        [VMEM] * 5 + kspecs,
        scratch=[pltpu.VMEM((k_rows, 128), F32), *bufs],
        name="coarse2",
    )(mine, other, upart, plog, seat, *kback)

    part, plog_cols, seats = call(
        step3_kernel,
        [sds((40, 128)), sds((8, 128)), sds((12, 128))],
        [VMEM] * 7 + kspecs * 2,
        scratch=[wide, pltpu.VMEM((8, k_cols), F32), *bufs],
        name="step3",
    )(logs, live_rows, live_cols, *spread_over(part, "x"), *kback, *back)
    mine = call(
        lambda *r: fold_y_kernel({"lse": [(0, 2), (16, 3)], "plog": None}, *r),
        sds((40, 128)),
        [VMEM] * 4,
        name="fold_y2",
    )(*spread_over(part, "y"))
    other = swap(mine, "c", 1)

    part = call(
        step4_kernel,
        sds((24, 128)),
        [VMEM, VMEM] + [VMEM] * 3 + kspecs * 2,
        scratch=[tall, pltpu.VMEM((k_rows, 128), F32), *bufs],
        name="step4",
    )(logs, live_rows, mine, other, plog_rows, *kback, *back)

    part, coarse = call(
        step5_kernel,
        [sds((24, 128)), sds((1, 128))],
        [VMEM] * 9 + kspecs,
        scratch=[pltpu.VMEM((k_cols, 128), F32), wide, *bufs],
        name="step5",
    )(logs, live_rows, live_cols, *spread_over(part, "x"), plog_cols, seats, *back)
    mine = call(
        lambda *r: fold_y_kernel({"lse": [(0, 3)], "plog": None}, *r),
        sds((24, 128)),
        [VMEM] * 4,
        name="fold_y3",
    )(*spread_over(part, "y"))
    other = swap(mine, "c", 1)

    part, col = call(
        step6_kernel,
        [sds((16, 128)), sds((3, 128))],
        [VMEM, VMEM] + [VMEM] * 2 + kspecs,
        scratch=[tall, *bufs],
        name="step6",
    )(logs, live_rows, mine, other, *back)
    row = call(last_kernel, sds((3, 128)), [VMEM, VMEM] + [VMEM] * 4, name="last")(
        logs, live_cols, *spread_over(part, "x")
    )
    return row.reshape(rows), col.reshape(rows), coarse[0, :quarter]


def solution(mesh):
    split = Mesh(mesh.devices.reshape(Z, X, Y, 2), ("z", "x", "y", "c"))
    every = P(("z", "x", "y", "c"))
    return jax.shard_map(
        local,
        mesh=split,
        in_specs=(P(("z", "x", "y", "c"), None), every, P()),
        out_specs=(every, every, every),
        check_vma=False,
    )
```

profile of v0, /device:TPU:0, one launch (start us, length us, event | category | flops | bytes accessed | tf_op | source)
XLA Modules:
  0.0 135.3 jit_solution(7656974385370600012)
XLA Ops:
  2.1 1.5 %pool.1 = (f32[128,896]{1,0:T(8,128)S(1)}, f32[128,896]{1,0:T(8,128)S(1)}, f32[24,128]{1,0:T(8,128)S(1)}, f32[12,128]{1,0:T(8,128)S(1)}, f32[3,128]{1,0:T(4,128)S(1)}, /*index=5*/f32[8,128]{1,0:T(8,128)S(1)}) custom-call(s32[5,32]{1,0:T(8,128)S(1)} %pad_add_fusion.info, bf16[384,768]{1,0:T(8,128)(2,1)} %own, s32[3,128]{1,0:T(4,128)S(1)} %bitcast.11), custom_call_target="tpu_custom_call" | custom-call | tf_op jit(solution)/shard_map/pool/pallas_call | solution.py:583
  3.6 2.1 %collective-permute-start.4 = (f32[128,896]{1,0:T(8,128)S(1)}, f32[128,896]{1,0:T(8,128)S(1)}, u32[]{:S(2)}, u32[]{:S(2)}) collective-permute-start(f32[128,896]{1,0:T(8,128)S(1)} %get-tuple-element.56), channel_id=1, source_target_pairs={{0,32},{32,0},{64,96},{96,64},{1,33},{33,1},{65,97},{97,65},{2,34}... | collective-permute-start | bytes 1376264 | tf_op jit(solution)/shard_map/ppermute | solution.py:547
  5.7 1.6 %collective-permute-start.2 = (bf16[384,768]{1,0:T(8,128)(2,1)}, bf16[384,768]{1,0:T(8,128)(2,1)S(1)}, u32[]{:S(2)}, u32[]{:S(2)}) collective-permute-start(bf16[384,768]{1,0:T(8,128)(2,1)} %own), channel_id=1, source_target_pairs={{0,2},{1,7},{2,4},{3,1},{4,6},{5,3},{6,0},{7,5},{8,10},{9,15},{10,... | collective-permute-start | bytes 1769480 | tf_op jit(solution)/shard_map/ppermute | solution.py:552
  7.2 2.8 %collective-permute-start.1 = (bf16[384,768]{1,0:T(8,128)(2,1)}, bf16[384,768]{1,0:T(8,128)(2,1)S(1)}, u32[]{:S(2)}, u32[]{:S(2)}) collective-permute-start(bf16[384,768]{1,0:T(8,128)(2,1)} %own), channel_id=1, source_target_pairs={{0,24},{1,9},{8,0},{9,17},{16,8},{17,25},{24,16},{25,1},{2,26},{3,... | collective-permute-start | bytes 1769480 | tf_op jit(solution)/shard_map/ppermute | solution.py:552
  10.0 1.7 %collective-permute-start.3 = (bf16[384,768]{1,0:T(8,128)(2,1)}, bf16[384,768]{1,0:T(8,128)(2,1)S(1)}, u32[]{:S(2)}, u32[]{:S(2)}) collective-permute-start(bf16[384,768]{1,0:T(8,128)(2,1)} %own), channel_id=1, source_target_pairs={{0,6},{1,3},{2,0},{3,5},{4,2},{5,7},{6,4},{7,1},{8,14},{9,11},{10,... | collective-permute-start | bytes 1769480 | tf_op jit(solution)/shard_map/ppermute | solution.py:552
  11.7 4.5 %collective-permute-done.4.got = f32[128,896]{1,0:T(8,128)S(1)} collective-permute-done((f32[128,896]{1,0:T(8,128)S(1)}, f32[128,896]{1,0:T(8,128)S(1)}, u32[]{:S(2)}, u32[]{:S(2)}) %collective-permute-start.4) | collective-permute-done | bytes 458784 | tf_op jit(solution)/shard_map/ppermute | solution.py:547
  16.2 3.9 %collective-permute-start.5 = (f32[64,896]{1,0:T(8,128)S(1)}, f32[64,896]{1,0:T(8,128)S(1)}, u32[]{:S(2)}, u32[]{:S(2)}) collective-permute-start(f32[64,896]{1,0:T(8,128)S(1)} %get-tuple-element.57), channel_id=1, source_target_pairs={{0,96},{32,64},{64,32},{96,0},{1,97},{33,65},{65,33},{97,1},{2,98}... | collective-permute-start | bytes 688136 | tf_op jit(solution)/shard_map/ppermute | solution.py:547
  20.2 3.8 %collective-permute-done.1.x3 = bf16[384,768]{1,0:T(8,128)(2,1)S(1)} collective-permute-done((bf16[384,768]{1,0:T(8,128)(2,1)}, bf16[384,768]{1,0:T(8,128)(2,1)S(1)}, u32[]{:S(2)}, u32[]{:S(2)}) %collective-permute-start.1) | collective-permute-done | bytes 589856 | tf_op jit(solution)/shard_map/ppermute | solution.py:552
  24.9 1.5 %collective-permute-start.6 = (bf16[384,768]{1,0:T(8,128)(2,1)S(1)}, bf16[384,768]{1,0:T(8,128)(2,1)S(1)}, u32[]{:S(2)}, u32[]{:S(2)}) collective-permute-start(bf16[384,768]{1,0:T(8,128)(2,1)S(1)} %collective-permute-done.x1), channel_id=1, source_target_pairs={{0,8},{1,25},{8,16},{9,1},{16,24},{17,9},{24,0},{25,17},{2,10},{3,... | collective-permute-start | bytes 1769480 | tf_op jit(solution)/shard_map/ppermute | solution.py:552
  26.4 1.6 %collective-permute-start.7 = (bf16[384,768]{1,0:T(8,128)(2,1)S(1)}, bf16[384,768]{1,0:T(8,128)(2,1)S(1)}, u32[]{:S(2)}, u32[]{:S(2)}) collective-permute-start(bf16[384,768]{1,0:T(8,128)(2,1)S(1)} %collective-permute-done.2.y1), channel_id=1, source_target_pairs={{0,2},{1,7},{2,4},{3,1},{4,6},{5,3},{6,0},{7,5},{8,10},{9,15},{10,... | collective-permute-start | bytes 1769480 | tf_op jit(solution)/shard_map/ppermute | solution.py:552
  28.1 3.0 %collective-permute-start.10 = (bf16[64,896]{1,0:T(8,128)(2,1)S(1)}, bf16[64,896]{1,0:T(8,128)(2,1)S(1)}, u32[]{:S(2)}, u32[]{:S(2)}) collective-permute-start(bf16[64,896]{1,0:T(8,128)(2,1)S(1)} %means.1.p0), channel_id=1, source_target_pairs={{0,96},{32,64},{64,32},{96,0},{1,97},{33,65},{65,33},{97,1},{2,98}... | collective-permute-start | bytes 344072 | tf_op jit(solution)/shard_map/ppermute | solution.py:547
  31.1 1.1 collective-permute-start.8
  32.2 4.1 %collective-permute-done.10.p3 = bf16[64,896]{1,0:T(8,128)(2,1)S(1)} collective-permute-done((bf16[64,896]{1,0:T(8,128)(2,1)S(1)}, bf16[64,896]{1,0:T(8,128)(2,1)S(1)}, u32[]{:S(2)}, u32[]{:S(2)}) %collective-permute-start.10) | collective-permute-done | bytes 114720 | tf_op jit(solution)/shard_map/ppermute | solution.py:547
  36.3 2.3 %collective-permute-done.9.p2 = bf16[64,896]{1,0:T(8,128)(2,1)S(1)} collective-permute-done((bf16[64,896]{1,0:T(8,128)(2,1)S(1)}, bf16[64,896]{1,0:T(8,128)(2,1)S(1)}, u32[]{:S(2)}, u32[]{:S(2)}) %collective-permute-start.9) | collective-permute-done | bytes 114720 | tf_op jit(solution)/shard_map/ppermute | solution.py:547
  39.9 1.0 collective-permute-start.18
  40.9 1.1 collective-permute-start.17
  42.0 1.0 collective-permute-start.16
  43.0 1.0 collective-permute-start.15
  44.1 10.7 %fine_tile.1 = (f32[3072,1536]{1,0:T(8,128)S(1)}, f32[12,128]{1,0:T(8,128)S(1)}, f32[8,128]{1,0:T(8,128)S(1)}, bf16[3072,768]{1,0:T(8,128)(2,1)}, bf16[1536,768]{1,0:T(8,128)(2,1)}) custom-call(s32[5,32]{1,0:T(8,128)S(1)} %pad_add_fusion.info, f32[24,128]{1,0:T(8,128)S(1)} %get-tuple-element.54.live_rows, bf16[384,768]{1,0:T(8,128)(2,1)} %own, ...), custom_call_target="tpu_custom_call" | custom-call | flops 7247757312 | tf_op jit(solution)/shard_map/fine_tile/pallas_call | solution.py:633
  56.5 1.0 collective-permute-start.19
  57.4 1.2 collective-permute-start.24
  58.6 5.4 %collective-permute-done.20.y2 = bf16[256,768]{1,0:T(8,128)(2,1)S(1)} collective-permute-done((bf16[256,768]{1,0:T(8,128)(2,1)S(1)}, bf16[256,768]{1,0:T(8,128)(2,1)S(1)}, u32[]{:S(2)}, u32[]{:S(2)}) %collective-permute-start.20) | collective-permute-done | bytes 393248 | tf_op jit(solution)/shard_map/ppermute | solution.py:552
  64.0 1.5 %collective-permute-done.19.x2 = bf16[256,768]{1,0:T(8,128)(2,1)S(1)} collective-permute-done((bf16[256,768]{1,0:T(8,128)(2,1)S(1)}, bf16[256,768]{1,0:T(8,128)(2,1)S(1)}, u32[]{:S(2)}, u32[]{:S(2)}) %collective-permute-start.19) | collective-permute-done | bytes 393248 | tf_op jit(solution)/shard_map/ppermute | solution.py:552
  65.7 7.3 %coarse_tile.1 = (f32[2048,1024]{1,0:T(8,128)S(1)}, f32[24,128]{1,0:T(8,128)S(1)}, f32[8,128]{1,0:T(8,128)S(1)}, bf16[2048,768]{1,0:T(8,128)(2,1)}, bf16[1024,768]{1,0:T(8,128)(2,1)}) custom-call(bf16[256,768]{1,0:T(8,128)(2,1)S(1)} %get-tuple-element.75.own, bf16[256,768]{1,0:T(8,128)(2,1)S(1)} %collective-permute-done.15.x1, ...), custom_call_target="tpu_custom_call" | custom-call | flops 3221225472 | tf_op jit(solution)/shard_map/coarse_tile/pallas_call | solution.py:641
  73.0 2.1 %collective-permute-start.27 = (f32[24,128]{1,0:T(8,128)S(1)}, f32[24,128]{1,0:T(8,128)S(1)}, u32[]{:S(2)}, u32[]{:S(2)}) collective-permute-start(f32[24,128]{1,0:T(8,128)S(1)} %get-tuple-element.81.r_0_), channel_id=1, source_target_pairs={{0,6},{1,3},{2,0},{3,5},{4,2},{5,7},{6,4},{7,1},{8,14},{9,11},{10,... | collective-permute-start | bytes 36872 | tf_op jit(solution)/shard_map/ppermute | solution.py:552
  75.1 1.4 collective-permute-start.26
  76.8 3.5 %collective-permute-done.26.r_2_ = f32[24,128]{1,0:T(8,128)S(1)} collective-permute-done((f32[24,128]{1,0:T(8,128)S(1)}, f32[24,128]{1,0:T(8,128)S(1)}, u32[]{:S(2)}, u32[]{:S(2)}) %collective-permute-start.26) | collective-permute-done | bytes 12320 | tf_op jit(solution)/shard_map/ppermute | solution.py:552
  80.3 1.1 collective-permute-done.25.r_1_
  81.5 1.2 collective-permute-done.28.other
  82.7 1.4 %coarse2.1 = (f32[32,128]{1,0:T(8,128)S(1)}, f32[16,128]{1,0:T(8,128)S(1)}) custom-call(f32[24,128]{1,0:T(8,128)S(1)} %fold_y1.1.mine, f32[24,128]{1,0:T(8,128)S(1)} %collective-permute-done.28.other, f32[12,128]{1,0:T(8,128)S(1)} %get-tuple-element.82.part, f32[8,128]{1,0:T(8,128)S(1)} %get-tuple-element.80.plog, f32[3,128]{1,0:T(4,128)S(1)} %get-tuple-element.83.seat, ...), custom_call_target="tpu_custom_call" | custom-call | tf_op jit(solution)/shard_map/coarse2/pallas_call | solution.py:655
  86.2 1.7 %collective-permute-done.31.p3 = f32[32,128]{1,0:T(8,128)S(1)} collective-permute-done((f32[32,128]{1,0:T(8,128)S(1)}, f32[32,128]{1,0:T(8,128)S(1)}, u32[]{:S(2)}, u32[]{:S(2)}) %collective-permute-start.31) | collective-permute-done | bytes 16416 | tf_op jit(solution)/shard_map/ppermute | solution.py:552
  87.9 2.3 %collective-permute-done.30.p2 = f32[32,128]{1,0:T(8,128)S(1)} collective-permute-done((f32[32,128]{1,0:T(8,128)S(1)}, f32[32,128]{1,0:T(8,128)S(1)}, u32[]{:S(2)}, u32[]{:S(2)}) %collective-permute-start.30) | collective-permute-done | bytes 16416 | tf_op jit(solution)/shard_map/ppermute | solution.py:552
  90.6 3.3 %step3.1 = (f32[40,128]{1,0:T(8,128)S(1)}, f32[8,128]{1,0:T(8,128)S(1)}, f32[12,128]{1,0:T(8,128)S(1)}) custom-call(f32[8,128]{1,0:T(8,128)S(1)} %get-tuple-element.52.logs, f32[24,128]{1,0:T(8,128)S(1)} %get-tuple-element.54.live_rows, f32[12,128]{1,0:T(8,128)S(1)} %get-tuple-element.53.live_cols, f32[32,128]{1,0:T(8,128)S(1)} %get-tuple-element.88.p0, ...), custom_call_target="tpu_custom_call" | custom-call | tf_op jit(solution)/shard_map/step3/pallas_call | solution.py:663
  93.9 1.4 %collective-permute-start.34 = (f32[40,128]{1,0:T(8,128)S(1)}, f32[40,128]{1,0:T(8,128)S(1)}, u32[]{:S(2)}, u32[]{:S(2)}) collective-permute-start(f32[40,128]{1,0:T(8,128)S(1)} %get-tuple-element.93.r_0_), channel_id=1, source_target_pairs={{0,6},{1,3},{2,0},{3,5},{4,2},{5,7},{6,4},{7,1},{8,14},{9,11},{10,... | collective-permute-start | bytes 61448 | tf_op jit(solution)/shard_map/ppermute | solution.py:552
  97.8 2.8 %collective-permute-done.33.r_2_ = f32[40,128]{1,0:T(8,128)S(1)} collective-permute-done((f32[40,128]{1,0:T(8,128)S(1)}, f32[40,128]{1,0:T(8,128)S(1)}, u32[]{:S(2)}, u32[]{:S(2)}) %collective-permute-start.33) | collective-permute-done | bytes 20512 | tf_op jit(solution)/shard_map/ppermute | solution.py:552
  101.3 1.2 collective-permute-done.35.other
  102.5 3.9 %step4.1.p0 = f32[24,128]{1,0:T(8,128)S(1)} custom-call(f32[8,128]{1,0:T(8,128)S(1)} %get-tuple-element.52.logs, f32[24,128]{1,0:T(8,128)S(1)} %get-tuple-element.54.live_rows, f32[40,128]{1,0:T(8,128)S(1)} %fold_y2.1.mine, f32[40,128]{1,0:T(8,128)S(1)} %collective-permute-done.35.other, f32[16,128]{1,0:T(8,128)S(1)} %get-tuple-element.94.plog_rows, ...), custom_call_target="tpu_custom_call" | custom-call | tf_op jit(solution)/shard_map/step4/pallas_call | solution.py:678
  106.4 1.3 collective-permute-start.38
  108.7 1.0 collective-permute-start.36
  110.2 2.8 %collective-permute-done.37.p2 = f32[24,128]{1,0:T(8,128)S(1)} collective-permute-done((f32[24,128]{1,0:T(8,128)S(1)}, f32[24,128]{1,0:T(8,128)S(1)}, u32[]{:S(2)}, u32[]{:S(2)}) %collective-permute-start.37) | collective-permute-done | bytes 12320 | tf_op jit(solution)/shard_map/ppermute | solution.py:552
  113.6 2.4 %step5.1 = (f32[24,128]{1,0:T(8,128)S(1)}, f32[1,128]{1,0:T(1,128)S(1)}) custom-call(f32[8,128]{1,0:T(8,128)S(1)} %get-tuple-element.52.logs, f32[24,128]{1,0:T(8,128)S(1)} %get-tuple-element.54.live_rows, f32[12,128]{1,0:T(8,128)S(1)} %get-tuple-element.53.live_cols, f32[24,128]{1,0:T(8,128)S(1)} %step4.1.p0, f32[24,128]{1,0:T(8,128)S(1)} %collective-permute-done.36.p1, ...), custom_call_target="tpu_custom_call" | custom-call | tf_op jit(solution)/shard_map/step5/pallas_call | solution.py:686
  116.0 2.1 %collective-permute-start.41 = (f32[24,128]{1,0:T(8,128)S(1)}, f32[24,128]{1,0:T(8,128)S(1)}, u32[]{:S(2)}, u32[]{:S(2)}) collective-permute-start(f32[24,128]{1,0:T(8,128)S(1)} %get-tuple-element.97.r_0_), channel_id=1, source_target_pairs={{0,6},{1,3},{2,0},{3,5},{4,2},{5,7},{6,4},{7,1},{8,14},{9,11},{10,... | collective-permute-start | bytes 36872 | tf_op jit(solution)/shard_map/ppermute | solution.py:552
  119.7 3.5 %collective-permute-done.40.r_2_ = f32[24,128]{1,0:T(8,128)S(1)} collective-permute-done((f32[24,128]{1,0:T(8,128)S(1)}, f32[24,128]{1,0:T(8,128)S(1)}, u32[]{:S(2)}, u32[]{:S(2)}) %collective-permute-start.40) | collective-permute-done | bytes 12320 | tf_op jit(solution)/shard_map/ppermute | solution.py:552
  124.0 1.2 collective-permute-done.42.other
  125.2 3.1 %step6.1 = (f32[16,128]{1,0:T(8,128)S(1)}, f32[3,128]{1,0:T(4,128)}) custom-call(f32[8,128]{1,0:T(8,128)S(1)} %get-tuple-element.52.logs, f32[24,128]{1,0:T(8,128)S(1)} %get-tuple-element.54.live_rows, f32[24,128]{1,0:T(8,128)S(1)} %fold_y3.1.mine, f32[24,128]{1,0:T(8,128)S(1)} %collective-permute-done.42.other, f32[3072,1536]{1,0:T(8,128)S(1)} %get-tuple-element.89.tile, ...), custom_call_target="tpu_custom_call" | custom-call | tf_op jit(solution)/shard_map/step6/pallas_call | solution.py:701
  128.9 0.9 collective-permute-start.44
  129.8 1.3 collective-permute-start.43
  132.0 2.1 %collective-permute-done.44.p2 = f32[16,128]{1,0:T(8,128)S(1)} collective-permute-done((f32[16,128]{1,0:T(8,128)S(1)}, f32[16,128]{1,0:T(8,128)S(1)}, u32[]{:S(2)}, u32[]{:S(2)}) %collective-permute-start.44) | collective-permute-done | bytes 8224 | tf_op jit(solution)/shard_map/ppermute | solution.py:552
  (64 shorter events, 19.1 us)
Async XLA Ops:
  1.4 0.7 copy-start
  3.6 12.6 %collective-permute-start.4 = (f32[128,896]{1,0:T(8,128)S(1)}, f32[128,896]{1,0:T(8,128)S(1)}, u32[]{:S(2)}, u32[]{:S(2)}) collective-permute-start(f32[128,896]{1,0:T(8,128)S(1)} %get-tuple-element.56), channel_id=1, source_target_pairs={{0,32},{32,0},{64,96},{96,64},{1,33},{33,1},{65,97},{97,65},{2,34}... | collective-permute-start | bytes 1376264 | tf_op jit(solution)/shard_map/ppermute | solution.py:547
  5.7 14.5 %collective-permute-start.2 = (bf16[384,768]{1,0:T(8,128)(2,1)}, bf16[384,768]{1,0:T(8,128)(2,1)S(1)}, u32[]{:S(2)}, u32[]{:S(2)}) collective-permute-start(bf16[384,768]{1,0:T(8,128)(2,1)} %own), channel_id=1, source_target_pairs={{0,2},{1,7},{2,4},{3,1},{4,6},{5,3},{6,0},{7,5},{8,10},{9,15},{10,... | collective-permute-start | bytes 1769480 | tf_op jit(solution)/shard_map/ppermute | solution.py:552
  7.2 16.7 %collective-permute-start.1 = (bf16[384,768]{1,0:T(8,128)(2,1)}, bf16[384,768]{1,0:T(8,128)(2,1)S(1)}, u32[]{:S(2)}, u32[]{:S(2)}) collective-permute-start(bf16[384,768]{1,0:T(8,128)(2,1)} %own), channel_id=1, source_target_pairs={{0,24},{1,9},{8,0},{9,17},{16,8},{17,25},{24,16},{25,1},{2,26},{3,... | collective-permute-start | bytes 1769480 | tf_op jit(solution)/shard_map/ppermute | solution.py:552
  10.0 14.6 %collective-permute-start = (bf16[384,768]{1,0:T(8,128)(2,1)}, bf16[384,768]{1,0:T(8,128)(2,1)S(1)}, u32[]{:S(2)}, u32[]{:S(2)}) collective-permute-start(bf16[384,768]{1,0:T(8,128)(2,1)} %own), channel_id=1, source_target_pairs={{0,8},{1,25},{8,16},{9,1},{16,24},{17,9},{24,0},{25,17},{2,10},{3,... | collective-permute-start | bytes 1769480 | tf_op jit(solution)/shard_map/ppermute | solution.py:552
  10.0 14.6 %collective-permute-start.3 = (bf16[384,768]{1,0:T(8,128)(2,1)}, bf16[384,768]{1,0:T(8,128)(2,1)S(1)}, u32[]{:S(2)}, u32[]{:S(2)}) collective-permute-start(bf16[384,768]{1,0:T(8,128)(2,1)} %own), channel_id=1, source_target_pairs={{0,6},{1,3},{2,0},{3,5},{4,2},{5,7},{6,4},{7,1},{8,14},{9,11},{10,... | collective-permute-start | bytes 1769480 | tf_op jit(solution)/shard_map/ppermute | solution.py:552
  16.2 8.7 %collective-permute-start.5 = (f32[64,896]{1,0:T(8,128)S(1)}, f32[64,896]{1,0:T(8,128)S(1)}, u32[]{:S(2)}, u32[]{:S(2)}) collective-permute-start(f32[64,896]{1,0:T(8,128)S(1)} %get-tuple-element.57), channel_id=1, source_target_pairs={{0,96},{32,64},{64,32},{96,0},{1,97},{33,65},{65,33},{97,1},{2,98}... | collective-permute-start | bytes 688136 | tf_op jit(solution)/shard_map/ppermute | solution.py:547
  24.9 13.7 %collective-permute-start.6 = (bf16[384,768]{1,0:T(8,128)(2,1)S(1)}, bf16[384,768]{1,0:T(8,128)(2,1)S(1)}, u32[]{:S(2)}, u32[]{:S(2)}) collective-permute-start(bf16[384,768]{1,0:T(8,128)(2,1)S(1)} %collective-permute-done.x1), channel_id=1, source_target_pairs={{0,8},{1,25},{8,16},{9,1},{16,24},{17,9},{24,0},{25,17},{2,10},{3,... | collective-permute-start | bytes 1769480 | tf_op jit(solution)/shard_map/ppermute | solution.py:552
  26.4 12.2 %collective-permute-start.7 = (bf16[384,768]{1,0:T(8,128)(2,1)S(1)}, bf16[384,768]{1,0:T(8,128)(2,1)S(1)}, u32[]{:S(2)}, u32[]{:S(2)}) collective-permute-start(bf16[384,768]{1,0:T(8,128)(2,1)S(1)} %collective-permute-done.2.y1), channel_id=1, source_target_pairs={{0,2},{1,7},{2,4},{3,1},{4,6},{5,3},{6,0},{7,5},{8,10},{9,15},{10,... | collective-permute-start | bytes 1769480 | tf_op jit(solution)/shard_map/ppermute | solution.py:552
  28.1 8.3 %collective-permute-start.10 = (bf16[64,896]{1,0:T(8,128)(2,1)S(1)}, bf16[64,896]{1,0:T(8,128)(2,1)S(1)}, u32[]{:S(2)}, u32[]{:S(2)}) collective-permute-start(bf16[64,896]{1,0:T(8,128)(2,1)S(1)} %means.1.p0), channel_id=1, source_target_pairs={{0,96},{32,64},{64,32},{96,0},{1,97},{33,65},{65,33},{97,1},{2,98}... | collective-permute-start | bytes 344072 | tf_op jit(solution)/shard_map/ppermute | solution.py:547
  31.1 7.5 %collective-permute-start.9 = (bf16[64,896]{1,0:T(8,128)(2,1)S(1)}, bf16[64,896]{1,0:T(8,128)(2,1)S(1)}, u32[]{:S(2)}, u32[]{:S(2)}) collective-permute-start(bf16[64,896]{1,0:T(8,128)(2,1)S(1)} %means.1.p0), channel_id=1, source_target_pairs={{0,64},{32,96},{64,0},{96,32},{1,65},{33,97},{65,1},{97,33},{2,66}... | collective-permute-start | bytes 344072 | tf_op jit(solution)/shard_map/ppermute | solution.py:547
  31.1 7.5 %collective-permute-start.8 = (bf16[64,896]{1,0:T(8,128)(2,1)S(1)}, bf16[64,896]{1,0:T(8,128)(2,1)S(1)}, u32[]{:S(2)}, u32[]{:S(2)}) collective-permute-start(bf16[64,896]{1,0:T(8,128)(2,1)S(1)} %means.1.p0), channel_id=1, source_target_pairs={{0,32},{32,0},{64,96},{96,64},{1,33},{33,1},{65,97},{97,65},{2,34}... | collective-permute-start | bytes 344072 | tf_op jit(solution)/shard_map/ppermute | solution.py:547
  38.6 2.3 %collective-permute-start.11 = (bf16[384,768]{1,0:T(8,128)(2,1)}, bf16[384,768]{1,0:T(8,128)(2,1)S(1)}, u32[]{:S(2)}, u32[]{:S(2)}) collective-permute-start(bf16[384,768]{1,0:T(8,128)(2,1)} %own), channel_id=1, source_target_pairs={{0,1},{1,0},{2,3},{3,2},{4,5},{5,4},{6,7},{7,6},{8,9},{9,8},{10,11... | collective-permute-start | bytes 1769480 | tf_op jit(solution)/shard_map/ppermute | solution.py:547
  38.7 3.3 %collective-permute-start.12 = (bf16[384,768]{1,0:T(8,128)(2,1)S(1)}, bf16[384,768]{1,0:T(8,128)(2,1)S(1)}, u32[]{:S(2)}, u32[]{:S(2)}) collective-permute-start(bf16[384,768]{1,0:T(8,128)(2,1)S(1)} %collective-permute-done.2.y1), channel_id=1, source_target_pairs={{0,1},{1,0},{2,3},{3,2},{4,5},{5,4},{6,7},{7,6},{8,9},{9,8},{10,11... | collective-permute-start | bytes 1769480 | tf_op jit(solution)/shard_map/ppermute | solution.py:547
  39.2 3.8 %collective-permute-start.13 = (bf16[384,768]{1,0:T(8,128)(2,1)S(1)}, bf16[384,768]{1,0:T(8,128)(2,1)S(1)}, u32[]{:S(2)}, u32[]{:S(2)}) collective-permute-start(bf16[384,768]{1,0:T(8,128)(2,1)S(1)} %collective-permute-done.7.y2), channel_id=1, source_target_pairs={{0,1},{1,0},{2,3},{3,2},{4,5},{5,4},{6,7},{7,6},{8,9},{9,8},{10,11... | collective-permute-start | bytes 1769480 | tf_op jit(solution)/shard_map/ppermute | solution.py:547
  39.3 4.7 %collective-permute-start.14 = (bf16[384,768]{1,0:T(8,128)(2,1)S(1)}, bf16[384,768]{1,0:T(8,128)(2,1)S(1)}, u32[]{:S(2)}, u32[]{:S(2)}) collective-permute-start(bf16[384,768]{1,0:T(8,128)(2,1)S(1)} %collective-permute-done.3.y3), channel_id=1, source_target_pairs={{0,1},{1,0},{2,3},{3,2},{4,5},{5,4},{6,7},{7,6},{8,9},{9,8},{10,11... | collective-permute-start | bytes 1769480 | tf_op jit(solution)/shard_map/ppermute | solution.py:547
  39.9 14.9 %collective-permute-start.18 = (bf16[256,768]{1,0:T(8,128)(2,1)S(1)}, bf16[256,768]{1,0:T(8,128)(2,1)S(1)}, u32[]{:S(2)}, u32[]{:S(2)}) collective-permute-start(bf16[256,768]{1,0:T(8,128)(2,1)S(1)} %get-tuple-element.75.own), channel_id=1, source_target_pairs={{0,6},{1,3},{2,0},{3,5},{4,2},{5,7},{6,4},{7,1},{8,14},{9,11},{10,... | collective-permute-start | bytes 1179656 | tf_op jit(solution)/shard_map/ppermute | solution.py:552
  40.9 13.9 %collective-permute-start.17 = (bf16[256,768]{1,0:T(8,128)(2,1)S(1)}, bf16[256,768]{1,0:T(8,128)(2,1)S(1)}, u32[]{:S(2)}, u32[]{:S(2)}) collective-permute-start(bf16[256,768]{1,0:T(8,128)(2,1)S(1)} %get-tuple-element.75.own), channel_id=1, source_target_pairs={{0,2},{1,7},{2,4},{3,1},{4,6},{5,3},{6,0},{7,5},{8,10},{9,15},{10,... | collective-permute-start | bytes 1179656 | tf_op jit(solution)/shard_map/ppermute | solution.py:552
  42.0 12.8 %collective-permute-start.16 = (bf16[256,768]{1,0:T(8,128)(2,1)S(1)}, bf16[256,768]{1,0:T(8,128)(2,1)S(1)}, u32[]{:S(2)}, u32[]{:S(2)}) collective-permute-start(bf16[256,768]{1,0:T(8,128)(2,1)S(1)} %get-tuple-element.75.own), channel_id=1, source_target_pairs={{0,24},{1,9},{8,0},{9,17},{16,8},{17,25},{24,16},{25,1},{2,26},{3,... | collective-permute-start | bytes 1179656 | tf_op jit(solution)/shard_map/ppermute | solution.py:552
  43.0 12.0 %collective-permute-start.15 = (bf16[256,768]{1,0:T(8,128)(2,1)S(1)}, bf16[256,768]{1,0:T(8,128)(2,1)S(1)}, u32[]{:S(2)}, u32[]{:S(2)}) collective-permute-start(bf16[256,768]{1,0:T(8,128)(2,1)S(1)} %get-tuple-element.75.own), channel_id=1, source_target_pairs={{0,8},{1,25},{8,16},{9,1},{16,24},{17,9},{24,0},{25,17},{2,10},{3,... | collective-permute-start | bytes 1179656 | tf_op jit(solution)/shard_map/ppermute | solution.py:552
  55.0 9.0 %collective-permute-start.20 = (bf16[256,768]{1,0:T(8,128)(2,1)S(1)}, bf16[256,768]{1,0:T(8,128)(2,1)S(1)}, u32[]{:S(2)}, u32[]{:S(2)}) collective-permute-start(bf16[256,768]{1,0:T(8,128)(2,1)S(1)} %collective-permute-done.17.y1), channel_id=1, source_target_pairs={{0,2},{1,7},{2,4},{3,1},{4,6},{5,3},{6,0},{7,5},{8,10},{9,15},{10,... | collective-permute-start | bytes 1179656 | tf_op jit(solution)/shard_map/ppermute | solution.py:552
  55.7 9.8 %collective-permute-start.22 = (bf16[256,768]{1,0:T(8,128)(2,1)S(1)}, bf16[256,768]{1,0:T(8,128)(2,1)S(1)}, u32[]{:S(2)}, u32[]{:S(2)}) collective-permute-start(bf16[256,768]{1,0:T(8,128)(2,1)S(1)} %collective-permute-done.17.y1), channel_id=1, source_target_pairs={{0,1},{1,0},{2,3},{3,2},{4,5},{5,4},{6,7},{7,6},{8,9},{9,8},{10,11... | collective-permute-start | bytes 1179656 | tf_op jit(solution)/shard_map/ppermute | solution.py:547
  56.4 7.6 %collective-permute-start.21 = (bf16[256,768]{1,0:T(8,128)(2,1)S(1)}, bf16[256,768]{1,0:T(8,128)(2,1)S(1)}, u32[]{:S(2)}, u32[]{:S(2)}) collective-permute-start(bf16[256,768]{1,0:T(8,128)(2,1)S(1)} %get-tuple-element.75.own), channel_id=1, source_target_pairs={{0,1},{1,0},{2,3},{3,2},{4,5},{5,4},{6,7},{7,6},{8,9},{9,8},{10,11... | collective-permute-start | bytes 1179656 | tf_op jit(solution)/shard_map/ppermute | solution.py:547
  56.5 9.0 %collective-permute-start.19 = (bf16[256,768]{1,0:T(8,128)(2,1)S(1)}, bf16[256,768]{1,0:T(8,128)(2,1)S(1)}, u32[]{:S(2)}, u32[]{:S(2)}) collective-permute-start(bf16[256,768]{1,0:T(8,128)(2,1)S(1)} %collective-permute-done.15.x1), channel_id=1, source_target_pairs={{0,8},{1,25},{8,16},{9,1},{16,24},{17,9},{24,0},{25,17},{2,10},{3,... | collective-permute-start | bytes 1179656 | tf_op jit(solution)/shard_map/ppermute | solution.py:552
  57.4 8.0 %collective-permute-start.24 = (bf16[256,768]{1,0:T(8,128)(2,1)S(1)}, bf16[256,768]{1,0:T(8,128)(2,1)S(1)}, u32[]{:S(2)}, u32[]{:S(2)}) collective-permute-start(bf16[256,768]{1,0:T(8,128)(2,1)S(1)} %collective-permute-done.18.y3), channel_id=1, source_target_pairs={{0,1},{1,0},{2,3},{3,2},{4,5},{5,4},{6,7},{7,6},{8,9},{9,8},{10,11... | collective-permute-start | bytes 1179656 | tf_op jit(solution)/shard_map/ppermute | solution.py:547
  64.0 1.7 %collective-permute-start.23 = (bf16[256,768]{1,0:T(8,128)(2,1)S(1)}, bf16[256,768]{1,0:T(8,128)(2,1)S(1)}, u32[]{:S(2)}, u32[]{:S(2)}) collective-permute-start(bf16[256,768]{1,0:T(8,128)(2,1)S(1)} %collective-permute-done.20.y2), channel_id=1, source_target_pairs={{0,1},{1,0},{2,3},{3,2},{4,5},{5,4},{6,7},{7,6},{8,9},{9,8},{10,11... | collective-permute-start | bytes 1179656 | tf_op jit(solution)/shard_map/ppermute | solution.py:547
  73.0 3.8 %collective-permute-start.27 = (f32[24,128]{1,0:T(8,128)S(1)}, f32[24,128]{1,0:T(8,128)S(1)}, u32[]{:S(2)}, u32[]{:S(2)}) collective-permute-start(f32[24,128]{1,0:T(8,128)S(1)} %get-tuple-element.81.r_0_), channel_id=1, source_target_pairs={{0,6},{1,3},{2,0},{3,5},{4,2},{5,7},{6,4},{7,1},{8,14},{9,11},{10,... | collective-permute-start | bytes 36872 | tf_op jit(solution)/shard_map/ppermute | solution.py:552
  75.1 5.2 %collective-permute-start.26 = (f32[24,128]{1,0:T(8,128)S(1)}, f32[24,128]{1,0:T(8,128)S(1)}, u32[]{:S(2)}, u32[]{:S(2)}) collective-permute-start(f32[24,128]{1,0:T(8,128)S(1)} %get-tuple-element.81.r_0_), channel_id=1, source_target_pairs={{0,4},{1,5},{2,6},{3,7},{4,0},{5,1},{6,2},{7,3},{8,12},{9,13},{10,... | collective-permute-start | bytes 36872 | tf_op jit(solution)/shard_map/ppermute | solution.py:552
  76.5 4.9 %collective-permute-start.25 = (f32[24,128]{1,0:T(8,128)S(1)}, f32[24,128]{1,0:T(8,128)S(1)}, u32[]{:S(2)}, u32[]{:S(2)}) collective-permute-start(f32[24,128]{1,0:T(8,128)S(1)} %get-tuple-element.81.r_0_), channel_id=1, source_target_pairs={{0,2},{1,7},{2,4},{3,1},{4,6},{5,3},{6,0},{7,5},{8,10},{9,15},{10,... | collective-permute-start | bytes 36872 | tf_op jit(solution)/shard_map/ppermute | solution.py:552
  81.4 1.3 collective-permute-start.28
  84.1 3.8 %collective-permute-start.31 = (f32[32,128]{1,0:T(8,128)S(1)}, f32[32,128]{1,0:T(8,128)S(1)}, u32[]{:S(2)}, u32[]{:S(2)}) collective-permute-start(f32[32,128]{1,0:T(8,128)S(1)} %get-tuple-element.88.p0), channel_id=1, source_target_pairs={{0,24},{1,9},{8,0},{9,17},{16,8},{17,25},{24,16},{25,1},{2,26},{3,... | collective-permute-start | bytes 49160 | tf_op jit(solution)/shard_map/ppermute | solution.py:552
  85.0 5.2 %collective-permute-start.30 = (f32[32,128]{1,0:T(8,128)S(1)}, f32[32,128]{1,0:T(8,128)S(1)}, u32[]{:S(2)}, u32[]{:S(2)}) collective-permute-start(f32[32,128]{1,0:T(8,128)S(1)} %get-tuple-element.88.p0), channel_id=1, source_target_pairs={{0,16},{1,17},{8,24},{9,25},{16,0},{17,1},{24,8},{25,9},{2,18},{3,... | collective-permute-start | bytes 49160 | tf_op jit(solution)/shard_map/ppermute | solution.py:552
  85.6 5.0 %collective-permute-start.29 = (f32[32,128]{1,0:T(8,128)S(1)}, f32[32,128]{1,0:T(8,128)S(1)}, u32[]{:S(2)}, u32[]{:S(2)}) collective-permute-start(f32[32,128]{1,0:T(8,128)S(1)} %get-tuple-element.88.p0), channel_id=1, source_target_pairs={{0,8},{1,25},{8,16},{9,1},{16,24},{17,9},{24,0},{25,17},{2,10},{3,... | collective-permute-start | bytes 49160 | tf_op jit(solution)/shard_map/ppermute | solution.py:552
  93.9 3.9 %collective-permute-start.34 = (f32[40,128]{1,0:T(8,128)S(1)}, f32[40,128]{1,0:T(8,128)S(1)}, u32[]{:S(2)}, u32[]{:S(2)}) collective-permute-start(f32[40,128]{1,0:T(8,128)S(1)} %get-tuple-element.93.r_0_), channel_id=1, source_target_pairs={{0,6},{1,3},{2,0},{3,5},{4,2},{5,7},{6,4},{7,1},{8,14},{9,11},{10,... | collective-permute-start | bytes 61448 | tf_op jit(solution)/shard_map/ppermute | solution.py:552
  95.3 5.3 %collective-permute-start.33 = (f32[40,128]{1,0:T(8,128)S(1)}, f32[40,128]{1,0:T(8,128)S(1)}, u32[]{:S(2)}, u32[]{:S(2)}) collective-permute-start(f32[40,128]{1,0:T(8,128)S(1)} %get-tuple-element.93.r_0_), channel_id=1, source_target_pairs={{0,4},{1,5},{2,6},{3,7},{4,0},{5,1},{6,2},{7,3},{8,12},{9,13},{10,... | collective-permute-start | bytes 61448 | tf_op jit(solution)/shard_map/ppermute | solution.py:552
  96.2 5.0 %collective-permute-start.32 = (f32[40,128]{1,0:T(8,128)S(1)}, f32[40,128]{1,0:T(8,128)S(1)}, u32[]{:S(2)}, u32[]{:S(2)}) collective-permute-start(f32[40,128]{1,0:T(8,128)S(1)} %get-tuple-element.93.r_0_), channel_id=1, source_target_pairs={{0,2},{1,7},{2,4},{3,1},{4,6},{5,3},{6,0},{7,5},{8,10},{9,15},{10,... | collective-permute-start | bytes 61448 | tf_op jit(solution)/shard_map/ppermute | solution.py:552
  101.2 1.3 collective-permute-start.35
  106.4 3.8 %collective-permute-start.38 = (f32[24,128]{1,0:T(8,128)S(1)}, f32[24,128]{1,0:T(8,128)S(1)}, u32[]{:S(2)}, u32[]{:S(2)}) collective-permute-start(f32[24,128]{1,0:T(8,128)S(1)} %step4.1.p0), channel_id=1, source_target_pairs={{0,24},{1,9},{8,0},{9,17},{16,8},{17,25},{24,16},{25,1},{2,26},{3,... | collective-permute-start | bytes 36872 | tf_op jit(solution)/shard_map/ppermute | solution.py:552
  107.8 5.2 %collective-permute-start.37 = (f32[24,128]{1,0:T(8,128)S(1)}, f32[24,128]{1,0:T(8,128)S(1)}, u32[]{:S(2)}, u32[]{:S(2)}) collective-permute-start(f32[24,128]{1,0:T(8,128)S(1)} %step4.1.p0), channel_id=1, source_target_pairs={{0,16},{1,17},{8,24},{9,25},{16,0},{17,1},{24,8},{25,9},{2,18},{3,... | collective-permute-start | bytes 36872 | tf_op jit(solution)/shard_map/ppermute | solution.py:552
  108.7 4.9 %collective-permute-start.36 = (f32[24,128]{1,0:T(8,128)S(1)}, f32[24,128]{1,0:T(8,128)S(1)}, u32[]{:S(2)}, u32[]{:S(2)}) collective-permute-start(f32[24,128]{1,0:T(8,128)S(1)} %step4.1.p0), channel_id=1, source_target_pairs={{0,8},{1,25},{8,16},{9,1},{16,24},{17,9},{24,0},{25,17},{2,10},{3,... | collective-permute-start | bytes 36872 | tf_op jit(solution)/shard_map/ppermute | solution.py:552
  116.0 3.8 %collective-permute-start.41 = (f32[24,128]{1,0:T(8,128)S(1)}, f32[24,128]{1,0:T(8,128)S(1)}, u32[]{:S(2)}, u32[]{:S(2)}) collective-permute-start(f32[24,128]{1,0:T(8,128)S(1)} %get-tuple-element.97.r_0_), channel_id=1, source_target_pairs={{0,6},{1,3},{2,0},{3,5},{4,2},{5,7},{6,4},{7,1},{8,14},{9,11},{10,... | collective-permute-start | bytes 36872 | tf_op jit(solution)/shard_map/ppermute | solution.py:552
  118.1 5.2 %collective-permute-start.40 = (f32[24,128]{1,0:T(8,128)S(1)}, f32[24,128]{1,0:T(8,128)S(1)}, u32[]{:S(2)}, u32[]{:S(2)}) collective-permute-start(f32[24,128]{1,0:T(8,128)S(1)} %get-tuple-element.97.r_0_), channel_id=1, source_target_pairs={{0,4},{1,5},{2,6},{3,7},{4,0},{5,1},{6,2},{7,3},{8,12},{9,13},{10,... | collective-permute-start | bytes 36872 | tf_op jit(solution)/shard_map/ppermute | solution.py:552
  119.0 4.9 %collective-permute-start.39 = (f32[24,128]{1,0:T(8,128)S(1)}, f32[24,128]{1,0:T(8,128)S(1)}, u32[]{:S(2)}, u32[]{:S(2)}) collective-permute-start(f32[24,128]{1,0:T(8,128)S(1)} %get-tuple-element.97.r_0_), channel_id=1, source_target_pairs={{0,2},{1,7},{2,4},{3,1},{4,6},{5,3},{6,0},{7,5},{8,10},{9,15},{10,... | collective-permute-start | bytes 36872 | tf_op jit(solution)/shard_map/ppermute | solution.py:552
  123.9 1.3 collective-permute-start.42
  128.2 3.7 %collective-permute-start.45 = (f32[16,128]{1,0:T(8,128)S(1)}, f32[16,128]{1,0:T(8,128)S(1)}, u32[]{:S(2)}, u32[]{:S(2)}) collective-permute-start(f32[16,128]{1,0:T(8,128)S(1)} %get-tuple-element.98.p0), channel_id=1, source_target_pairs={{0,24},{1,9},{8,0},{9,17},{16,8},{17,25},{24,16},{25,1},{2,26},{3,... | collective-permute-start | bytes 24584 | tf_op jit(solution)/shard_map/ppermute | solution.py:552
  128.9 5.2 %collective-permute-start.44 = (f32[16,128]{1,0:T(8,128)S(1)}, f32[16,128]{1,0:T(8,128)S(1)}, u32[]{:S(2)}, u32[]{:S(2)}) collective-permute-start(f32[16,128]{1,0:T(8,128)S(1)} %get-tuple-element.98.p0), channel_id=1, source_target_pairs={{0,16},{1,17},{8,24},{9,25},{16,0},{17,1},{24,8},{25,9},{2,18},{3,... | collective-permute-start | bytes 24584 | tf_op jit(solution)/shard_map/ppermute | solution.py:552
  129.8 4.9 %collective-permute-start.43 = (f32[16,128]{1,0:T(8,128)S(1)}, f32[16,128]{1,0:T(8,128)S(1)}, u32[]{:S(2)}, u32[]{:S(2)}) collective-permute-start(f32[16,128]{1,0:T(8,128)S(1)} %get-tuple-element.98.p0), channel_id=1, source_target_pairs={{0,8},{1,25},{8,16},{9,1},{16,24},{17,9},{24,0},{25,17},{2,10},{3,... | collective-permute-start | bytes 24584 | tf_op jit(solution)/shard_map/ppermute | solution.py:552
where the time goes:
time: 136 us; the launch traced here: 135 us
  waiting for transfers between devices  51.6 us (38%)
  starting transfers between devices  46.3 us (34%)
  Pallas kernels  34.6 us (25%)
    ppermute x30, waiting for transfers between devices, turn(): lax.ppermute(v, (axis, 'c'), [(i * 2 + c, (i + (k if c == 0 else n - k))...  36.6 us
    ppermute x30, starting transfers between devices, turn(): lax.ppermute(v, (axis, 'c'), [(i * 2 + c, (i + (k if c == 0 else n - k))...  32.8 us
    ppermute x16, waiting for transfers between devices, swap(): return lax.ppermute(v, axis, [(i, i ^ bit) for i in range(n)])  15 us
    ppermute x16, starting transfers between devices, swap(): return lax.ppermute(v, axis, [(i, i ^ bit) for i in range(n)])  13.5 us
    pallas_call x1, Pallas kernels, local(): tile_call(fine_tile_kernel, n_rows, n_cols, n_cols // 128, [SMEM, VMEM] +...  10.7 us
    pallas_call x1, Pallas kernels, local(): tile_call(coarse_tile_kernel, k_rows, k_cols, 24, [ANY] * 11 + [VMEM], [p...  7.32 us
    pallas_call x1, Pallas kernels, local(): call(step4_kernel, sds((24, 128)), [VMEM, VMEM] + [VMEM] * 3 + kspecs * 2...  3.9 us
    pallas_call x1, Pallas kernels, local(): call(step3_kernel, [sds((40, 128)), sds((8, 128)), sds((12, 128))], [VMEM...  3.28 us
  transfers between devices with their start and end apart: 46, of which 30 were waited for; matrix products, arithmetic and copies ran while one was open for 0% of the time, Pallas kernels for 8%

commit v1 on v0

--- a/solution.py
+++ b/solution.py
@@ -271,12 +271,12 @@
     )
 
 
-def pool_kernel(info, emb, members, keep, send, live_rows, live_cols, seat, logs):
+def pool_kernel(info, emb, table, keep, send, live_rows, live_cols, seat, logs):
     idx = info_place(info)
     z, x, y, c = idx
     quarter = PROTO_BLOCK // Z
-    per = members.shape[0]
-    ids = members[...]
+    per = seat.shape[0]
+    ids = table[Z + 1:Z + 1 + per, :]
     which = lax.shift_right_logical(ids, 11)
     within = jnp.bitwise_and(ids, quarter - 1)
     turn = jnp.bitwise_xor(which, z)
@@ -287,12 +287,14 @@
     live = iota((1, rows), 1) < count_at(info, z, x, y, c)
     hot = ((iota((PROTO_BLOCK, rows), 0) == local) & live).astype(BF16)
     sums = jnp.dot(hot, emb[...], preferred_element_type=F32)
-    sizes = jnp.dot(hot, jnp.ones((rows, PAD), BF16), preferred_element_type=F32)
+    sizes = lax.dot_general(
+        jnp.ones((8, rows), BF16), hot, (((1,), (1,)), ((), ())), preferred_element_type=F32
+    )
     half = 2 * quarter
-    keep[:, 0:d] = sums[0:half]
-    keep[:, d:] = sizes[0:half]
-    send[:, 0:d] = sums[half:]
-    send[:, d:] = sizes[half:]
+    keep[0:half, :] = sums[0:half]
+    keep[half:, :] = size_rows(sizes[:, 0:half], d)
+    send[0:half, :] = sums[half:]
+    send[half:, :] = size_rows(sizes[:, half:], d)
     live_rows[...] = live_mask(row_counts(info, idx), per)
     live_cols[...] = live_mask(col_counts(info, idx), per)
     mine, total = 0, 0
@@ -305,6 +307,10 @@
     logs[...] = jnp.concatenate([log2_of(mine), log2_of(total), jnp.zeros((6, 128), F32)], axis=0)
 
 
+def size_rows(sizes, d):
+    return jnp.concatenate([sizes, jnp.zeros((sizes.shape[0], d - sizes.shape[1]), F32)], axis=1)
+
+
 def code_sizes(sizes):
     high = jnp.floor(sizes * (1.0 / 256.0))
     low = sizes - 256.0 * high
@@ -317,16 +323,20 @@
 
 
 def pool2_kernel(mine, got, keep, send):
-    quarter = mine.shape[0] // 2
-    keep[...] = mine[0:quarter, :] + got[0:quarter, :]
-    send[...] = mine[quarter:, :] + got[quarter:, :]
+    half, d = mine.shape[0] - 8, mine.shape[1]
+    quarter = half // 2
+    keep[0:quarter, :] = mine[0:quarter, :] + got[0:quarter, :]
+    send[0:quarter, :] = mine[quarter:half, :] + got[quarter:half, :]
+    sizes = mine[half:, 0:half] + got[half:, 0:half]
+    keep[quarter:, :] = size_rows(sizes, d)
+    send[quarter:, :] = size_rows(jnp.concatenate([sizes[:, quarter:], sizes[:, 0:quarter]], axis=1), d)
 
 
 def means_kernel(mine, got, out):
-    d = mine.shape[1] - PAD
-    sums = mine[...] + got[...]
-    sizes = sums[:, d:]
-    out[:, 0:d] = (sums[:, 0:d] / sizes[:, 0:1]).astype(BF16)
+    quarter, d = mine.shape[0] - 8, mine.shape[1]
+    lanes = mine[quarter:, 0:128] + got[quarter:, 0:128]
+    sizes = jnp.transpose(jnp.broadcast_to(lanes[0:1, :], (128, 128)))[0:quarter, :]
+    out[:, 0:d] = ((mine[0:quarter, :] + got[0:quarter, :]) / sizes[:, 0:1]).astype(BF16)
     out[:, d:] = code_sizes(sizes)
 
 
@@ -569,7 +579,14 @@
 def local(embeddings, members, counts):
     rows, d = embeddings.shape
     here = jnp.stack([lax.axis_index(a) for a in ("z", "x", "y", "c")]).astype(jnp.int32)
-    info = jnp.concatenate([counts, jnp.pad(here[None], ((0, 0), (0, counts.shape[1] - 4)))], axis=0)
+    info = jnp.concatenate(
+        [
+            jnp.pad(counts, ((0, 0), (0, 128 - counts.shape[1]))),
+            jnp.pad(here[None], ((0, 0), (0, 124))),
+            members.reshape(rows // 128, 128),
+        ],
+        axis=0,
+    )
     per = rows // 128
     n_rows, n_cols = rows * Y * 2, rows * X
     k_rows, k_cols = PROTO_BLOCK * Y * 2, PROTO_BLOCK * X
@@ -583,14 +600,14 @@
     keep, send, live_rows, live_cols, seat, logs = call(
         pool_kernel,
         [
-            sds((2 * quarter, width)), sds((2 * quarter, width)), sds((n_rows // 128, 128)),
+            sds((2 * quarter + 8, d)), sds((2 * quarter + 8, d)), sds((n_rows // 128, 128)),
             sds((n_cols // 128, 128)), sds((per, 128)), sds((8, 128)),
         ],
         [SMEM, VMEM, VMEM],
         name="pool",
-    )(info, embeddings, members.reshape(per, 128))
+    )(info, embeddings, info)
     keep, send = call(
-        pool2_kernel, [sds((quarter, width)), sds((quarter, width))], [VMEM] * 2, name="pool2"
+        pool2_kernel, [sds((quarter + 8, d)), sds((quarter + 8, d))], [VMEM] * 2, name="pool2"
     )(keep, swap(send, "z", 1))
     got = swap(send, "z", 3)
     x1, x3, y1, y3, got = lax.optimization_barrier((x1, x3, y1, y3, got))

time: 136 us -> 134 us (0.985)
  transfers between devices with their start and end apart: 46 -> 46, of which waited for: 30 -> 29; matrix products, arithmetic and copies ran while one was open for 0% -> 0% of each run, Pallas kernels for 8% -> 8%
where the time goes in v1:
time: 134 us
  waiting for transfers between devices  50.6 us (38%)
  starting transfers between devices  46.2 us (34%)
  Pallas kernels  34.7 us (26%)
    ppermute x30, waiting for transfers between devices, turn(): lax.ppermute(v, (axis, 'c'), [(i * 2 + c, (i + (k if c == 0 else n - k))...  36.9 us
    ppermute x30, starting transfers between devices, turn(): lax.ppermute(v, (axis, 'c'), [(i * 2 + c, (i + (k if c == 0 else n - k))...  33 us
    ppermute x16, waiting for transfers between devices, swap(): return lax.ppermute(v, axis, [(i, i ^ bit) for i in range(n)])  13.7 us
    ppermute x16, starting transfers between devices, swap(): return lax.ppermute(v, axis, [(i, i ^ bit) for i in range(n)])  13.2 us
    pallas_call x1, Pallas kernels, local(): tile_call(fine_tile_kernel, n_rows, n_cols, n_cols // 128, [SMEM, VMEM] +...  10.7 us
    pallas_call x1, Pallas kernels, local(): tile_call(coarse_tile_kernel, k_rows, k_cols, 24, [ANY] * 11 + [VMEM], [p...  7.31 us
    pallas_call x1, Pallas kernels, local(): call(step4_kernel, sds((24, 128)), [VMEM, VMEM] + [VMEM] * 3 + kspecs * 2...  3.9 us
    pallas_call x1, Pallas kernels, local(): call(step3_kernel, [sds((40, 128)), sds((8, 128)), sds((12, 128))], [VMEM...  3.28 us
  transfers between devices with their start and end apart: 46, of which 29 were waited for; matrix products, arithmetic and copies ran while one was open for 0% of the time, Pallas kernels for 8%

profile of v1, /device:TPU:0, one launch (start us, length us, event | category | flops | bytes accessed | tf_op | source)
XLA Modules:
  0.0 133.6 jit_solution(16817313330144213181)
XLA Ops:
  1.4 1.5 %pool.1 = (f32[136,768]{1,0:T(8,128)S(1)}, f32[136,768]{1,0:T(8,128)S(1)}, f32[24,128]{1,0:T(8,128)S(1)}, f32[12,128]{1,0:T(8,128)S(1)}, f32[3,128]{1,0:T(4,128)S(1)}, /*index=5*/f32[8,128]{1,0:T(8,128)S(1)}) custom-call(s32[8,128]{1,0:T(8,128)S(1)} %fusion.info.table, bf16[384,768]{1,0:T(8,128)(2,1)} %own, s32[8,128]{1,0:T(8,128)S(1)} %fusion.info.table), custom_call_target="tpu_custom_call" | custom-call | tf_op jit(solution)/shard_map/pool/pallas_call | solution.py:600
  2.9 2.1 %collective-permute-start.4 = (f32[136,768]{1,0:T(8,128)S(1)}, f32[136,768]{1,0:T(8,128)S(1)}, u32[]{:S(2)}, u32[]{:S(2)}) collective-permute-start(f32[136,768]{1,0:T(8,128)S(1)} %get-tuple-element.56), channel_id=1, source_target_pairs={{0,32},{32,0},{64,96},{96,64},{1,33},{33,1},{65,97},{97,65},{2,34}... | collective-permute-start | bytes 1253384 | tf_op jit(solution)/shard_map/ppermute | solution.py:557
  5.0 1.6 %collective-permute-start.2 = (bf16[384,768]{1,0:T(8,128)(2,1)}, bf16[384,768]{1,0:T(8,128)(2,1)S(1)}, u32[]{:S(2)}, u32[]{:S(2)}) collective-permute-start(bf16[384,768]{1,0:T(8,128)(2,1)} %own), channel_id=1, source_target_pairs={{0,2},{1,7},{2,4},{3,1},{4,6},{5,3},{6,0},{7,5},{8,10},{9,15},{10,... | collective-permute-start | bytes 1769480 | tf_op jit(solution)/shard_map/ppermute | solution.py:562
  6.5 2.8 %collective-permute-start.1 = (bf16[384,768]{1,0:T(8,128)(2,1)}, bf16[384,768]{1,0:T(8,128)(2,1)S(1)}, u32[]{:S(2)}, u32[]{:S(2)}) collective-permute-start(bf16[384,768]{1,0:T(8,128)(2,1)} %own), channel_id=1, source_target_pairs={{0,24},{1,9},{8,0},{9,17},{16,8},{17,25},{24,16},{25,1},{2,26},{3,... | collective-permute-start | bytes 1769480 | tf_op jit(solution)/shard_map/ppermute | solution.py:562
  9.3 1.7 %collective-permute-start.3 = (bf16[384,768]{1,0:T(8,128)(2,1)}, bf16[384,768]{1,0:T(8,128)(2,1)S(1)}, u32[]{:S(2)}, u32[]{:S(2)}) collective-permute-start(bf16[384,768]{1,0:T(8,128)(2,1)} %own), channel_id=1, source_target_pairs={{0,6},{1,3},{2,0},{3,5},{4,2},{5,7},{6,4},{7,1},{8,14},{9,11},{10,... | collective-permute-start | bytes 1769480 | tf_op jit(solution)/shard_map/ppermute | solution.py:562
  11.0 3.6 %collective-permute-done.4.got = f32[136,768]{1,0:T(8,128)S(1)} collective-permute-done((f32[136,768]{1,0:T(8,128)S(1)}, f32[136,768]{1,0:T(8,128)S(1)}, u32[]{:S(2)}, u32[]{:S(2)}) %collective-permute-start.4) | collective-permute-done | bytes 417824 | tf_op jit(solution)/shard_map/ppermute | solution.py:557
  14.7 3.9 %collective-permute-start.5 = (f32[72,768]{1,0:T(8,128)S(1)}, f32[72,768]{1,0:T(8,128)S(1)}, u32[]{:S(2)}, u32[]{:S(2)}) collective-permute-start(f32[72,768]{1,0:T(8,128)S(1)} %get-tuple-element.57), channel_id=1, source_target_pairs={{0,96},{32,64},{64,32},{96,0},{1,97},{33,65},{65,33},{97,1},{2,98}... | collective-permute-start | bytes 663560 | tf_op jit(solution)/shard_map/ppermute | solution.py:557
  18.6 4.7 %collective-permute-done.1.x3 = bf16[384,768]{1,0:T(8,128)(2,1)S(1)} collective-permute-done((bf16[384,768]{1,0:T(8,128)(2,1)}, bf16[384,768]{1,0:T(8,128)(2,1)S(1)}, u32[]{:S(2)}, u32[]{:S(2)}) %collective-permute-start.1) | collective-permute-done | bytes 589856 | tf_op jit(solution)/shard_map/ppermute | solution.py:562
  24.6 1.6 %collective-permute-start.7 = (bf16[384,768]{1,0:T(8,128)(2,1)S(1)}, bf16[384,768]{1,0:T(8,128)(2,1)S(1)}, u32[]{:S(2)}, u32[]{:S(2)}) collective-permute-start(bf16[384,768]{1,0:T(8,128)(2,1)S(1)} %collective-permute-done.2.y1), channel_id=1, source_target_pairs={{0,2},{1,7},{2,4},{3,1},{4,6},{5,3},{6,0},{7,5},{8,10},{9,15},{10,... | collective-permute-start | bytes 1769480 | tf_op jit(solution)/shard_map/ppermute | solution.py:562
  26.4 3.0 %collective-permute-start.10 = (bf16[64,896]{1,0:T(8,128)(2,1)S(1)}, bf16[64,896]{1,0:T(8,128)(2,1)S(1)}, u32[]{:S(2)}, u32[]{:S(2)}) collective-permute-start(bf16[64,896]{1,0:T(8,128)(2,1)S(1)} %means.1.p0), channel_id=1, source_target_pairs={{0,96},{32,64},{64,32},{96,0},{1,97},{33,65},{65,33},{97,1},{2,98}... | collective-permute-start | bytes 344072 | tf_op jit(solution)/shard_map/ppermute | solution.py:557
  29.4 1.1 collective-permute-start.8
  30.6 4.1 %collective-permute-done.10.p3 = bf16[64,896]{1,0:T(8,128)(2,1)S(1)} collective-permute-done((bf16[64,896]{1,0:T(8,128)(2,1)S(1)}, bf16[64,896]{1,0:T(8,128)(2,1)S(1)}, u32[]{:S(2)}, u32[]{:S(2)}) %collective-permute-start.10) | collective-permute-done | bytes 114720 | tf_op jit(solution)/shard_map/ppermute | solution.py:557
  34.7 2.3 %collective-permute-done.9.p2 = bf16[64,896]{1,0:T(8,128)(2,1)S(1)} collective-permute-done((bf16[64,896]{1,0:T(8,128)(2,1)S(1)}, bf16[64,896]{1,0:T(8,128)(2,1)S(1)}, u32[]{:S(2)}, u32[]{:S(2)}) %collective-permute-start.9) | collective-permute-done | bytes 114720 | tf_op jit(solution)/shard_map/ppermute | solution.py:557
  38.2 1.0 collective-permute-start.18
  39.3 1.6 %collective-permute-start.17 = (bf16[256,768]{1,0:T(8,128)(2,1)S(1)}, bf16[256,768]{1,0:T(8,128)(2,1)S(1)}, u32[]{:S(2)}, u32[]{:S(2)}) collective-permute-start(bf16[256,768]{1,0:T(8,128)(2,1)S(1)} %get-tuple-element.75.own), channel_id=1, source_target_pairs={{0,2},{1,7},{2,4},{3,1},{4,6},{5,3},{6,0},{7,5},{8,10},{9,15},{10,... | collective-permute-start | bytes 1179656 | tf_op jit(solution)/shard_map/ppermute | solution.py:562
  41.6 1.3 collective-permute-start.15
  42.9 10.7 %fine_tile.1 = (f32[3072,1536]{1,0:T(8,128)S(1)}, f32[12,128]{1,0:T(8,128)S(1)}, f32[8,128]{1,0:T(8,128)S(1)}, bf16[3072,768]{1,0:T(8,128)(2,1)}, bf16[1536,768]{1,0:T(8,128)(2,1)}) custom-call(s32[8,128]{1,0:T(8,128)S(1)} %fusion.info.table, f32[24,128]{1,0:T(8,128)S(1)} %get-tuple-element.54.live_rows, bf16[384,768]{1,0:T(8,128)(2,1)} %own, ...), custom_call_target="tpu_custom_call" | custom-call | flops 7247757312 | tf_op jit(solution)/shard_map/fine_tile/pallas_call | solution.py:650
  53.6 1.2 collective-permute-start.20
  55.7 1.2 collective-permute-start.24
  56.9 5.7 %collective-permute-done.20.y2 = bf16[256,768]{1,0:T(8,128)(2,1)S(1)} collective-permute-done((bf16[256,768]{1,0:T(8,128)(2,1)S(1)}, bf16[256,768]{1,0:T(8,128)(2,1)S(1)}, u32[]{:S(2)}, u32[]{:S(2)}) %collective-permute-start.20) | collective-permute-done | bytes 393248 | tf_op jit(solution)/shard_map/ppermute | solution.py:562
  62.7 1.6 %collective-permute-done.19.x2 = bf16[256,768]{1,0:T(8,128)(2,1)S(1)} collective-permute-done((bf16[256,768]{1,0:T(8,128)(2,1)S(1)}, bf16[256,768]{1,0:T(8,128)(2,1)S(1)}, u32[]{:S(2)}, u32[]{:S(2)}) %collective-permute-start.19) | collective-permute-done | bytes 393248 | tf_op jit(solution)/shard_map/ppermute | solution.py:562
  64.4 7.3 %coarse_tile.1 = (f32[2048,1024]{1,0:T(8,128)S(1)}, f32[24,128]{1,0:T(8,128)S(1)}, f32[8,128]{1,0:T(8,128)S(1)}, bf16[2048,768]{1,0:T(8,128)(2,1)}, bf16[1024,768]{1,0:T(8,128)(2,1)}) custom-call(bf16[256,768]{1,0:T(8,128)(2,1)S(1)} %get-tuple-element.75.own, bf16[256,768]{1,0:T(8,128)(2,1)S(1)} %collective-permute-done.15.x1, ...), custom_call_target="tpu_custom_call" | custom-call | flops 3221225472 | tf_op jit(solution)/shard_map/coarse_tile/pallas_call | solution.py:658
  71.7 2.1 %collective-permute-start.27 = (f32[24,128]{1,0:T(8,128)S(1)}, f32[24,128]{1,0:T(8,128)S(1)}, u32[]{:S(2)}, u32[]{:S(2)}) collective-permute-start(f32[24,128]{1,0:T(8,128)S(1)} %get-tuple-element.81.r_0_), channel_id=1, source_target_pairs={{0,6},{1,3},{2,0},{3,5},{4,2},{5,7},{6,4},{7,1},{8,14},{9,11},{10,... | collective-permute-start | bytes 36872 | tf_op jit(solution)/shard_map/ppermute | solution.py:562
  73.8 1.0 collective-permute-start.26
  75.5 3.6 %collective-permute-done.26.r_2_ = f32[24,128]{1,0:T(8,128)S(1)} collective-permute-done((f32[24,128]{1,0:T(8,128)S(1)}, f32[24,128]{1,0:T(8,128)S(1)}, u32[]{:S(2)}, u32[]{:S(2)}) %collective-permute-start.26) | collective-permute-done | bytes 12320 | tf_op jit(solution)/shard_map/ppermute | solution.py:562
  79.9 1.2 collective-permute-done.28.other
  81.0 1.4 %coarse2.1 = (f32[32,128]{1,0:T(8,128)S(1)}, f32[16,128]{1,0:T(8,128)S(1)}) custom-call(f32[24,128]{1,0:T(8,128)S(1)} %fold_y1.1.mine, f32[24,128]{1,0:T(8,128)S(1)} %collective-permute-done.28.other, f32[12,128]{1,0:T(8,128)S(1)} %get-tuple-element.82.part, f32[8,128]{1,0:T(8,128)S(1)} %get-tuple-element.80.plog, f32[3,128]{1,0:T(4,128)S(1)} %get-tuple-element.83.seat, ...), custom_call_target="tpu_custom_call" | custom-call | tf_op jit(solution)/shard_map/coarse2/pallas_call | solution.py:672
  82.5 1.1 collective-permute-start.31
  84.0 1.1 collective-permute-start.29
  85.1 1.2 collective-permute-done.31.p3
  86.3 2.6 %collective-permute-done.30.p2 = f32[32,128]{1,0:T(8,128)S(1)} collective-permute-done((f32[32,128]{1,0:T(8,128)S(1)}, f32[32,128]{1,0:T(8,128)S(1)}, u32[]{:S(2)}, u32[]{:S(2)}) %collective-permute-start.30) | collective-permute-done | bytes 16416 | tf_op jit(solution)/shard_map/ppermute | solution.py:562
  89.0 3.3 %step3.1 = (f32[40,128]{1,0:T(8,128)S(1)}, f32[8,128]{1,0:T(8,128)S(1)}, f32[12,128]{1,0:T(8,128)S(1)}) custom-call(f32[8,128]{1,0:T(8,128)S(1)} %get-tuple-element.52.logs, f32[24,128]{1,0:T(8,128)S(1)} %get-tuple-element.54.live_rows, f32[12,128]{1,0:T(8,128)S(1)} %get-tuple-element.53.live_cols, f32[32,128]{1,0:T(8,128)S(1)} %get-tuple-element.88.p0, ...), custom_call_target="tpu_custom_call" | custom-call | tf_op jit(solution)/shard_map/step3/pallas_call | solution.py:680
  92.3 1.4 %collective-permute-start.34 = (f32[40,128]{1,0:T(8,128)S(1)}, f32[40,128]{1,0:T(8,128)S(1)}, u32[]{:S(2)}, u32[]{:S(2)}) collective-permute-start(f32[40,128]{1,0:T(8,128)S(1)} %get-tuple-element.93.r_0_), channel_id=1, source_target_pairs={{0,6},{1,3},{2,0},{3,5},{4,2},{5,7},{6,4},{7,1},{8,14},{9,11},{10,... | collective-permute-start | bytes 61448 | tf_op jit(solution)/shard_map/ppermute | solution.py:562
  94.6 0.9 collective-permute-start.32
  96.2 2.8 %collective-permute-done.33.r_2_ = f32[40,128]{1,0:T(8,128)S(1)} collective-permute-done((f32[40,128]{1,0:T(8,128)S(1)}, f32[40,128]{1,0:T(8,128)S(1)}, u32[]{:S(2)}, u32[]{:S(2)}) %collective-permute-start.33) | collective-permute-done | bytes 20512 | tf_op jit(solution)/shard_map/ppermute | solution.py:562
  99.8 1.2 collective-permute-done.35.other
  100.9 3.9 %step4.1.p0 = f32[24,128]{1,0:T(8,128)S(1)} custom-call(f32[8,128]{1,0:T(8,128)S(1)} %get-tuple-element.52.logs, f32[24,128]{1,0:T(8,128)S(1)} %get-tuple-element.54.live_rows, f32[40,128]{1,0:T(8,128)S(1)} %fold_y2.1.mine, f32[40,128]{1,0:T(8,128)S(1)} %collective-permute-done.35.other, f32[16,128]{1,0:T(8,128)S(1)} %get-tuple-element.94.plog_rows, ...), custom_call_target="tpu_custom_call" | custom-call | tf_op jit(solution)/shard_map/step4/pallas_call | solution.py:695
  104.8 1.3 collective-permute-start.38
  106.1 0.9 collective-permute-start.37
  107.0 1.2 collective-permute-start.36
  108.6 2.7 %collective-permute-done.37.p2 = f32[24,128]{1,0:T(8,128)S(1)} collective-permute-done((f32[24,128]{1,0:T(8,128)S(1)}, f32[24,128]{1,0:T(8,128)S(1)}, u32[]{:S(2)}, u32[]{:S(2)}) %collective-permute-start.37) | collective-permute-done | bytes 12320 | tf_op jit(solution)/shard_map/ppermute | solution.py:562
  111.9 2.4 %step5.1 = (f32[24,128]{1,0:T(8,128)S(1)}, f32[1,128]{1,0:T(1,128)S(1)}) custom-call(f32[8,128]{1,0:T(8,128)S(1)} %get-tuple-element.52.logs, f32[24,128]{1,0:T(8,128)S(1)} %get-tuple-element.54.live_rows, f32[12,128]{1,0:T(8,128)S(1)} %get-tuple-element.53.live_cols, f32[24,128]{1,0:T(8,128)S(1)} %step4.1.p0, f32[24,128]{1,0:T(8,128)S(1)} %collective-permute-done.36.p1, ...), custom_call_target="tpu_custom_call" | custom-call | tf_op jit(solution)/shard_map/step5/pallas_call | solution.py:703
  114.3 2.1 %collective-permute-start.41 = (f32[24,128]{1,0:T(8,128)S(1)}, f32[24,128]{1,0:T(8,128)S(1)}, u32[]{:S(2)}, u32[]{:S(2)}) collective-permute-start(f32[24,128]{1,0:T(8,128)S(1)} %get-tuple-element.97.r_0_), channel_id=1, source_target_pairs={{0,6},{1,3},{2,0},{3,5},{4,2},{5,7},{6,4},{7,1},{8,14},{9,11},{10,... | collective-permute-start | bytes 36872 | tf_op jit(solution)/shard_map/ppermute | solution.py:562
  118.1 3.5 %collective-permute-done.40.r_2_ = f32[24,128]{1,0:T(8,128)S(1)} collective-permute-done((f32[24,128]{1,0:T(8,128)S(1)}, f32[24,128]{1,0:T(8,128)S(1)}, u32[]{:S(2)}, u32[]{:S(2)}) %collective-permute-start.40) | collective-permute-done | bytes 12320 | tf_op jit(solution)/shard_map/ppermute | solution.py:562
  122.4 1.2 collective-permute-done.42.other
  123.5 3.1 %step6.1 = (f32[16,128]{1,0:T(8,128)S(1)}, f32[3,128]{1,0:T(4,128)}) custom-call(f32[8,128]{1,0:T(8,128)S(1)} %get-tuple-element.52.logs, f32[24,128]{1,0:T(8,128)S(1)} %get-tuple-element.54.live_rows, f32[24,128]{1,0:T(8,128)S(1)} %fold_y3.1.mine, f32[24,128]{1,0:T(8,128)S(1)} %collective-permute-done.42.other, f32[3072,1536]{1,0:T(8,128)S(1)} %get-tuple-element.89.tile, ...), custom_call_target="tpu_custom_call" | custom-call | tf_op jit(solution)/shard_map/step6/pallas_call | solution.py:718
  128.2 1.3 collective-permute-start.43
  130.3 2.1 %collective-permute-done.44.p2 = f32[16,128]{1,0:T(8,128)S(1)} collective-permute-done((f32[16,128]{1,0:T(8,128)S(1)}, f32[16,128]{1,0:T(8,128)S(1)}, u32[]{:S(2)}, u32[]{:S(2)}) %collective-permute-start.44) | collective-permute-done | bytes 8224 | tf_op jit(solution)/shard_map/ppermute | solution.py:562
  (62 shorter events, 16.9 us)
Async XLA Ops:
  2.9 11.7 %collective-permute-start.4 = (f32[136,768]{1,0:T(8,128)S(1)}, f32[136,768]{1,0:T(8,128)S(1)}, u32[]{:S(2)}, u32[]{:S(2)}) collective-permute-start(f32[136,768]{1,0:T(8,128)S(1)} %get-tuple-element.56), channel_id=1, source_target_pairs={{0,32},{32,0},{64,96},{96,64},{1,33},{33,1},{65,97},{97,65},{2,34}... | collective-permute-start | bytes 1253384 | tf_op jit(solution)/shard_map/ppermute | solution.py:557
  5.0 13.6 %collective-permute-start.2 = (bf16[384,768]{1,0:T(8,128)(2,1)}, bf16[384,768]{1,0:T(8,128)(2,1)S(1)}, u32[]{:S(2)}, u32[]{:S(2)}) collective-permute-start(bf16[384,768]{1,0:T(8,128)(2,1)} %own), channel_id=1, source_target_pairs={{0,2},{1,7},{2,4},{3,1},{4,6},{5,3},{6,0},{7,5},{8,10},{9,15},{10,... | collective-permute-start | bytes 1769480 | tf_op jit(solution)/shard_map/ppermute | solution.py:562
  6.5 16.7 %collective-permute-start.1 = (bf16[384,768]{1,0:T(8,128)(2,1)}, bf16[384,768]{1,0:T(8,128)(2,1)S(1)}, u32[]{:S(2)}, u32[]{:S(2)}) collective-permute-start(bf16[384,768]{1,0:T(8,128)(2,1)} %own), channel_id=1, source_target_pairs={{0,24},{1,9},{8,0},{9,17},{16,8},{17,25},{24,16},{25,1},{2,26},{3,... | collective-permute-start | bytes 1769480 | tf_op jit(solution)/shard_map/ppermute | solution.py:562
  9.3 14.6 %collective-permute-start = (bf16[384,768]{1,0:T(8,128)(2,1)}, bf16[384,768]{1,0:T(8,128)(2,1)S(1)}, u32[]{:S(2)}, u32[]{:S(2)}) collective-permute-start(bf16[384,768]{1,0:T(8,128)(2,1)} %own), channel_id=1, source_target_pairs={{0,8},{1,25},{8,16},{9,1},{16,24},{17,9},{24,0},{25,17},{2,10},{3,... | collective-permute-start | bytes 1769480 | tf_op jit(solution)/shard_map/ppermute | solution.py:562
  9.3 14.6 %collective-permute-start.3 = (bf16[384,768]{1,0:T(8,128)(2,1)}, bf16[384,768]{1,0:T(8,128)(2,1)S(1)}, u32[]{:S(2)}, u32[]{:S(2)}) collective-permute-start(bf16[384,768]{1,0:T(8,128)(2,1)} %own), channel_id=1, source_target_pairs={{0,6},{1,3},{2,0},{3,5},{4,2},{5,7},{6,4},{7,1},{8,14},{9,11},{10,... | collective-permute-start | bytes 1769480 | tf_op jit(solution)/shard_map/ppermute | solution.py:562
  14.7 9.2 %collective-permute-start.5 = (f32[72,768]{1,0:T(8,128)S(1)}, f32[72,768]{1,0:T(8,128)S(1)}, u32[]{:S(2)}, u32[]{:S(2)}) collective-permute-start(f32[72,768]{1,0:T(8,128)S(1)} %get-tuple-element.57), channel_id=1, source_target_pairs={{0,96},{32,64},{64,32},{96,0},{1,97},{33,65},{65,33},{97,1},{2,98}... | collective-permute-start | bytes 663560 | tf_op jit(solution)/shard_map/ppermute | solution.py:557
  23.9 13.0 %collective-permute-start.6 = (bf16[384,768]{1,0:T(8,128)(2,1)S(1)}, bf16[384,768]{1,0:T(8,128)(2,1)S(1)}, u32[]{:S(2)}, u32[]{:S(2)}) collective-permute-start(bf16[384,768]{1,0:T(8,128)(2,1)S(1)} %collective-permute-done.x1), channel_id=1, source_target_pairs={{0,8},{1,25},{8,16},{9,1},{16,24},{17,9},{24,0},{25,17},{2,10},{3,... | collective-permute-start | bytes 1769480 | tf_op jit(solution)/shard_map/ppermute | solution.py:562
  24.6 12.3 %collective-permute-start.7 = (bf16[384,768]{1,0:T(8,128)(2,1)S(1)}, bf16[384,768]{1,0:T(8,128)(2,1)S(1)}, u32[]{:S(2)}, u32[]{:S(2)}) collective-permute-start(bf16[384,768]{1,0:T(8,128)(2,1)S(1)} %collective-permute-done.2.y1), channel_id=1, source_target_pairs={{0,2},{1,7},{2,4},{3,1},{4,6},{5,3},{6,0},{7,5},{8,10},{9,15},{10,... | collective-permute-start | bytes 1769480 | tf_op jit(solution)/shard_map/ppermute | solution.py:562
  26.4 8.3 %collective-permute-start.10 = (bf16[64,896]{1,0:T(8,128)(2,1)S(1)}, bf16[64,896]{1,0:T(8,128)(2,1)S(1)}, u32[]{:S(2)}, u32[]{:S(2)}) collective-permute-start(bf16[64,896]{1,0:T(8,128)(2,1)S(1)} %means.1.p0), channel_id=1, source_target_pairs={{0,96},{32,64},{64,32},{96,0},{1,97},{33,65},{65,33},{97,1},{2,98}... | collective-permute-start | bytes 344072 | tf_op jit(solution)/shard_map/ppermute | solution.py:557
  29.4 7.5 %collective-permute-start.9 = (bf16[64,896]{1,0:T(8,128)(2,1)S(1)}, bf16[64,896]{1,0:T(8,128)(2,1)S(1)}, u32[]{:S(2)}, u32[]{:S(2)}) collective-permute-start(bf16[64,896]{1,0:T(8,128)(2,1)S(1)} %means.1.p0), channel_id=1, source_target_pairs={{0,64},{32,96},{64,0},{96,32},{1,65},{33,97},{65,1},{97,33},{2,66}... | collective-permute-start | bytes 344072 | tf_op jit(solution)/shard_map/ppermute | solution.py:557
  29.4 7.5 %collective-permute-start.8 = (bf16[64,896]{1,0:T(8,128)(2,1)S(1)}, bf16[64,896]{1,0:T(8,128)(2,1)S(1)}, u32[]{:S(2)}, u32[]{:S(2)}) collective-permute-start(bf16[64,896]{1,0:T(8,128)(2,1)S(1)} %means.1.p0), channel_id=1, source_target_pairs={{0,32},{32,0},{64,96},{96,64},{1,33},{33,1},{65,97},{97,65},{2,34}... | collective-permute-start | bytes 344072 | tf_op jit(solution)/shard_map/ppermute | solution.py:557
  37.0 2.3 %collective-permute-start.11 = (bf16[384,768]{1,0:T(8,128)(2,1)}, bf16[384,768]{1,0:T(8,128)(2,1)S(1)}, u32[]{:S(2)}, u32[]{:S(2)}) collective-permute-start(bf16[384,768]{1,0:T(8,128)(2,1)} %own), channel_id=1, source_target_pairs={{0,1},{1,0},{2,3},{3,2},{4,5},{5,4},{6,7},{7,6},{8,9},{9,8},{10,11... | collective-permute-start | bytes 1769480 | tf_op jit(solution)/shard_map/ppermute | solution.py:557
  37.1 3.8 %collective-permute-start.12 = (bf16[384,768]{1,0:T(8,128)(2,1)S(1)}, bf16[384,768]{1,0:T(8,128)(2,1)S(1)}, u32[]{:S(2)}, u32[]{:S(2)}) collective-permute-start(bf16[384,768]{1,0:T(8,128)(2,1)S(1)} %collective-permute-done.2.y1), channel_id=1, source_target_pairs={{0,1},{1,0},{2,3},{3,2},{4,5},{5,4},{6,7},{7,6},{8,9},{9,8},{10,11... | collective-permute-start | bytes 1769480 | tf_op jit(solution)/shard_map/ppermute | solution.py:557
  37.5 4.0 %collective-permute-start.13 = (bf16[384,768]{1,0:T(8,128)(2,1)S(1)}, bf16[384,768]{1,0:T(8,128)(2,1)S(1)}, u32[]{:S(2)}, u32[]{:S(2)}) collective-permute-start(bf16[384,768]{1,0:T(8,128)(2,1)S(1)} %collective-permute-done.7.y2), channel_id=1, source_target_pairs={{0,1},{1,0},{2,3},{3,2},{4,5},{5,4},{6,7},{7,6},{8,9},{9,8},{10,11... | collective-permute-start | bytes 1769480 | tf_op jit(solution)/shard_map/ppermute | solution.py:557
  37.6 5.2 %collective-permute-start.14 = (bf16[384,768]{1,0:T(8,128)(2,1)S(1)}, bf16[384,768]{1,0:T(8,128)(2,1)S(1)}, u32[]{:S(2)}, u32[]{:S(2)}) collective-permute-start(bf16[384,768]{1,0:T(8,128)(2,1)S(1)} %collective-permute-done.3.y3), channel_id=1, source_target_pairs={{0,1},{1,0},{2,3},{3,2},{4,5},{5,4},{6,7},{7,6},{8,9},{9,8},{10,11... | collective-permute-start | bytes 1769480 | tf_op jit(solution)/shard_map/ppermute | solution.py:557
  38.2 15.3 %collective-permute-start.18 = (bf16[256,768]{1,0:T(8,128)(2,1)S(1)}, bf16[256,768]{1,0:T(8,128)(2,1)S(1)}, u32[]{:S(2)}, u32[]{:S(2)}) collective-permute-start(bf16[256,768]{1,0:T(8,128)(2,1)S(1)} %get-tuple-element.75.own), channel_id=1, source_target_pairs={{0,6},{1,3},{2,0},{3,5},{4,2},{5,7},{6,4},{7,1},{8,14},{9,11},{10,... | collective-permute-start | bytes 1179656 | tf_op jit(solution)/shard_map/ppermute | solution.py:562
  39.3 14.3 %collective-permute-start.17 = (bf16[256,768]{1,0:T(8,128)(2,1)S(1)}, bf16[256,768]{1,0:T(8,128)(2,1)S(1)}, u32[]{:S(2)}, u32[]{:S(2)}) collective-permute-start(bf16[256,768]{1,0:T(8,128)(2,1)S(1)} %get-tuple-element.75.own), channel_id=1, source_target_pairs={{0,2},{1,7},{2,4},{3,1},{4,6},{5,3},{6,0},{7,5},{8,10},{9,15},{10,... | collective-permute-start | bytes 1179656 | tf_op jit(solution)/shard_map/ppermute | solution.py:562
  40.8 12.8 %collective-permute-start.16 = (bf16[256,768]{1,0:T(8,128)(2,1)S(1)}, bf16[256,768]{1,0:T(8,128)(2,1)S(1)}, u32[]{:S(2)}, u32[]{:S(2)}) collective-permute-start(bf16[256,768]{1,0:T(8,128)(2,1)S(1)} %get-tuple-element.75.own), channel_id=1, source_target_pairs={{0,24},{1,9},{8,0},{9,17},{16,8},{17,25},{24,16},{25,1},{2,26},{3,... | collective-permute-start | bytes 1179656 | tf_op jit(solution)/shard_map/ppermute | solution.py:562
  41.6 12.0 %collective-permute-start.15 = (bf16[256,768]{1,0:T(8,128)(2,1)S(1)}, bf16[256,768]{1,0:T(8,128)(2,1)S(1)}, u32[]{:S(2)}, u32[]{:S(2)}) collective-permute-start(bf16[256,768]{1,0:T(8,128)(2,1)S(1)} %get-tuple-element.75.own), channel_id=1, source_target_pairs={{0,8},{1,25},{8,16},{9,1},{16,24},{17,9},{24,0},{25,17},{2,10},{3,... | collective-permute-start | bytes 1179656 | tf_op jit(solution)/shard_map/ppermute | solution.py:562
  53.6 9.1 %collective-permute-start.20 = (bf16[256,768]{1,0:T(8,128)(2,1)S(1)}, bf16[256,768]{1,0:T(8,128)(2,1)S(1)}, u32[]{:S(2)}, u32[]{:S(2)}) collective-permute-start(bf16[256,768]{1,0:T(8,128)(2,1)S(1)} %collective-permute-done.17.y1), channel_id=1, source_target_pairs={{0,2},{1,7},{2,4},{3,1},{4,6},{5,3},{6,0},{7,5},{8,10},{9,15},{10,... | collective-permute-start | bytes 1179656 | tf_op jit(solution)/shard_map/ppermute | solution.py:562
  54.8 9.5 %collective-permute-start.22 = (bf16[256,768]{1,0:T(8,128)(2,1)S(1)}, bf16[256,768]{1,0:T(8,128)(2,1)S(1)}, u32[]{:S(2)}, u32[]{:S(2)}) collective-permute-start(bf16[256,768]{1,0:T(8,128)(2,1)S(1)} %collective-permute-done.17.y1), channel_id=1, source_target_pairs={{0,1},{1,0},{2,3},{3,2},{4,5},{5,4},{6,7},{7,6},{8,9},{9,8},{10,11... | collective-permute-start | bytes 1179656 | tf_op jit(solution)/shard_map/ppermute | solution.py:557
  54.8 7.9 %collective-permute-start.21 = (bf16[256,768]{1,0:T(8,128)(2,1)S(1)}, bf16[256,768]{1,0:T(8,128)(2,1)S(1)}, u32[]{:S(2)}, u32[]{:S(2)}) collective-permute-start(bf16[256,768]{1,0:T(8,128)(2,1)S(1)} %get-tuple-element.75.own), channel_id=1, source_target_pairs={{0,1},{1,0},{2,3},{3,2},{4,5},{5,4},{6,7},{7,6},{8,9},{9,8},{10,11... | collective-permute-start | bytes 1179656 | tf_op jit(solution)/shard_map/ppermute | solution.py:557
  55.3 9.0 %collective-permute-start.19 = (bf16[256,768]{1,0:T(8,128)(2,1)S(1)}, bf16[256,768]{1,0:T(8,128)(2,1)S(1)}, u32[]{:S(2)}, u32[]{:S(2)}) collective-permute-start(bf16[256,768]{1,0:T(8,128)(2,1)S(1)} %collective-permute-done.15.x1), channel_id=1, source_target_pairs={{0,8},{1,25},{8,16},{9,1},{16,24},{17,9},{24,0},{25,17},{2,10},{3,... | collective-permute-start | bytes 1179656 | tf_op jit(solution)/shard_map/ppermute | solution.py:562
  55.7 8.6 %collective-permute-start.24 = (bf16[256,768]{1,0:T(8,128)(2,1)S(1)}, bf16[256,768]{1,0:T(8,128)(2,1)S(1)}, u32[]{:S(2)}, u32[]{:S(2)}) collective-permute-start(bf16[256,768]{1,0:T(8,128)(2,1)S(1)} %collective-permute-done.18.y3), channel_id=1, source_target_pairs={{0,1},{1,0},{2,3},{3,2},{4,5},{5,4},{6,7},{7,6},{8,9},{9,8},{10,11... | collective-permute-start | bytes 1179656 | tf_op jit(solution)/shard_map/ppermute | solution.py:557
  62.7 1.7 %collective-permute-start.23 = (bf16[256,768]{1,0:T(8,128)(2,1)S(1)}, bf16[256,768]{1,0:T(8,128)(2,1)S(1)}, u32[]{:S(2)}, u32[]{:S(2)}) collective-permute-start(bf16[256,768]{1,0:T(8,128)(2,1)S(1)} %collective-permute-done.20.y2), channel_id=1, source_target_pairs={{0,1},{1,0},{2,3},{3,2},{4,5},{5,4},{6,7},{7,6},{8,9},{9,8},{10,11... | collective-permute-start | bytes 1179656 | tf_op jit(solution)/shard_map/ppermute | solution.py:557
  71.7 3.8 %collective-permute-start.27 = (f32[24,128]{1,0:T(8,128)S(1)}, f32[24,128]{1,0:T(8,128)S(1)}, u32[]{:S(2)}, u32[]{:S(2)}) collective-permute-start(f32[24,128]{1,0:T(8,128)S(1)} %get-tuple-element.81.r_0_), channel_id=1, source_target_pairs={{0,6},{1,3},{2,0},{3,5},{4,2},{5,7},{6,4},{7,1},{8,14},{9,11},{10,... | collective-permute-start | bytes 36872 | tf_op jit(solution)/shard_map/ppermute | solution.py:562
  73.8 5.2 %collective-permute-start.26 = (f32[24,128]{1,0:T(8,128)S(1)}, f32[24,128]{1,0:T(8,128)S(1)}, u32[]{:S(2)}, u32[]{:S(2)}) collective-permute-start(f32[24,128]{1,0:T(8,128)S(1)} %get-tuple-element.81.r_0_), channel_id=1, source_target_pairs={{0,4},{1,5},{2,6},{3,7},{4,0},{5,1},{6,2},{7,3},{8,12},{9,13},{10,... | collective-permute-start | bytes 36872 | tf_op jit(solution)/shard_map/ppermute | solution.py:562
  74.8 4.9 %collective-permute-start.25 = (f32[24,128]{1,0:T(8,128)S(1)}, f32[24,128]{1,0:T(8,128)S(1)}, u32[]{:S(2)}, u32[]{:S(2)}) collective-permute-start(f32[24,128]{1,0:T(8,128)S(1)} %get-tuple-element.81.r_0_), channel_id=1, source_target_pairs={{0,2},{1,7},{2,4},{3,1},{4,6},{5,3},{6,0},{7,5},{8,10},{9,15},{10,... | collective-permute-start | bytes 36872 | tf_op jit(solution)/shard_map/ppermute | solution.py:562
  79.8 1.3 collective-permute-start.28
  82.5 3.8 %collective-permute-start.31 = (f32[32,128]{1,0:T(8,128)S(1)}, f32[32,128]{1,0:T(8,128)S(1)}, u32[]{:S(2)}, u32[]{:S(2)}) collective-permute-start(f32[32,128]{1,0:T(8,128)S(1)} %get-tuple-element.88.p0), channel_id=1, source_target_pairs={{0,24},{1,9},{8,0},{9,17},{16,8},{17,25},{24,16},{25,1},{2,26},{3,... | collective-permute-start | bytes 49160 | tf_op jit(solution)/shard_map/ppermute | solution.py:562
  83.6 5.2 %collective-permute-start.30 = (f32[32,128]{1,0:T(8,128)S(1)}, f32[32,128]{1,0:T(8,128)S(1)}, u32[]{:S(2)}, u32[]{:S(2)}) collective-permute-start(f32[32,128]{1,0:T(8,128)S(1)} %get-tuple-element.88.p0), channel_id=1, source_target_pairs={{0,16},{1,17},{8,24},{9,25},{16,0},{17,1},{24,8},{25,9},{2,18},{3,... | collective-permute-start | bytes 49160 | tf_op jit(solution)/shard_map/ppermute | solution.py:562
  84.0 5.1 %collective-permute-start.29 = (f32[32,128]{1,0:T(8,128)S(1)}, f32[32,128]{1,0:T(8,128)S(1)}, u32[]{:S(2)}, u32[]{:S(2)}) collective-permute-start(f32[32,128]{1,0:T(8,128)S(1)} %get-tuple-element.88.p0), channel_id=1, source_target_pairs={{0,8},{1,25},{8,16},{9,1},{16,24},{17,9},{24,0},{25,17},{2,10},{3,... | collective-permute-start | bytes 49160 | tf_op jit(solution)/shard_map/ppermute | solution.py:562
  92.3 3.9 %collective-permute-start.34 = (f32[40,128]{1,0:T(8,128)S(1)}, f32[40,128]{1,0:T(8,128)S(1)}, u32[]{:S(2)}, u32[]{:S(2)}) collective-permute-start(f32[40,128]{1,0:T(8,128)S(1)} %get-tuple-element.93.r_0_), channel_id=1, source_target_pairs={{0,6},{1,3},{2,0},{3,5},{4,2},{5,7},{6,4},{7,1},{8,14},{9,11},{10,... | collective-permute-start | bytes 61448 | tf_op jit(solution)/shard_map/ppermute | solution.py:562
  93.7 5.3 %collective-permute-start.33 = (f32[40,128]{1,0:T(8,128)S(1)}, f32[40,128]{1,0:T(8,128)S(1)}, u32[]{:S(2)}, u32[]{:S(2)}) collective-permute-start(f32[40,128]{1,0:T(8,128)S(1)} %get-tuple-element.93.r_0_), channel_id=1, source_target_pairs={{0,4},{1,5},{2,6},{3,7},{4,0},{5,1},{6,2},{7,3},{8,12},{9,13},{10,... | collective-permute-start | bytes 61448 | tf_op jit(solution)/shard_map/ppermute | solution.py:562
  94.6 5.0 %collective-permute-start.32 = (f32[40,128]{1,0:T(8,128)S(1)}, f32[40,128]{1,0:T(8,128)S(1)}, u32[]{:S(2)}, u32[]{:S(2)}) collective-permute-start(f32[40,128]{1,0:T(8,128)S(1)} %get-tuple-element.93.r_0_), channel_id=1, source_target_pairs={{0,2},{1,7},{2,4},{3,1},{4,6},{5,3},{6,0},{7,5},{8,10},{9,15},{10,... | collective-permute-start | bytes 61448 | tf_op jit(solution)/shard_map/ppermute | solution.py:562
  99.7 1.3 collective-permute-start.35
  104.8 3.8 %collective-permute-start.38 = (f32[24,128]{1,0:T(8,128)S(1)}, f32[24,128]{1,0:T(8,128)S(1)}, u32[]{:S(2)}, u32[]{:S(2)}) collective-permute-start(f32[24,128]{1,0:T(8,128)S(1)} %step4.1.p0), channel_id=1, source_target_pairs={{0,24},{1,9},{8,0},{9,17},{16,8},{17,25},{24,16},{25,1},{2,26},{3,... | collective-permute-start | bytes 36872 | tf_op jit(solution)/shard_map/ppermute | solution.py:562
  106.1 5.2 %collective-permute-start.37 = (f32[24,128]{1,0:T(8,128)S(1)}, f32[24,128]{1,0:T(8,128)S(1)}, u32[]{:S(2)}, u32[]{:S(2)}) collective-permute-start(f32[24,128]{1,0:T(8,128)S(1)} %step4.1.p0), channel_id=1, source_target_pairs={{0,16},{1,17},{8,24},{9,25},{16,0},{17,1},{24,8},{25,9},{2,18},{3,... | collective-permute-start | bytes 36872 | tf_op jit(solution)/shard_map/ppermute | solution.py:562
  107.0 4.9 %collective-permute-start.36 = (f32[24,128]{1,0:T(8,128)S(1)}, f32[24,128]{1,0:T(8,128)S(1)}, u32[]{:S(2)}, u32[]{:S(2)}) collective-permute-start(f32[24,128]{1,0:T(8,128)S(1)} %step4.1.p0), channel_id=1, source_target_pairs={{0,8},{1,25},{8,16},{9,1},{16,24},{17,9},{24,0},{25,17},{2,10},{3,... | collective-permute-start | bytes 36872 | tf_op jit(solution)/shard_map/ppermute | solution.py:562
  114.3 3.8 %collective-permute-start.41 = (f32[24,128]{1,0:T(8,128)S(1)}, f32[24,128]{1,0:T(8,128)S(1)}, u32[]{:S(2)}, u32[]{:S(2)}) collective-permute-start(f32[24,128]{1,0:T(8,128)S(1)} %get-tuple-element.97.r_0_), channel_id=1, source_target_pairs={{0,6},{1,3},{2,0},{3,5},{4,2},{5,7},{6,4},{7,1},{8,14},{9,11},{10,... | collective-permute-start | bytes 36872 | tf_op jit(solution)/shard_map/ppermute | solution.py:562
  116.4 5.2 %collective-permute-start.40 = (f32[24,128]{1,0:T(8,128)S(1)}, f32[24,128]{1,0:T(8,128)S(1)}, u32[]{:S(2)}, u32[]{:S(2)}) collective-permute-start(f32[24,128]{1,0:T(8,128)S(1)} %get-tuple-element.97.r_0_), channel_id=1, source_target_pairs={{0,4},{1,5},{2,6},{3,7},{4,0},{5,1},{6,2},{7,3},{8,12},{9,13},{10,... | collective-permute-start | bytes 36872 | tf_op jit(solution)/shard_map/ppermute | solution.py:562
  117.3 4.9 %collective-permute-start.39 = (f32[24,128]{1,0:T(8,128)S(1)}, f32[24,128]{1,0:T(8,128)S(1)}, u32[]{:S(2)}, u32[]{:S(2)}) collective-permute-start(f32[24,128]{1,0:T(8,128)S(1)} %get-tuple-element.97.r_0_), channel_id=1, source_target_pairs={{0,2},{1,7},{2,4},{3,1},{4,6},{5,3},{6,0},{7,5},{8,10},{9,15},{10,... | collective-permute-start | bytes 36872 | tf_op jit(solution)/shard_map/ppermute | solution.py:562
  122.3 1.3 collective-permute-start.42
  126.6 3.7 %collective-permute-start.45 = (f32[16,128]{1,0:T(8,128)S(1)}, f32[16,128]{1,0:T(8,128)S(1)}, u32[]{:S(2)}, u32[]{:S(2)}) collective-permute-start(f32[16,128]{1,0:T(8,128)S(1)} %get-tuple-element.98.p0), channel_id=1, source_target_pairs={{0,24},{1,9},{8,0},{9,17},{16,8},{17,25},{24,16},{25,1},{2,26},{3,... | collective-permute-start | bytes 24584 | tf_op jit(solution)/shard_map/ppermute | solution.py:562
  127.3 5.2 %collective-permute-start.44 = (f32[16,128]{1,0:T(8,128)S(1)}, f32[16,128]{1,0:T(8,128)S(1)}, u32[]{:S(2)}, u32[]{:S(2)}) collective-permute-start(f32[16,128]{1,0:T(8,128)S(1)} %get-tuple-element.98.p0), channel_id=1, source_target_pairs={{0,16},{1,17},{8,24},{9,25},{16,0},{17,1},{24,8},{25,9},{2,18},{3,... | collective-permute-start | bytes 24584 | tf_op jit(solution)/shard_map/ppermute | solution.py:562
  128.2 4.9 %collective-permute-start.43 = (f32[16,128]{1,0:T(8,128)S(1)}, f32[16,128]{1,0:T(8,128)S(1)}, u32[]{:S(2)}, u32[]{:S(2)}) collective-permute-start(f32[16,128]{1,0:T(8,128)S(1)} %get-tuple-element.98.p0), channel_id=1, source_target_pairs={{0,8},{1,25},{8,16},{9,1},{16,24},{17,9},{24,0},{25,17},{2,10},{3,... | collective-permute-start | bytes 24584 | tf_op jit(solution)/shard_map/ppermute | solution.py:562

commit v2 on v1

--- a/solution.py
+++ b/solution.py
@@ -69,6 +69,23 @@
         )
 
 
+def to_rows_by_product(vals, out_ref):
+    k = vals.shape[0]
+    parts, rest = [], jnp.concatenate([vals, jnp.zeros((32 - k, 128), F32)], axis=0)
+    for _ in range(3):
+        part = rest.astype(BF16).astype(F32)
+        parts.append(part)
+        rest = rest - part
+    cols = jnp.transpose(jnp.concatenate([*parts, jnp.zeros((32, 128), F32)], axis=0)).astype(BF16)
+    which = jnp.bitwise_and(iota((128, 128), 0), 31)
+    step = 8
+    for j in range(0, k, step):
+        pick = jnp.concatenate([jnp.where(which == j + i, 1.0, 0.0).astype(BF16) for i in range(step)], axis=1)
+        wide = jnp.dot(cols, pick, preferred_element_type=F32)
+        for i in range(step):
+            out_ref[(j + i) * 128:(j + i + 1) * 128, :] = wide[:, i * 128:(i + 1) * 128]
+
+
 def lse2(parts):
     top = parts[0]
     for p in parts[1:]:
@@ -79,9 +96,14 @@
     return top + jnp.log2(total)
 
 
-def in_range(total, peak):
-    outside = jnp.sum(jnp.where((total > LOW) & (total < HIGH), 0.0, 1.0))
-    return (outside == 0.0) & (peak <= PEAK)
+def most_of(x):
+    return jnp.max(jnp.max(x, axis=0, keepdims=True), axis=1, keepdims=True)
+
+
+def out_of_range(total, peak):
+    bad = jnp.sum(jnp.where((total > LOW) & (total < HIGH), 0.0, 1.0), axis=0, keepdims=True)
+    bad = bad + jnp.sum(jnp.where(peak <= PEAK, 0.0, 1.0), axis=0, keepdims=True)
+    return jnp.sum(bad) > 0.0
 
 
 def spread(vals, wide_ref):
@@ -91,20 +113,17 @@
 
 def store_lse(total, shift, peak, out_ref, safe):
     n = total.shape[0]
-    good = in_range(total, peak)
-
-    @pl.when(good)
-    def _():
-        out_ref[0:n, :] = jnp.log2(total) + shift
-
-    @pl.when(jnp.logical_not(good))
+    bad = out_of_range(total, peak)
+    out_ref[0:n, :] = jnp.log2(total) + shift
+
+    @pl.when(bad)
     def _():
         safe()
 
 
 def reduce_columns(tile, h, guard, out_ref, wide_ref, backup, live=None):
     rows, cols = tile.shape
-    shift = jnp.max(h)
+    shift = most_of(h)
     spread(jnp.exp2(h - shift), wide_ref)
     lane, sub = iota((8, 128), 1), iota((8, 128), 0)
 
@@ -121,14 +140,14 @@
     total = out_ref[0:rows // 128, :]
     if live is not None:
         total = jnp.where(live[...] > 0.0, total, 1.0)
-    store_lse(total, shift, jnp.max(guard[...]), out_ref, lambda: safe_columns(backup, h, out_ref, wide_ref))
+    store_lse(total, shift, guard[...], out_ref, lambda: safe_columns(backup, h, out_ref, wide_ref))
 
 
 def reduce_rows(tile, h, guard, out_ref, tall_ref, backup):
     rows, cols = tile.shape
-    shift = jnp.max(h)
-    to_rows(jnp.exp2(h - shift), tall_ref)
-    width, chunk = 512, 64
+    shift = most_of(h)
+    to_rows_by_product(jnp.exp2(h - shift), tall_ref)
+    width, chunk = cols // 2, 64
     groups = width // 128
     for strip in range(cols // width):
         at = pl.ds(strip * width, width)
@@ -144,7 +163,7 @@
             row = strip * groups + k
             out_ref[row:row + 1, :] = acc[:, k * 128:(k + 1) * 128]
     store_lse(
-        out_ref[0:cols // 128, :], shift, jnp.max(guard[...]), out_ref,
+        out_ref[0:cols // 128, :], shift, guard[...], out_ref,
         lambda: safe_rows(backup, h, out_ref, tall_ref),
     )
 
@@ -435,10 +454,9 @@
 
     lax.fori_loop(0, rows // 128, body, 0, unroll=4)
     total = payload[0:rows // 128, :]
-    most = jnp.max(total)
-    peak[...] = jnp.full(peak.shape, most, F32)
+    peak[...] = jnp.broadcast_to(most_of(total), peak.shape)
     store_lse(
-        total, 0.0, most, payload,
+        total, 0.0, peak[...], payload,
         lambda: safe_columns(
             (rows_out, cols_out, n, a_buf, b_buf, sem), jnp.zeros((cols // 128, 128), F32), payload, wide
         ),
@@ -460,10 +478,9 @@
     for k in range(cols // 128):
         part[k:k + 1, :] = total[:, k * 128:(k + 1) * 128]
     h = jnp.where(live_rows[...] > 0.0, 0.0, NEG)
-    most = jnp.max(total)
-    peak[...] = jnp.full(peak.shape, most, F32)
+    peak[...] = jnp.broadcast_to(most_of(total), peak.shape)
     store_lse(
-        part[...], 0.0, most, part,
+        part[...], 0.0, peak[...], part,
         lambda: safe_rows((rows_out, cols_out, n, a_buf, b_buf, sem), h, part, tall),
     )
 

time: 134 us -> 133 us (level)
  no operation moved by 1% of the time
where the time goes in v2:
time: 133 us
  waiting for transfers between devices  50.6 us (38%)
  starting transfers between devices  46.2 us (35%)
  Pallas kernels  34.3 us (26%)
    ppermute x30, waiting for transfers between devices, turn(): lax.ppermute(v, (axis, 'c'), [(i * 2 + c, (i + (k if c == 0 else n - k))...  36.9 us
    ppermute x30, starting transfers between devices, turn(): lax.ppermute(v, (axis, 'c'), [(i * 2 + c, (i + (k if c == 0 else n - k))...  33 us
    ppermute x16, waiting for transfers between devices, swap(): return lax.ppermute(v, axis, [(i, i ^ bit) for i in range(n)])  13.7 us
    ppermute x16, starting transfers between devices, swap(): return lax.ppermute(v, axis, [(i, i ^ bit) for i in range(n)])  13.2 us
    pallas_call x1, Pallas kernels, local(): tile_call(fine_tile_kernel, n_rows, n_cols, n_cols // 128, [SMEM, VMEM] +...  10.8 us
    pallas_call x1, Pallas kernels, local(): tile_call(coarse_tile_kernel, k_rows, k_cols, 24, [ANY] * 11 + [VMEM], [p...  7.4 us
    pallas_call x1, Pallas kernels, local(): call(step4_kernel, sds((24, 128)), [VMEM, VMEM] + [VMEM] * 3 + kspecs * 2...  3.65 us
    pallas_call x1, Pallas kernels, local(): call(step3_kernel, [sds((40, 128)), sds((8, 128)), sds((12, 128))], [VMEM...  3.21 us
  transfers between devices with their start and end apart: 46, of which 29 were waited for; matrix products, arithmetic and copies ran while one was open for 0% of the time, Pallas kernels for 8%

profile of v2, /device:TPU:0, one launch (start us, length us, event | category | flops | bytes accessed | tf_op | source)
XLA Modules:
  0.0 133.2 jit_solution(16509198584337813370)
XLA Ops:
  1.4 1.5 %pool.1 = (f32[136,768]{1,0:T(8,128)S(1)}, f32[136,768]{1,0:T(8,128)S(1)}, f32[24,128]{1,0:T(8,128)S(1)}, f32[12,128]{1,0:T(8,128)S(1)}, f32[3,128]{1,0:T(4,128)S(1)}, /*index=5*/f32[8,128]{1,0:T(8,128)S(1)}) custom-call(s32[8,128]{1,0:T(8,128)S(1)} %fusion.info.table, bf16[384,768]{1,0:T(8,128)(2,1)} %own, s32[8,128]{1,0:T(8,128)S(1)} %fusion.info.table), custom_call_target="tpu_custom_call" | custom-call | tf_op jit(solution)/shard_map/pool/pallas_call | solution.py:617
  2.9 2.1 %collective-permute-start.4 = (f32[136,768]{1,0:T(8,128)S(1)}, f32[136,768]{1,0:T(8,128)S(1)}, u32[]{:S(2)}, u32[]{:S(2)}) collective-permute-start(f32[136,768]{1,0:T(8,128)S(1)} %get-tuple-element.56), channel_id=1, source_target_pairs={{0,32},{32,0},{64,96},{96,64},{1,33},{33,1},{65,97},{97,65},{2,34}... | collective-permute-start | bytes 1253384 | tf_op jit(solution)/shard_map/ppermute | solution.py:574
  5.0 1.6 %collective-permute-start.2 = (bf16[384,768]{1,0:T(8,128)(2,1)}, bf16[384,768]{1,0:T(8,128)(2,1)S(1)}, u32[]{:S(2)}, u32[]{:S(2)}) collective-permute-start(bf16[384,768]{1,0:T(8,128)(2,1)} %own), channel_id=1, source_target_pairs={{0,2},{1,7},{2,4},{3,1},{4,6},{5,3},{6,0},{7,5},{8,10},{9,15},{10,... | collective-permute-start | bytes 1769480 | tf_op jit(solution)/shard_map/ppermute | solution.py:579
  6.5 2.8 %collective-permute-start.1 = (bf16[384,768]{1,0:T(8,128)(2,1)}, bf16[384,768]{1,0:T(8,128)(2,1)S(1)}, u32[]{:S(2)}, u32[]{:S(2)}) collective-permute-start(bf16[384,768]{1,0:T(8,128)(2,1)} %own), channel_id=1, source_target_pairs={{0,24},{1,9},{8,0},{9,17},{16,8},{17,25},{24,16},{25,1},{2,26},{3,... | collective-permute-start | bytes 1769480 | tf_op jit(solution)/shard_map/ppermute | solution.py:579
  9.3 1.7 %collective-permute-start.3 = (bf16[384,768]{1,0:T(8,128)(2,1)}, bf16[384,768]{1,0:T(8,128)(2,1)S(1)}, u32[]{:S(2)}, u32[]{:S(2)}) collective-permute-start(bf16[384,768]{1,0:T(8,128)(2,1)} %own), channel_id=1, source_target_pairs={{0,6},{1,3},{2,0},{3,5},{4,2},{5,7},{6,4},{7,1},{8,14},{9,11},{10,... | collective-permute-start | bytes 1769480 | tf_op jit(solution)/shard_map/ppermute | solution.py:579
  11.0 3.6 %collective-permute-done.4.got = f32[136,768]{1,0:T(8,128)S(1)} collective-permute-done((f32[136,768]{1,0:T(8,128)S(1)}, f32[136,768]{1,0:T(8,128)S(1)}, u32[]{:S(2)}, u32[]{:S(2)}) %collective-permute-start.4) | collective-permute-done | bytes 417824 | tf_op jit(solution)/shard_map/ppermute | solution.py:574
  14.7 3.9 %collective-permute-start.5 = (f32[72,768]{1,0:T(8,128)S(1)}, f32[72,768]{1,0:T(8,128)S(1)}, u32[]{:S(2)}, u32[]{:S(2)}) collective-permute-start(f32[72,768]{1,0:T(8,128)S(1)} %get-tuple-element.57), channel_id=1, source_target_pairs={{0,96},{32,64},{64,32},{96,0},{1,97},{33,65},{65,33},{97,1},{2,98}... | collective-permute-start | bytes 663560 | tf_op jit(solution)/shard_map/ppermute | solution.py:574
  18.6 4.7 %collective-permute-done.1.x3 = bf16[384,768]{1,0:T(8,128)(2,1)S(1)} collective-permute-done((bf16[384,768]{1,0:T(8,128)(2,1)}, bf16[384,768]{1,0:T(8,128)(2,1)S(1)}, u32[]{:S(2)}, u32[]{:S(2)}) %collective-permute-start.1) | collective-permute-done | bytes 589856 | tf_op jit(solution)/shard_map/ppermute | solution.py:579
  24.6 1.6 %collective-permute-start.7 = (bf16[384,768]{1,0:T(8,128)(2,1)S(1)}, bf16[384,768]{1,0:T(8,128)(2,1)S(1)}, u32[]{:S(2)}, u32[]{:S(2)}) collective-permute-start(bf16[384,768]{1,0:T(8,128)(2,1)S(1)} %collective-permute-done.2.y1), channel_id=1, source_target_pairs={{0,2},{1,7},{2,4},{3,1},{4,6},{5,3},{6,0},{7,5},{8,10},{9,15},{10,... | collective-permute-start | bytes 1769480 | tf_op jit(solution)/shard_map/ppermute | solution.py:579
  26.4 3.0 %collective-permute-start.10 = (bf16[64,896]{1,0:T(8,128)(2,1)S(1)}, bf16[64,896]{1,0:T(8,128)(2,1)S(1)}, u32[]{:S(2)}, u32[]{:S(2)}) collective-permute-start(bf16[64,896]{1,0:T(8,128)(2,1)S(1)} %means.1.p0), channel_id=1, source_target_pairs={{0,96},{32,64},{64,32},{96,0},{1,97},{33,65},{65,33},{97,1},{2,98}... | collective-permute-start | bytes 344072 | tf_op jit(solution)/shard_map/ppermute | solution.py:574
  29.4 1.1 collective-permute-start.8
  30.6 4.1 %collective-permute-done.10.p3 = bf16[64,896]{1,0:T(8,128)(2,1)S(1)} collective-permute-done((bf16[64,896]{1,0:T(8,128)(2,1)S(1)}, bf16[64,896]{1,0:T(8,128)(2,1)S(1)}, u32[]{:S(2)}, u32[]{:S(2)}) %collective-permute-start.10) | collective-permute-done | bytes 114720 | tf_op jit(solution)/shard_map/ppermute | solution.py:574
  34.7 2.3 %collective-permute-done.9.p2 = bf16[64,896]{1,0:T(8,128)(2,1)S(1)} collective-permute-done((bf16[64,896]{1,0:T(8,128)(2,1)S(1)}, bf16[64,896]{1,0:T(8,128)(2,1)S(1)}, u32[]{:S(2)}, u32[]{:S(2)}) %collective-permute-start.9) | collective-permute-done | bytes 114720 | tf_op jit(solution)/shard_map/ppermute | solution.py:574
  38.2 1.0 collective-permute-start.18
  39.3 1.6 %collective-permute-start.17 = (bf16[256,768]{1,0:T(8,128)(2,1)S(1)}, bf16[256,768]{1,0:T(8,128)(2,1)S(1)}, u32[]{:S(2)}, u32[]{:S(2)}) collective-permute-start(bf16[256,768]{1,0:T(8,128)(2,1)S(1)} %get-tuple-element.75.own), channel_id=1, source_target_pairs={{0,2},{1,7},{2,4},{3,1},{4,6},{5,3},{6,0},{7,5},{8,10},{9,15},{10,... | collective-permute-start | bytes 1179656 | tf_op jit(solution)/shard_map/ppermute | solution.py:579
  41.6 1.3 collective-permute-start.15
  42.9 10.8 %fine_tile.1 = (f32[3072,1536]{1,0:T(8,128)S(1)}, f32[12,128]{1,0:T(8,128)S(1)}, f32[8,128]{1,0:T(8,128)S(1)}, bf16[3072,768]{1,0:T(8,128)(2,1)}, bf16[1536,768]{1,0:T(8,128)(2,1)}) custom-call(s32[8,128]{1,0:T(8,128)S(1)} %fusion.info.table, f32[24,128]{1,0:T(8,128)S(1)} %get-tuple-element.54.live_rows, bf16[384,768]{1,0:T(8,128)(2,1)} %own, ...), custom_call_target="tpu_custom_call" | custom-call | flops 7247757312 | tf_op jit(solution)/shard_map/fine_tile/pallas_call | solution.py:667
  53.7 1.2 collective-permute-start.20
  55.8 1.2 collective-permute-start.24
  57.0 5.7 %collective-permute-done.20.y2 = bf16[256,768]{1,0:T(8,128)(2,1)S(1)} collective-permute-done((bf16[256,768]{1,0:T(8,128)(2,1)S(1)}, bf16[256,768]{1,0:T(8,128)(2,1)S(1)}, u32[]{:S(2)}, u32[]{:S(2)}) %collective-permute-start.20) | collective-permute-done | bytes 393248 | tf_op jit(solution)/shard_map/ppermute | solution.py:579
  62.8 1.6 %collective-permute-done.19.x2 = bf16[256,768]{1,0:T(8,128)(2,1)S(1)} collective-permute-done((bf16[256,768]{1,0:T(8,128)(2,1)S(1)}, bf16[256,768]{1,0:T(8,128)(2,1)S(1)}, u32[]{:S(2)}, u32[]{:S(2)}) %collective-permute-start.19) | collective-permute-done | bytes 393248 | tf_op jit(solution)/shard_map/ppermute | solution.py:579
  64.5 7.4 %coarse_tile.1 = (f32[2048,1024]{1,0:T(8,128)S(1)}, f32[24,128]{1,0:T(8,128)S(1)}, f32[8,128]{1,0:T(8,128)S(1)}, bf16[2048,768]{1,0:T(8,128)(2,1)}, bf16[1024,768]{1,0:T(8,128)(2,1)}) custom-call(bf16[256,768]{1,0:T(8,128)(2,1)S(1)} %get-tuple-element.75.own, bf16[256,768]{1,0:T(8,128)(2,1)S(1)} %collective-permute-done.15.x1, ...), custom_call_target="tpu_custom_call" | custom-call | flops 3221225472 | tf_op jit(solution)/shard_map/coarse_tile/pallas_call | solution.py:675
  71.9 2.1 %collective-permute-start.27 = (f32[24,128]{1,0:T(8,128)S(1)}, f32[24,128]{1,0:T(8,128)S(1)}, u32[]{:S(2)}, u32[]{:S(2)}) collective-permute-start(f32[24,128]{1,0:T(8,128)S(1)} %get-tuple-element.81.r_0_), channel_id=1, source_target_pairs={{0,6},{1,3},{2,0},{3,5},{4,2},{5,7},{6,4},{7,1},{8,14},{9,11},{10,... | collective-permute-start | bytes 36872 | tf_op jit(solution)/shard_map/ppermute | solution.py:579
  74.0 1.0 collective-permute-start.26
  75.6 3.6 %collective-permute-done.26.r_2_ = f32[24,128]{1,0:T(8,128)S(1)} collective-permute-done((f32[24,128]{1,0:T(8,128)S(1)}, f32[24,128]{1,0:T(8,128)S(1)}, u32[]{:S(2)}, u32[]{:S(2)}) %collective-permute-start.26) | collective-permute-done | bytes 12320 | tf_op jit(solution)/shard_map/ppermute | solution.py:579
  80.0 1.2 collective-permute-done.28.other
  81.2 1.4 %coarse2.1 = (f32[32,128]{1,0:T(8,128)S(1)}, f32[16,128]{1,0:T(8,128)S(1)}) custom-call(f32[24,128]{1,0:T(8,128)S(1)} %fold_y1.1.mine, f32[24,128]{1,0:T(8,128)S(1)} %collective-permute-done.28.other, f32[12,128]{1,0:T(8,128)S(1)} %get-tuple-element.82.part, f32[8,128]{1,0:T(8,128)S(1)} %get-tuple-element.80.plog, f32[3,128]{1,0:T(4,128)S(1)} %get-tuple-element.83.seat, ...), custom_call_target="tpu_custom_call" | custom-call | tf_op jit(solution)/shard_map/coarse2/pallas_call | solution.py:689
  82.6 1.1 collective-permute-start.31
  84.1 1.1 collective-permute-start.29
  85.2 1.2 collective-permute-done.31.p3
  86.4 2.6 %collective-permute-done.30.p2 = f32[32,128]{1,0:T(8,128)S(1)} collective-permute-done((f32[32,128]{1,0:T(8,128)S(1)}, f32[32,128]{1,0:T(8,128)S(1)}, u32[]{:S(2)}, u32[]{:S(2)}) %collective-permute-start.30) | collective-permute-done | bytes 16416 | tf_op jit(solution)/shard_map/ppermute | solution.py:579
  89.2 3.2 %step3.1 = (f32[40,128]{1,0:T(8,128)S(1)}, f32[8,128]{1,0:T(8,128)S(1)}, f32[12,128]{1,0:T(8,128)S(1)}) custom-call(f32[8,128]{1,0:T(8,128)S(1)} %get-tuple-element.52.logs, f32[24,128]{1,0:T(8,128)S(1)} %get-tuple-element.54.live_rows, f32[12,128]{1,0:T(8,128)S(1)} %get-tuple-element.53.live_cols, f32[32,128]{1,0:T(8,128)S(1)} %get-tuple-element.88.p0, ...), custom_call_target="tpu_custom_call" | custom-call | tf_op jit(solution)/shard_map/step3/pallas_call | solution.py:697
  92.4 1.4 %collective-permute-start.34 = (f32[40,128]{1,0:T(8,128)S(1)}, f32[40,128]{1,0:T(8,128)S(1)}, u32[]{:S(2)}, u32[]{:S(2)}) collective-permute-start(f32[40,128]{1,0:T(8,128)S(1)} %get-tuple-element.93.r_0_), channel_id=1, source_target_pairs={{0,6},{1,3},{2,0},{3,5},{4,2},{5,7},{6,4},{7,1},{8,14},{9,11},{10,... | collective-permute-start | bytes 61448 | tf_op jit(solution)/shard_map/ppermute | solution.py:579
  94.7 0.9 collective-permute-start.32
  96.2 2.8 %collective-permute-done.33.r_2_ = f32[40,128]{1,0:T(8,128)S(1)} collective-permute-done((f32[40,128]{1,0:T(8,128)S(1)}, f32[40,128]{1,0:T(8,128)S(1)}, u32[]{:S(2)}, u32[]{:S(2)}) %collective-permute-start.33) | collective-permute-done | bytes 20512 | tf_op jit(solution)/shard_map/ppermute | solution.py:579
  99.8 1.2 collective-permute-done.35.other
  101.0 3.7 %step4.1.p0 = f32[24,128]{1,0:T(8,128)S(1)} custom-call(f32[8,128]{1,0:T(8,128)S(1)} %get-tuple-element.52.logs, f32[24,128]{1,0:T(8,128)S(1)} %get-tuple-element.54.live_rows, f32[40,128]{1,0:T(8,128)S(1)} %fold_y2.1.mine, f32[40,128]{1,0:T(8,128)S(1)} %collective-permute-done.35.other, f32[16,128]{1,0:T(8,128)S(1)} %get-tuple-element.94.plog_rows, ...), custom_call_target="tpu_custom_call" | custom-call | tf_op jit(solution)/shard_map/step4/pallas_call | solution.py:712
  104.7 1.3 collective-permute-start.38
  105.9 0.9 collective-permute-start.37
  106.8 1.2 collective-permute-start.36
  108.4 2.7 %collective-permute-done.37.p2 = f32[24,128]{1,0:T(8,128)S(1)} collective-permute-done((f32[24,128]{1,0:T(8,128)S(1)}, f32[24,128]{1,0:T(8,128)S(1)}, u32[]{:S(2)}, u32[]{:S(2)}) %collective-permute-start.37) | collective-permute-done | bytes 12320 | tf_op jit(solution)/shard_map/ppermute | solution.py:579
  111.7 2.4 %step5.1 = (f32[24,128]{1,0:T(8,128)S(1)}, f32[1,128]{1,0:T(1,128)S(1)}) custom-call(f32[8,128]{1,0:T(8,128)S(1)} %get-tuple-element.52.logs, f32[24,128]{1,0:T(8,128)S(1)} %get-tuple-element.54.live_rows, f32[12,128]{1,0:T(8,128)S(1)} %get-tuple-element.53.live_cols, f32[24,128]{1,0:T(8,128)S(1)} %step4.1.p0, f32[24,128]{1,0:T(8,128)S(1)} %collective-permute-done.36.p1, ...), custom_call_target="tpu_custom_call" | custom-call | tf_op jit(solution)/shard_map/step5/pallas_call | solution.py:720
  114.1 2.1 %collective-permute-start.41 = (f32[24,128]{1,0:T(8,128)S(1)}, f32[24,128]{1,0:T(8,128)S(1)}, u32[]{:S(2)}, u32[]{:S(2)}) collective-permute-start(f32[24,128]{1,0:T(8,128)S(1)} %get-tuple-element.97.r_0_), channel_id=1, source_target_pairs={{0,6},{1,3},{2,0},{3,5},{4,2},{5,7},{6,4},{7,1},{8,14},{9,11},{10,... | collective-permute-start | bytes 36872 | tf_op jit(solution)/shard_map/ppermute | solution.py:579
  117.9 3.5 %collective-permute-done.40.r_2_ = f32[24,128]{1,0:T(8,128)S(1)} collective-permute-done((f32[24,128]{1,0:T(8,128)S(1)}, f32[24,128]{1,0:T(8,128)S(1)}, u32[]{:S(2)}, u32[]{:S(2)}) %collective-permute-start.40) | collective-permute-done | bytes 12320 | tf_op jit(solution)/shard_map/ppermute | solution.py:579
  122.2 1.2 collective-permute-done.42.other
  123.3 2.8 %step6.1 = (f32[16,128]{1,0:T(8,128)S(1)}, f32[3,128]{1,0:T(4,128)}) custom-call(f32[8,128]{1,0:T(8,128)S(1)} %get-tuple-element.52.logs, f32[24,128]{1,0:T(8,128)S(1)} %get-tuple-element.54.live_rows, f32[24,128]{1,0:T(8,128)S(1)} %fold_y3.1.mine, f32[24,128]{1,0:T(8,128)S(1)} %collective-permute-done.42.other, f32[3072,1536]{1,0:T(8,128)S(1)} %get-tuple-element.89.tile, ...), custom_call_target="tpu_custom_call" | custom-call | tf_op jit(solution)/shard_map/step6/pallas_call | solution.py:735
  127.8 1.3 collective-permute-start.43
  129.9 2.1 %collective-permute-done.44.p2 = f32[16,128]{1,0:T(8,128)S(1)} collective-permute-done((f32[16,128]{1,0:T(8,128)S(1)}, f32[16,128]{1,0:T(8,128)S(1)}, u32[]{:S(2)}, u32[]{:S(2)}) %collective-permute-start.44) | collective-permute-done | bytes 8224 | tf_op jit(solution)/shard_map/ppermute | solution.py:579
  (62 shorter events, 16.9 us)
Async XLA Ops:
  2.9 11.7 %collective-permute-start.4 = (f32[136,768]{1,0:T(8,128)S(1)}, f32[136,768]{1,0:T(8,128)S(1)}, u32[]{:S(2)}, u32[]{:S(2)}) collective-permute-start(f32[136,768]{1,0:T(8,128)S(1)} %get-tuple-element.56), channel_id=1, source_target_pairs={{0,32},{32,0},{64,96},{96,64},{1,33},{33,1},{65,97},{97,65},{2,34}... | collective-permute-start | bytes 1253384 | tf_op jit(solution)/shard_map/ppermute | solution.py:574
  5.0 13.6 %collective-permute-start.2 = (bf16[384,768]{1,0:T(8,128)(2,1)}, bf16[384,768]{1,0:T(8,128)(2,1)S(1)}, u32[]{:S(2)}, u32[]{:S(2)}) collective-permute-start(bf16[384,768]{1,0:T(8,128)(2,1)} %own), channel_id=1, source_target_pairs={{0,2},{1,7},{2,4},{3,1},{4,6},{5,3},{6,0},{7,5},{8,10},{9,15},{10,... | collective-permute-start | bytes 1769480 | tf_op jit(solution)/shard_map/ppermute | solution.py:579
  6.5 16.7 %collective-permute-start.1 = (bf16[384,768]{1,0:T(8,128)(2,1)}, bf16[384,768]{1,0:T(8,128)(2,1)S(1)}, u32[]{:S(2)}, u32[]{:S(2)}) collective-permute-start(bf16[384,768]{1,0:T(8,128)(2,1)} %own), channel_id=1, source_target_pairs={{0,24},{1,9},{8,0},{9,17},{16,8},{17,25},{24,16},{25,1},{2,26},{3,... | collective-permute-start | bytes 1769480 | tf_op jit(solution)/shard_map/ppermute | solution.py:579
  9.3 14.6 %collective-permute-start = (bf16[384,768]{1,0:T(8,128)(2,1)}, bf16[384,768]{1,0:T(8,128)(2,1)S(1)}, u32[]{:S(2)}, u32[]{:S(2)}) collective-permute-start(bf16[384,768]{1,0:T(8,128)(2,1)} %own), channel_id=1, source_target_pairs={{0,8},{1,25},{8,16},{9,1},{16,24},{17,9},{24,0},{25,17},{2,10},{3,... | collective-permute-start | bytes 1769480 | tf_op jit(solution)/shard_map/ppermute | solution.py:579
  9.3 14.6 %collective-permute-start.3 = (bf16[384,768]{1,0:T(8,128)(2,1)}, bf16[384,768]{1,0:T(8,128)(2,1)S(1)}, u32[]{:S(2)}, u32[]{:S(2)}) collective-permute-start(bf16[384,768]{1,0:T(8,128)(2,1)} %own), channel_id=1, source_target_pairs={{0,6},{1,3},{2,0},{3,5},{4,2},{5,7},{6,4},{7,1},{8,14},{9,11},{10,... | collective-permute-start | bytes 1769480 | tf_op jit(solution)/shard_map/ppermute | solution.py:579
  14.7 9.2 %collective-permute-start.5 = (f32[72,768]{1,0:T(8,128)S(1)}, f32[72,768]{1,0:T(8,128)S(1)}, u32[]{:S(2)}, u32[]{:S(2)}) collective-permute-start(f32[72,768]{1,0:T(8,128)S(1)} %get-tuple-element.57), channel_id=1, source_target_pairs={{0,96},{32,64},{64,32},{96,0},{1,97},{33,65},{65,33},{97,1},{2,98}... | collective-permute-start | bytes 663560 | tf_op jit(solution)/shard_map/ppermute | solution.py:574
  23.9 13.0 %collective-permute-start.6 = (bf16[384,768]{1,0:T(8,128)(2,1)S(1)}, bf16[384,768]{1,0:T(8,128)(2,1)S(1)}, u32[]{:S(2)}, u32[]{:S(2)}) collective-permute-start(bf16[384,768]{1,0:T(8,128)(2,1)S(1)} %collective-permute-done.x1), channel_id=1, source_target_pairs={{0,8},{1,25},{8,16},{9,1},{16,24},{17,9},{24,0},{25,17},{2,10},{3,... | collective-permute-start | bytes 1769480 | tf_op jit(solution)/shard_map/ppermute | solution.py:579
  24.6 12.3 %collective-permute-start.7 = (bf16[384,768]{1,0:T(8,128)(2,1)S(1)}, bf16[384,768]{1,0:T(8,128)(2,1)S(1)}, u32[]{:S(2)}, u32[]{:S(2)}) collective-permute-start(bf16[384,768]{1,0:T(8,128)(2,1)S(1)} %collective-permute-done.2.y1), channel_id=1, source_target_pairs={{0,2},{1,7},{2,4},{3,1},{4,6},{5,3},{6,0},{7,5},{8,10},{9,15},{10,... | collective-permute-start | bytes 1769480 | tf_op jit(solution)/shard_map/ppermute | solution.py:579
  26.4 8.3 %collective-permute-start.10 = (bf16[64,896]{1,0:T(8,128)(2,1)S(1)}, bf16[64,896]{1,0:T(8,128)(2,1)S(1)}, u32[]{:S(2)}, u32[]{:S(2)}) collective-permute-start(bf16[64,896]{1,0:T(8,128)(2,1)S(1)} %means.1.p0), channel_id=1, source_target_pairs={{0,96},{32,64},{64,32},{96,0},{1,97},{33,65},{65,33},{97,1},{2,98}... | collective-permute-start | bytes 344072 | tf_op jit(solution)/shard_map/ppermute | solution.py:574
  29.4 7.5 %collective-permute-start.9 = (bf16[64,896]{1,0:T(8,128)(2,1)S(1)}, bf16[64,896]{1,0:T(8,128)(2,1)S(1)}, u32[]{:S(2)}, u32[]{:S(2)}) collective-permute-start(bf16[64,896]{1,0:T(8,128)(2,1)S(1)} %means.1.p0), channel_id=1, source_target_pairs={{0,64},{32,96},{64,0},{96,32},{1,65},{33,97},{65,1},{97,33},{2,66}... | collective-permute-start | bytes 344072 | tf_op jit(solution)/shard_map/ppermute | solution.py:574
  29.4 7.5 %collective-permute-start.8 = (bf16[64,896]{1,0:T(8,128)(2,1)S(1)}, bf16[64,896]{1,0:T(8,128)(2,1)S(1)}, u32[]{:S(2)}, u32[]{:S(2)}) collective-permute-start(bf16[64,896]{1,0:T(8,128)(2,1)S(1)} %means.1.p0), channel_id=1, source_target_pairs={{0,32},{32,0},{64,96},{96,64},{1,33},{33,1},{65,97},{97,65},{2,34}... | collective-permute-start | bytes 344072 | tf_op jit(solution)/shard_map/ppermute | solution.py:574
  37.0 2.3 %collective-permute-start.11 = (bf16[384,768]{1,0:T(8,128)(2,1)}, bf16[384,768]{1,0:T(8,128)(2,1)S(1)}, u32[]{:S(2)}, u32[]{:S(2)}) collective-permute-start(bf16[384,768]{1,0:T(8,128)(2,1)} %own), channel_id=1, source_target_pairs={{0,1},{1,0},{2,3},{3,2},{4,5},{5,4},{6,7},{7,6},{8,9},{9,8},{10,11... | collective-permute-start | bytes 1769480 | tf_op jit(solution)/shard_map/ppermute | solution.py:574
  37.1 3.8 %collective-permute-start.12 = (bf16[384,768]{1,0:T(8,128)(2,1)S(1)}, bf16[384,768]{1,0:T(8,128)(2,1)S(1)}, u32[]{:S(2)}, u32[]{:S(2)}) collective-permute-start(bf16[384,768]{1,0:T(8,128)(2,1)S(1)} %collective-permute-done.2.y1), channel_id=1, source_target_pairs={{0,1},{1,0},{2,3},{3,2},{4,5},{5,4},{6,7},{7,6},{8,9},{9,8},{10,11... | collective-permute-start | bytes 1769480 | tf_op jit(solution)/shard_map/ppermute | solution.py:574
  37.5 4.0 %collective-permute-start.13 = (bf16[384,768]{1,0:T(8,128)(2,1)S(1)}, bf16[384,768]{1,0:T(8,128)(2,1)S(1)}, u32[]{:S(2)}, u32[]{:S(2)}) collective-permute-start(bf16[384,768]{1,0:T(8,128)(2,1)S(1)} %collective-permute-done.7.y2), channel_id=1, source_target_pairs={{0,1},{1,0},{2,3},{3,2},{4,5},{5,4},{6,7},{7,6},{8,9},{9,8},{10,11... | collective-permute-start | bytes 1769480 | tf_op jit(solution)/shard_map/ppermute | solution.py:574
  37.6 5.2 %collective-permute-start.14 = (bf16[384,768]{1,0:T(8,128)(2,1)S(1)}, bf16[384,768]{1,0:T(8,128)(2,1)S(1)}, u32[]{:S(2)}, u32[]{:S(2)}) collective-permute-start(bf16[384,768]{1,0:T(8,128)(2,1)S(1)} %collective-permute-done.3.y3), channel_id=1, source_target_pairs={{0,1},{1,0},{2,3},{3,2},{4,5},{5,4},{6,7},{7,6},{8,9},{9,8},{10,11... | collective-permute-start | bytes 1769480 | tf_op jit(solution)/shard_map/ppermute | solution.py:574
  38.2 15.4 %collective-permute-start.18 = (bf16[256,768]{1,0:T(8,128)(2,1)S(1)}, bf16[256,768]{1,0:T(8,128)(2,1)S(1)}, u32[]{:S(2)}, u32[]{:S(2)}) collective-permute-start(bf16[256,768]{1,0:T(8,128)(2,1)S(1)} %get-tuple-element.75.own), channel_id=1, source_target_pairs={{0,6},{1,3},{2,0},{3,5},{4,2},{5,7},{6,4},{7,1},{8,14},{9,11},{10,... | collective-permute-start | bytes 1179656 | tf_op jit(solution)/shard_map/ppermute | solution.py:579
  39.3 14.4 %collective-permute-start.17 = (bf16[256,768]{1,0:T(8,128)(2,1)S(1)}, bf16[256,768]{1,0:T(8,128)(2,1)S(1)}, u32[]{:S(2)}, u32[]{:S(2)}) collective-permute-start(bf16[256,768]{1,0:T(8,128)(2,1)S(1)} %get-tuple-element.75.own), channel_id=1, source_target_pairs={{0,2},{1,7},{2,4},{3,1},{4,6},{5,3},{6,0},{7,5},{8,10},{9,15},{10,... | collective-permute-start | bytes 1179656 | tf_op jit(solution)/shard_map/ppermute | solution.py:579
  40.8 12.8 %collective-permute-start.16 = (bf16[256,768]{1,0:T(8,128)(2,1)S(1)}, bf16[256,768]{1,0:T(8,128)(2,1)S(1)}, u32[]{:S(2)}, u32[]{:S(2)}) collective-permute-start(bf16[256,768]{1,0:T(8,128)(2,1)S(1)} %get-tuple-element.75.own), channel_id=1, source_target_pairs={{0,24},{1,9},{8,0},{9,17},{16,8},{17,25},{24,16},{25,1},{2,26},{3,... | collective-permute-start | bytes 1179656 | tf_op jit(solution)/shard_map/ppermute | solution.py:579
  41.6 12.1 %collective-permute-start.15 = (bf16[256,768]{1,0:T(8,128)(2,1)S(1)}, bf16[256,768]{1,0:T(8,128)(2,1)S(1)}, u32[]{:S(2)}, u32[]{:S(2)}) collective-permute-start(bf16[256,768]{1,0:T(8,128)(2,1)S(1)} %get-tuple-element.75.own), channel_id=1, source_target_pairs={{0,8},{1,25},{8,16},{9,1},{16,24},{17,9},{24,0},{25,17},{2,10},{3,... | collective-permute-start | bytes 1179656 | tf_op jit(solution)/shard_map/ppermute | solution.py:579
  53.7 9.1 %collective-permute-start.20 = (bf16[256,768]{1,0:T(8,128)(2,1)S(1)}, bf16[256,768]{1,0:T(8,128)(2,1)S(1)}, u32[]{:S(2)}, u32[]{:S(2)}) collective-permute-start(bf16[256,768]{1,0:T(8,128)(2,1)S(1)} %collective-permute-done.17.y1), channel_id=1, source_target_pairs={{0,2},{1,7},{2,4},{3,1},{4,6},{5,3},{6,0},{7,5},{8,10},{9,15},{10,... | collective-permute-start | bytes 1179656 | tf_op jit(solution)/shard_map/ppermute | solution.py:579
  54.9 9.5 %collective-permute-start.22 = (bf16[256,768]{1,0:T(8,128)(2,1)S(1)}, bf16[256,768]{1,0:T(8,128)(2,1)S(1)}, u32[]{:S(2)}, u32[]{:S(2)}) collective-permute-start(bf16[256,768]{1,0:T(8,128)(2,1)S(1)} %collective-permute-done.17.y1), channel_id=1, source_target_pairs={{0,1},{1,0},{2,3},{3,2},{4,5},{5,4},{6,7},{7,6},{8,9},{9,8},{10,11... | collective-permute-start | bytes 1179656 | tf_op jit(solution)/shard_map/ppermute | solution.py:574
  54.9 7.9 %collective-permute-start.21 = (bf16[256,768]{1,0:T(8,128)(2,1)S(1)}, bf16[256,768]{1,0:T(8,128)(2,1)S(1)}, u32[]{:S(2)}, u32[]{:S(2)}) collective-permute-start(bf16[256,768]{1,0:T(8,128)(2,1)S(1)} %get-tuple-element.75.own), channel_id=1, source_target_pairs={{0,1},{1,0},{2,3},{3,2},{4,5},{5,4},{6,7},{7,6},{8,9},{9,8},{10,11... | collective-permute-start | bytes 1179656 | tf_op jit(solution)/shard_map/ppermute | solution.py:574
  55.4 9.0 %collective-permute-start.19 = (bf16[256,768]{1,0:T(8,128)(2,1)S(1)}, bf16[256,768]{1,0:T(8,128)(2,1)S(1)}, u32[]{:S(2)}, u32[]{:S(2)}) collective-permute-start(bf16[256,768]{1,0:T(8,128)(2,1)S(1)} %collective-permute-done.15.x1), channel_id=1, source_target_pairs={{0,8},{1,25},{8,16},{9,1},{16,24},{17,9},{24,0},{25,17},{2,10},{3,... | collective-permute-start | bytes 1179656 | tf_op jit(solution)/shard_map/ppermute | solution.py:579
  55.8 8.6 %collective-permute-start.24 = (bf16[256,768]{1,0:T(8,128)(2,1)S(1)}, bf16[256,768]{1,0:T(8,128)(2,1)S(1)}, u32[]{:S(2)}, u32[]{:S(2)}) collective-permute-start(bf16[256,768]{1,0:T(8,128)(2,1)S(1)} %collective-permute-done.18.y3), channel_id=1, source_target_pairs={{0,1},{1,0},{2,3},{3,2},{4,5},{5,4},{6,7},{7,6},{8,9},{9,8},{10,11... | collective-permute-start | bytes 1179656 | tf_op jit(solution)/shard_map/ppermute | solution.py:574
  62.7 1.7 %collective-permute-start.23 = (bf16[256,768]{1,0:T(8,128)(2,1)S(1)}, bf16[256,768]{1,0:T(8,128)(2,1)S(1)}, u32[]{:S(2)}, u32[]{:S(2)}) collective-permute-start(bf16[256,768]{1,0:T(8,128)(2,1)S(1)} %collective-permute-done.20.y2), channel_id=1, source_target_pairs={{0,1},{1,0},{2,3},{3,2},{4,5},{5,4},{6,7},{7,6},{8,9},{9,8},{10,11... | collective-permute-start | bytes 1179656 | tf_op jit(solution)/shard_map/ppermute | solution.py:574
  71.9 3.8 %collective-permute-start.27 = (f32[24,128]{1,0:T(8,128)S(1)}, f32[24,128]{1,0:T(8,128)S(1)}, u32[]{:S(2)}, u32[]{:S(2)}) collective-permute-start(f32[24,128]{1,0:T(8,128)S(1)} %get-tuple-element.81.r_0_), channel_id=1, source_target_pairs={{0,6},{1,3},{2,0},{3,5},{4,2},{5,7},{6,4},{7,1},{8,14},{9,11},{10,... | collective-permute-start | bytes 36872 | tf_op jit(solution)/shard_map/ppermute | solution.py:579
  74.0 5.2 %collective-permute-start.26 = (f32[24,128]{1,0:T(8,128)S(1)}, f32[24,128]{1,0:T(8,128)S(1)}, u32[]{:S(2)}, u32[]{:S(2)}) collective-permute-start(f32[24,128]{1,0:T(8,128)S(1)} %get-tuple-element.81.r_0_), channel_id=1, source_target_pairs={{0,4},{1,5},{2,6},{3,7},{4,0},{5,1},{6,2},{7,3},{8,12},{9,13},{10,... | collective-permute-start | bytes 36872 | tf_op jit(solution)/shard_map/ppermute | solution.py:579
  75.0 4.9 %collective-permute-start.25 = (f32[24,128]{1,0:T(8,128)S(1)}, f32[24,128]{1,0:T(8,128)S(1)}, u32[]{:S(2)}, u32[]{:S(2)}) collective-permute-start(f32[24,128]{1,0:T(8,128)S(1)} %get-tuple-element.81.r_0_), channel_id=1, source_target_pairs={{0,2},{1,7},{2,4},{3,1},{4,6},{5,3},{6,0},{7,5},{8,10},{9,15},{10,... | collective-permute-start | bytes 36872 | tf_op jit(solution)/shard_map/ppermute | solution.py:579
  79.9 1.3 collective-permute-start.28
  82.6 3.8 %collective-permute-start.31 = (f32[32,128]{1,0:T(8,128)S(1)}, f32[32,128]{1,0:T(8,128)S(1)}, u32[]{:S(2)}, u32[]{:S(2)}) collective-permute-start(f32[32,128]{1,0:T(8,128)S(1)} %get-tuple-element.88.p0), channel_id=1, source_target_pairs={{0,24},{1,9},{8,0},{9,17},{16,8},{17,25},{24,16},{25,1},{2,26},{3,... | collective-permute-start | bytes 49160 | tf_op jit(solution)/shard_map/ppermute | solution.py:579
  83.7 5.2 %collective-permute-start.30 = (f32[32,128]{1,0:T(8,128)S(1)}, f32[32,128]{1,0:T(8,128)S(1)}, u32[]{:S(2)}, u32[]{:S(2)}) collective-permute-start(f32[32,128]{1,0:T(8,128)S(1)} %get-tuple-element.88.p0), channel_id=1, source_target_pairs={{0,16},{1,17},{8,24},{9,25},{16,0},{17,1},{24,8},{25,9},{2,18},{3,... | collective-permute-start | bytes 49160 | tf_op jit(solution)/shard_map/ppermute | solution.py:579
  84.1 5.1 %collective-permute-start.29 = (f32[32,128]{1,0:T(8,128)S(1)}, f32[32,128]{1,0:T(8,128)S(1)}, u32[]{:S(2)}, u32[]{:S(2)}) collective-permute-start(f32[32,128]{1,0:T(8,128)S(1)} %get-tuple-element.88.p0), channel_id=1, source_target_pairs={{0,8},{1,25},{8,16},{9,1},{16,24},{17,9},{24,0},{25,17},{2,10},{3,... | collective-permute-start | bytes 49160 | tf_op jit(solution)/shard_map/ppermute | solution.py:579
  92.4 3.9 %collective-permute-start.34 = (f32[40,128]{1,0:T(8,128)S(1)}, f32[40,128]{1,0:T(8,128)S(1)}, u32[]{:S(2)}, u32[]{:S(2)}) collective-permute-start(f32[40,128]{1,0:T(8,128)S(1)} %get-tuple-element.93.r_0_), channel_id=1, source_target_pairs={{0,6},{1,3},{2,0},{3,5},{4,2},{5,7},{6,4},{7,1},{8,14},{9,11},{10,... | collective-permute-start | bytes 61448 | tf_op jit(solution)/shard_map/ppermute | solution.py:579
  93.8 5.3 %collective-permute-start.33 = (f32[40,128]{1,0:T(8,128)S(1)}, f32[40,128]{1,0:T(8,128)S(1)}, u32[]{:S(2)}, u32[]{:S(2)}) collective-permute-start(f32[40,128]{1,0:T(8,128)S(1)} %get-tuple-element.93.r_0_), channel_id=1, source_target_pairs={{0,4},{1,5},{2,6},{3,7},{4,0},{5,1},{6,2},{7,3},{8,12},{9,13},{10,... | collective-permute-start | bytes 61448 | tf_op jit(solution)/shard_map/ppermute | solution.py:579
  94.7 5.0 %collective-permute-start.32 = (f32[40,128]{1,0:T(8,128)S(1)}, f32[40,128]{1,0:T(8,128)S(1)}, u32[]{:S(2)}, u32[]{:S(2)}) collective-permute-start(f32[40,128]{1,0:T(8,128)S(1)} %get-tuple-element.93.r_0_), channel_id=1, source_target_pairs={{0,2},{1,7},{2,4},{3,1},{4,6},{5,3},{6,0},{7,5},{8,10},{9,15},{10,... | collective-permute-start | bytes 61448 | tf_op jit(solution)/shard_map/ppermute | solution.py:579
  99.7 1.3 collective-permute-start.35
  104.7 3.8 %collective-permute-start.38 = (f32[24,128]{1,0:T(8,128)S(1)}, f32[24,128]{1,0:T(8,128)S(1)}, u32[]{:S(2)}, u32[]{:S(2)}) collective-permute-start(f32[24,128]{1,0:T(8,128)S(1)} %step4.1.p0), channel_id=1, source_target_pairs={{0,24},{1,9},{8,0},{9,17},{16,8},{17,25},{24,16},{25,1},{2,26},{3,... | collective-permute-start | bytes 36872 | tf_op jit(solution)/shard_map/ppermute | solution.py:579
  105.9 5.2 %collective-permute-start.37 = (f32[24,128]{1,0:T(8,128)S(1)}, f32[24,128]{1,0:T(8,128)S(1)}, u32[]{:S(2)}, u32[]{:S(2)}) collective-permute-start(f32[24,128]{1,0:T(8,128)S(1)} %step4.1.p0), channel_id=1, source_target_pairs={{0,16},{1,17},{8,24},{9,25},{16,0},{17,1},{24,8},{25,9},{2,18},{3,... | collective-permute-start | bytes 36872 | tf_op jit(solution)/shard_map/ppermute | solution.py:579
  106.8 4.9 %collective-permute-start.36 = (f32[24,128]{1,0:T(8,128)S(1)}, f32[24,128]{1,0:T(8,128)S(1)}, u32[]{:S(2)}, u32[]{:S(2)}) collective-permute-start(f32[24,128]{1,0:T(8,128)S(1)} %step4.1.p0), channel_id=1, source_target_pairs={{0,8},{1,25},{8,16},{9,1},{16,24},{17,9},{24,0},{25,17},{2,10},{3,... | collective-permute-start | bytes 36872 | tf_op jit(solution)/shard_map/ppermute | solution.py:579
  114.1 3.8 %collective-permute-start.41 = (f32[24,128]{1,0:T(8,128)S(1)}, f32[24,128]{1,0:T(8,128)S(1)}, u32[]{:S(2)}, u32[]{:S(2)}) collective-permute-start(f32[24,128]{1,0:T(8,128)S(1)} %get-tuple-element.97.r_0_), channel_id=1, source_target_pairs={{0,6},{1,3},{2,0},{3,5},{4,2},{5,7},{6,4},{7,1},{8,14},{9,11},{10,... | collective-permute-start | bytes 36872 | tf_op jit(solution)/shard_map/ppermute | solution.py:579
  116.2 5.2 %collective-permute-start.40 = (f32[24,128]{1,0:T(8,128)S(1)}, f32[24,128]{1,0:T(8,128)S(1)}, u32[]{:S(2)}, u32[]{:S(2)}) collective-permute-start(f32[24,128]{1,0:T(8,128)S(1)} %get-tuple-element.97.r_0_), channel_id=1, source_target_pairs={{0,4},{1,5},{2,6},{3,7},{4,0},{5,1},{6,2},{7,3},{8,12},{9,13},{10,... | collective-permute-start | bytes 36872 | tf_op jit(solution)/shard_map/ppermute | solution.py:579
  117.1 4.9 %collective-permute-start.39 = (f32[24,128]{1,0:T(8,128)S(1)}, f32[24,128]{1,0:T(8,128)S(1)}, u32[]{:S(2)}, u32[]{:S(2)}) collective-permute-start(f32[24,128]{1,0:T(8,128)S(1)} %get-tuple-element.97.r_0_), channel_id=1, source_target_pairs={{0,2},{1,7},{2,4},{3,1},{4,6},{5,3},{6,0},{7,5},{8,10},{9,15},{10,... | collective-permute-start | bytes 36872 | tf_op jit(solution)/shard_map/ppermute | solution.py:579
  122.1 1.3 collective-permute-start.42
  126.2 3.7 %collective-permute-start.45 = (f32[16,128]{1,0:T(8,128)S(1)}, f32[16,128]{1,0:T(8,128)S(1)}, u32[]{:S(2)}, u32[]{:S(2)}) collective-permute-start(f32[16,128]{1,0:T(8,128)S(1)} %get-tuple-element.98.p0), channel_id=1, source_target_pairs={{0,24},{1,9},{8,0},{9,17},{16,8},{17,25},{24,16},{25,1},{2,26},{3,... | collective-permute-start | bytes 24584 | tf_op jit(solution)/shard_map/ppermute | solution.py:579
  126.9 5.2 %collective-permute-start.44 = (f32[16,128]{1,0:T(8,128)S(1)}, f32[16,128]{1,0:T(8,128)S(1)}, u32[]{:S(2)}, u32[]{:S(2)}) collective-permute-start(f32[16,128]{1,0:T(8,128)S(1)} %get-tuple-element.98.p0), channel_id=1, source_target_pairs={{0,16},{1,17},{8,24},{9,25},{16,0},{17,1},{24,8},{25,9},{2,18},{3,... | collective-permute-start | bytes 24584 | tf_op jit(solution)/shard_map/ppermute | solution.py:579
  127.8 4.9 %collective-permute-start.43 = (f32[16,128]{1,0:T(8,128)S(1)}, f32[16,128]{1,0:T(8,128)S(1)}, u32[]{:S(2)}, u32[]{:S(2)}) collective-permute-start(f32[16,128]{1,0:T(8,128)S(1)} %get-tuple-element.98.p0), channel_id=1, source_target_pairs={{0,8},{1,25},{8,16},{9,1},{16,24},{17,9},{24,0},{25,17},{2,10},{3,... | collective-permute-start | bytes 24584 | tf_op jit(solution)/shard_map/ppermute | solution.py:579

commit v3 on v2

--- a/solution.py
+++ b/solution.py
@@ -452,7 +452,7 @@
         payload[pl.ds(r, 1), :] = jnp.sum(acc, axis=0, keepdims=True)
         return 0
 
-    lax.fori_loop(0, rows // 128, body, 0, unroll=4)
+    lax.fori_loop(0, rows // 128, body, 0, unroll=8)
     total = payload[0:rows // 128, :]
     peak[...] = jnp.broadcast_to(most_of(total), peak.shape)
     store_lse(

time: 133 us -> 133 us (level)
  no operation moved by 1% of the time
where the time goes in v3:
time: 133 us
  waiting for transfers between devices  50.6 us (38%)
  starting transfers between devices  46.2 us (35%)
  Pallas kernels  34.1 us (26%)
    ppermute x30, waiting for transfers between devices, turn(): lax.ppermute(v, (axis, 'c'), [(i * 2 + c, (i + (k if c == 0 else n - k))...  36.9 us
    ppermute x30, starting transfers between devices, turn(): lax.ppermute(v, (axis, 'c'), [(i * 2 + c, (i + (k if c == 0 else n - k))...  33.1 us
    ppermute x16, waiting for transfers between devices, swap(): return lax.ppermute(v, axis, [(i, i ^ bit) for i in range(n)])  13.7 us
    ppermute x16, starting transfers between devices, swap(): return lax.ppermute(v, axis, [(i, i ^ bit) for i in range(n)])  13.2 us
    pallas_call x1, Pallas kernels, local(): tile_call(fine_tile_kernel, n_rows, n_cols, n_cols // 128, [SMEM, VMEM] +...  10.8 us
    pallas_call x1, Pallas kernels, local(): tile_call(coarse_tile_kernel, k_rows, k_cols, 24, [ANY] * 11 + [VMEM], [p...  7.23 us
    pallas_call x1, Pallas kernels, local(): call(step4_kernel, sds((24, 128)), [VMEM, VMEM] + [VMEM] * 3 + kspecs * 2...  3.64 us
    pallas_call x1, Pallas kernels, local(): call(step3_kernel, [sds((40, 128)), sds((8, 128)), sds((12, 128))], [VMEM...  3.21 us
  transfers between devices with their start and end apart: 46, of which 29 were waited for; matrix products, arithmetic and copies ran while one was open for 0% of the time, Pallas kernels for 8%

profile of v3, /device:TPU:0, one launch (start us, length us, event | category | flops | bytes accessed | tf_op | source)
XLA Modules:
  0.0 133.1 jit_solution(13332552478331098797)
XLA Ops:
  1.4 1.5 %pool.1 = (f32[136,768]{1,0:T(8,128)S(1)}, f32[136,768]{1,0:T(8,128)S(1)}, f32[24,128]{1,0:T(8,128)S(1)}, f32[12,128]{1,0:T(8,128)S(1)}, f32[3,128]{1,0:T(4,128)S(1)}, /*index=5*/f32[8,128]{1,0:T(8,128)S(1)}) custom-call(s32[8,128]{1,0:T(8,128)S(1)} %fusion.info.table, bf16[384,768]{1,0:T(8,128)(2,1)} %own, s32[8,128]{1,0:T(8,128)S(1)} %fusion.info.table), custom_call_target="tpu_custom_call" | custom-call | tf_op jit(solution)/shard_map/pool/pallas_call | solution.py:617
  2.9 2.1 %collective-permute-start.4 = (f32[136,768]{1,0:T(8,128)S(1)}, f32[136,768]{1,0:T(8,128)S(1)}, u32[]{:S(2)}, u32[]{:S(2)}) collective-permute-start(f32[136,768]{1,0:T(8,128)S(1)} %get-tuple-element.56), channel_id=1, source_target_pairs={{0,32},{32,0},{64,96},{96,64},{1,33},{33,1},{65,97},{97,65},{2,34}... | collective-permute-start | bytes 1253384 | tf_op jit(solution)/shard_map/ppermute | solution.py:574
  5.0 1.6 %collective-permute-start.2 = (bf16[384,768]{1,0:T(8,128)(2,1)}, bf16[384,768]{1,0:T(8,128)(2,1)S(1)}, u32[]{:S(2)}, u32[]{:S(2)}) collective-permute-start(bf16[384,768]{1,0:T(8,128)(2,1)} %own), channel_id=1, source_target_pairs={{0,2},{1,7},{2,4},{3,1},{4,6},{5,3},{6,0},{7,5},{8,10},{9,15},{10,... | collective-permute-start | bytes 1769480 | tf_op jit(solution)/shard_map/ppermute | solution.py:579
  6.5 2.8 %collective-permute-start.1 = (bf16[384,768]{1,0:T(8,128)(2,1)}, bf16[384,768]{1,0:T(8,128)(2,1)S(1)}, u32[]{:S(2)}, u32[]{:S(2)}) collective-permute-start(bf16[384,768]{1,0:T(8,128)(2,1)} %own), channel_id=1, source_target_pairs={{0,24},{1,9},{8,0},{9,17},{16,8},{17,25},{24,16},{25,1},{2,26},{3,... | collective-permute-start | bytes 1769480 | tf_op jit(solution)/shard_map/ppermute | solution.py:579
  9.3 1.7 %collective-permute-start.3 = (bf16[384,768]{1,0:T(8,128)(2,1)}, bf16[384,768]{1,0:T(8,128)(2,1)S(1)}, u32[]{:S(2)}, u32[]{:S(2)}) collective-permute-start(bf16[384,768]{1,0:T(8,128)(2,1)} %own), channel_id=1, source_target_pairs={{0,6},{1,3},{2,0},{3,5},{4,2},{5,7},{6,4},{7,1},{8,14},{9,11},{10,... | collective-permute-start | bytes 1769480 | tf_op jit(solution)/shard_map/ppermute | solution.py:579
  11.0 3.6 %collective-permute-done.4.got = f32[136,768]{1,0:T(8,128)S(1)} collective-permute-done((f32[136,768]{1,0:T(8,128)S(1)}, f32[136,768]{1,0:T(8,128)S(1)}, u32[]{:S(2)}, u32[]{:S(2)}) %collective-permute-start.4) | collective-permute-done | bytes 417824 | tf_op jit(solution)/shard_map/ppermute | solution.py:574
  14.7 3.9 %collective-permute-start.5 = (f32[72,768]{1,0:T(8,128)S(1)}, f32[72,768]{1,0:T(8,128)S(1)}, u32[]{:S(2)}, u32[]{:S(2)}) collective-permute-start(f32[72,768]{1,0:T(8,128)S(1)} %get-tuple-element.57), channel_id=1, source_target_pairs={{0,96},{32,64},{64,32},{96,0},{1,97},{33,65},{65,33},{97,1},{2,98}... | collective-permute-start | bytes 663560 | tf_op jit(solution)/shard_map/ppermute | solution.py:574
  18.6 4.7 %collective-permute-done.1.x3 = bf16[384,768]{1,0:T(8,128)(2,1)S(1)} collective-permute-done((bf16[384,768]{1,0:T(8,128)(2,1)}, bf16[384,768]{1,0:T(8,128)(2,1)S(1)}, u32[]{:S(2)}, u32[]{:S(2)}) %collective-permute-start.1) | collective-permute-done | bytes 589856 | tf_op jit(solution)/shard_map/ppermute | solution.py:579
  24.6 1.6 %collective-permute-start.7 = (bf16[384,768]{1,0:T(8,128)(2,1)S(1)}, bf16[384,768]{1,0:T(8,128)(2,1)S(1)}, u32[]{:S(2)}, u32[]{:S(2)}) collective-permute-start(bf16[384,768]{1,0:T(8,128)(2,1)S(1)} %collective-permute-done.2.y1), channel_id=1, source_target_pairs={{0,2},{1,7},{2,4},{3,1},{4,6},{5,3},{6,0},{7,5},{8,10},{9,15},{10,... | collective-permute-start | bytes 1769480 | tf_op jit(solution)/shard_map/ppermute | solution.py:579
  26.4 3.0 %collective-permute-start.10 = (bf16[64,896]{1,0:T(8,128)(2,1)S(1)}, bf16[64,896]{1,0:T(8,128)(2,1)S(1)}, u32[]{:S(2)}, u32[]{:S(2)}) collective-permute-start(bf16[64,896]{1,0:T(8,128)(2,1)S(1)} %means.1.p0), channel_id=1, source_target_pairs={{0,96},{32,64},{64,32},{96,0},{1,97},{33,65},{65,33},{97,1},{2,98}... | collective-permute-start | bytes 344072 | tf_op jit(solution)/shard_map/ppermute | solution.py:574
  29.4 1.1 collective-permute-start.8
  30.6 4.1 %collective-permute-done.10.p3 = bf16[64,896]{1,0:T(8,128)(2,1)S(1)} collective-permute-done((bf16[64,896]{1,0:T(8,128)(2,1)S(1)}, bf16[64,896]{1,0:T(8,128)(2,1)S(1)}, u32[]{:S(2)}, u32[]{:S(2)}) %collective-permute-start.10) | collective-permute-done | bytes 114720 | tf_op jit(solution)/shard_map/ppermute | solution.py:574
  34.7 2.3 %collective-permute-done.9.p2 = bf16[64,896]{1,0:T(8,128)(2,1)S(1)} collective-permute-done((bf16[64,896]{1,0:T(8,128)(2,1)S(1)}, bf16[64,896]{1,0:T(8,128)(2,1)S(1)}, u32[]{:S(2)}, u32[]{:S(2)}) %collective-permute-start.9) | collective-permute-done | bytes 114720 | tf_op jit(solution)/shard_map/ppermute | solution.py:574
  38.2 1.0 collective-permute-start.18
  39.3 1.6 %collective-permute-start.17 = (bf16[256,768]{1,0:T(8,128)(2,1)S(1)}, bf16[256,768]{1,0:T(8,128)(2,1)S(1)}, u32[]{:S(2)}, u32[]{:S(2)}) collective-permute-start(bf16[256,768]{1,0:T(8,128)(2,1)S(1)} %get-tuple-element.75.own), channel_id=1, source_target_pairs={{0,2},{1,7},{2,4},{3,1},{4,6},{5,3},{6,0},{7,5},{8,10},{9,15},{10,... | collective-permute-start | bytes 1179656 | tf_op jit(solution)/shard_map/ppermute | solution.py:579
  41.6 1.3 collective-permute-start.15
  42.9 10.8 %fine_tile.1 = (f32[3072,1536]{1,0:T(8,128)S(1)}, f32[12,128]{1,0:T(8,128)S(1)}, f32[8,128]{1,0:T(8,128)S(1)}, bf16[3072,768]{1,0:T(8,128)(2,1)}, bf16[1536,768]{1,0:T(8,128)(2,1)}) custom-call(s32[8,128]{1,0:T(8,128)S(1)} %fusion.info.table, f32[24,128]{1,0:T(8,128)S(1)} %get-tuple-element.54.live_rows, bf16[384,768]{1,0:T(8,128)(2,1)} %own, ...), custom_call_target="tpu_custom_call" | custom-call | flops 7247757312 | tf_op jit(solution)/shard_map/fine_tile/pallas_call | solution.py:667
  53.7 1.2 collective-permute-start.20
  55.8 1.2 collective-permute-start.24
  57.0 5.7 %collective-permute-done.20.y2 = bf16[256,768]{1,0:T(8,128)(2,1)S(1)} collective-permute-done((bf16[256,768]{1,0:T(8,128)(2,1)S(1)}, bf16[256,768]{1,0:T(8,128)(2,1)S(1)}, u32[]{:S(2)}, u32[]{:S(2)}) %collective-permute-start.20) | collective-permute-done | bytes 393248 | tf_op jit(solution)/shard_map/ppermute | solution.py:579
  62.8 1.6 %collective-permute-done.19.x2 = bf16[256,768]{1,0:T(8,128)(2,1)S(1)} collective-permute-done((bf16[256,768]{1,0:T(8,128)(2,1)S(1)}, bf16[256,768]{1,0:T(8,128)(2,1)S(1)}, u32[]{:S(2)}, u32[]{:S(2)}) %collective-permute-start.19) | collective-permute-done | bytes 393248 | tf_op jit(solution)/shard_map/ppermute | solution.py:579
  64.5 7.2 %coarse_tile.1 = (f32[2048,1024]{1,0:T(8,128)S(1)}, f32[24,128]{1,0:T(8,128)S(1)}, f32[8,128]{1,0:T(8,128)S(1)}, bf16[2048,768]{1,0:T(8,128)(2,1)}, bf16[1024,768]{1,0:T(8,128)(2,1)}) custom-call(bf16[256,768]{1,0:T(8,128)(2,1)S(1)} %get-tuple-element.75.own, bf16[256,768]{1,0:T(8,128)(2,1)S(1)} %collective-permute-done.15.x1, ...), custom_call_target="tpu_custom_call" | custom-call | flops 3221225472 | tf_op jit(solution)/shard_map/coarse_tile/pallas_call | solution.py:675
  71.7 2.1 %collective-permute-start.27 = (f32[24,128]{1,0:T(8,128)S(1)}, f32[24,128]{1,0:T(8,128)S(1)}, u32[]{:S(2)}, u32[]{:S(2)}) collective-permute-start(f32[24,128]{1,0:T(8,128)S(1)} %get-tuple-element.81.r_0_), channel_id=1, source_target_pairs={{0,6},{1,3},{2,0},{3,5},{4,2},{5,7},{6,4},{7,1},{8,14},{9,11},{10,... | collective-permute-start | bytes 36872 | tf_op jit(solution)/shard_map/ppermute | solution.py:579
  73.8 1.0 collective-permute-start.26
  75.5 3.6 %collective-permute-done.26.r_2_ = f32[24,128]{1,0:T(8,128)S(1)} collective-permute-done((f32[24,128]{1,0:T(8,128)S(1)}, f32[24,128]{1,0:T(8,128)S(1)}, u32[]{:S(2)}, u32[]{:S(2)}) %collective-permute-start.26) | collective-permute-done | bytes 12320 | tf_op jit(solution)/shard_map/ppermute | solution.py:579
  79.9 1.2 collective-permute-done.28.other
  81.0 1.4 %coarse2.1 = (f32[32,128]{1,0:T(8,128)S(1)}, f32[16,128]{1,0:T(8,128)S(1)}) custom-call(f32[24,128]{1,0:T(8,128)S(1)} %fold_y1.1.mine, f32[24,128]{1,0:T(8,128)S(1)} %collective-permute-done.28.other, f32[12,128]{1,0:T(8,128)S(1)} %get-tuple-element.82.part, f32[8,128]{1,0:T(8,128)S(1)} %get-tuple-element.80.plog, f32[3,128]{1,0:T(4,128)S(1)} %get-tuple-element.83.seat, ...), custom_call_target="tpu_custom_call" | custom-call | tf_op jit(solution)/shard_map/coarse2/pallas_call | solution.py:689
  82.4 1.1 collective-permute-start.31
  83.9 1.1 collective-permute-start.29
  85.0 1.2 collective-permute-done.31.p3
  86.2 2.6 %collective-permute-done.30.p2 = f32[32,128]{1,0:T(8,128)S(1)} collective-permute-done((f32[32,128]{1,0:T(8,128)S(1)}, f32[32,128]{1,0:T(8,128)S(1)}, u32[]{:S(2)}, u32[]{:S(2)}) %collective-permute-start.30) | collective-permute-done | bytes 16416 | tf_op jit(solution)/shard_map/ppermute | solution.py:579
  89.0 3.2 %step3.1 = (f32[40,128]{1,0:T(8,128)S(1)}, f32[8,128]{1,0:T(8,128)S(1)}, f32[12,128]{1,0:T(8,128)S(1)}) custom-call(f32[8,128]{1,0:T(8,128)S(1)} %get-tuple-element.52.logs, f32[24,128]{1,0:T(8,128)S(1)} %get-tuple-element.54.live_rows, f32[12,128]{1,0:T(8,128)S(1)} %get-tuple-element.53.live_cols, f32[32,128]{1,0:T(8,128)S(1)} %get-tuple-element.88.p0, ...), custom_call_target="tpu_custom_call" | custom-call | tf_op jit(solution)/shard_map/step3/pallas_call | solution.py:697
  92.2 1.4 %collective-permute-start.34 = (f32[40,128]{1,0:T(8,128)S(1)}, f32[40,128]{1,0:T(8,128)S(1)}, u32[]{:S(2)}, u32[]{:S(2)}) collective-permute-start(f32[40,128]{1,0:T(8,128)S(1)} %get-tuple-element.93.r_0_), channel_id=1, source_target_pairs={{0,6},{1,3},{2,0},{3,5},{4,2},{5,7},{6,4},{7,1},{8,14},{9,11},{10,... | collective-permute-start | bytes 61448 | tf_op jit(solution)/shard_map/ppermute | solution.py:579
  94.5 0.9 collective-permute-start.32
  96.1 2.8 %collective-permute-done.33.r_2_ = f32[40,128]{1,0:T(8,128)S(1)} collective-permute-done((f32[40,128]{1,0:T(8,128)S(1)}, f32[40,128]{1,0:T(8,128)S(1)}, u32[]{:S(2)}, u32[]{:S(2)}) %collective-permute-start.33) | collective-permute-done | bytes 20512 | tf_op jit(solution)/shard_map/ppermute | solution.py:579
  99.7 1.2 collective-permute-done.35.other
  100.8 3.6 %step4.1.p0 = f32[24,128]{1,0:T(8,128)S(1)} custom-call(f32[8,128]{1,0:T(8,128)S(1)} %get-tuple-element.52.logs, f32[24,128]{1,0:T(8,128)S(1)} %get-tuple-element.54.live_rows, f32[40,128]{1,0:T(8,128)S(1)} %fold_y2.1.mine, f32[40,128]{1,0:T(8,128)S(1)} %collective-permute-done.35.other, f32[16,128]{1,0:T(8,128)S(1)} %get-tuple-element.94.plog_rows, ...), custom_call_target="tpu_custom_call" | custom-call | tf_op jit(solution)/shard_map/step4/pallas_call | solution.py:712
  104.5 1.3 collective-permute-start.38
  105.7 0.9 collective-permute-start.37
  106.7 1.2 collective-permute-start.36
  108.2 2.7 %collective-permute-done.37.p2 = f32[24,128]{1,0:T(8,128)S(1)} collective-permute-done((f32[24,128]{1,0:T(8,128)S(1)}, f32[24,128]{1,0:T(8,128)S(1)}, u32[]{:S(2)}, u32[]{:S(2)}) %collective-permute-start.37) | collective-permute-done | bytes 12320 | tf_op jit(solution)/shard_map/ppermute | solution.py:579
  111.6 2.4 %step5.1 = (f32[24,128]{1,0:T(8,128)S(1)}, f32[1,128]{1,0:T(1,128)S(1)}) custom-call(f32[8,128]{1,0:T(8,128)S(1)} %get-tuple-element.52.logs, f32[24,128]{1,0:T(8,128)S(1)} %get-tuple-element.54.live_rows, f32[12,128]{1,0:T(8,128)S(1)} %get-tuple-element.53.live_cols, f32[24,128]{1,0:T(8,128)S(1)} %step4.1.p0, f32[24,128]{1,0:T(8,128)S(1)} %collective-permute-done.36.p1, ...), custom_call_target="tpu_custom_call" | custom-call | tf_op jit(solution)/shard_map/step5/pallas_call | solution.py:720
  114.0 2.1 %collective-permute-start.41 = (f32[24,128]{1,0:T(8,128)S(1)}, f32[24,128]{1,0:T(8,128)S(1)}, u32[]{:S(2)}, u32[]{:S(2)}) collective-permute-start(f32[24,128]{1,0:T(8,128)S(1)} %get-tuple-element.97.r_0_), channel_id=1, source_target_pairs={{0,6},{1,3},{2,0},{3,5},{4,2},{5,7},{6,4},{7,1},{8,14},{9,11},{10,... | collective-permute-start | bytes 36872 | tf_op jit(solution)/shard_map/ppermute | solution.py:579
  117.7 3.5 %collective-permute-done.40.r_2_ = f32[24,128]{1,0:T(8,128)S(1)} collective-permute-done((f32[24,128]{1,0:T(8,128)S(1)}, f32[24,128]{1,0:T(8,128)S(1)}, u32[]{:S(2)}, u32[]{:S(2)}) %collective-permute-start.40) | collective-permute-done | bytes 12320 | tf_op jit(solution)/shard_map/ppermute | solution.py:579
  122.0 1.2 collective-permute-done.42.other
  123.2 2.8 %step6.1 = (f32[16,128]{1,0:T(8,128)S(1)}, f32[3,128]{1,0:T(4,128)}) custom-call(f32[8,128]{1,0:T(8,128)S(1)} %get-tuple-element.52.logs, f32[24,128]{1,0:T(8,128)S(1)} %get-tuple-element.54.live_rows, f32[24,128]{1,0:T(8,128)S(1)} %fold_y3.1.mine, f32[24,128]{1,0:T(8,128)S(1)} %collective-permute-done.42.other, f32[3072,1536]{1,0:T(8,128)S(1)} %get-tuple-element.89.tile, ...), custom_call_target="tpu_custom_call" | custom-call | tf_op jit(solution)/shard_map/step6/pallas_call | solution.py:735
  127.6 1.3 collective-permute-start.43
  129.7 2.1 %collective-permute-done.44.p2 = f32[16,128]{1,0:T(8,128)S(1)} collective-permute-done((f32[16,128]{1,0:T(8,128)S(1)}, f32[16,128]{1,0:T(8,128)S(1)}, u32[]{:S(2)}, u32[]{:S(2)}) %collective-permute-start.44) | collective-permute-done | bytes 8224 | tf_op jit(solution)/shard_map/ppermute | solution.py:579
  (62 shorter events, 16.9 us)
Async XLA Ops:
  2.9 11.7 %collective-permute-start.4 = (f32[136,768]{1,0:T(8,128)S(1)}, f32[136,768]{1,0:T(8,128)S(1)}, u32[]{:S(2)}, u32[]{:S(2)}) collective-permute-start(f32[136,768]{1,0:T(8,128)S(1)} %get-tuple-element.56), channel_id=1, source_target_pairs={{0,32},{32,0},{64,96},{96,64},{1,33},{33,1},{65,97},{97,65},{2,34}... | collective-permute-start | bytes 1253384 | tf_op jit(solution)/shard_map/ppermute | solution.py:574
  5.0 13.6 %collective-permute-start.2 = (bf16[384,768]{1,0:T(8,128)(2,1)}, bf16[384,768]{1,0:T(8,128)(2,1)S(1)}, u32[]{:S(2)}, u32[]{:S(2)}) collective-permute-start(bf16[384,768]{1,0:T(8,128)(2,1)} %own), channel_id=1, source_target_pairs={{0,2},{1,7},{2,4},{3,1},{4,6},{5,3},{6,0},{7,5},{8,10},{9,15},{10,... | collective-permute-start | bytes 1769480 | tf_op jit(solution)/shard_map/ppermute | solution.py:579
  6.5 16.7 %collective-permute-start.1 = (bf16[384,768]{1,0:T(8,128)(2,1)}, bf16[384,768]{1,0:T(8,128)(2,1)S(1)}, u32[]{:S(2)}, u32[]{:S(2)}) collective-permute-start(bf16[384,768]{1,0:T(8,128)(2,1)} %own), channel_id=1, source_target_pairs={{0,24},{1,9},{8,0},{9,17},{16,8},{17,25},{24,16},{25,1},{2,26},{3,... | collective-permute-start | bytes 1769480 | tf_op jit(solution)/shard_map/ppermute | solution.py:579
  9.3 14.6 %collective-permute-start = (bf16[384,768]{1,0:T(8,128)(2,1)}, bf16[384,768]{1,0:T(8,128)(2,1)S(1)}, u32[]{:S(2)}, u32[]{:S(2)}) collective-permute-start(bf16[384,768]{1,0:T(8,128)(2,1)} %own), channel_id=1, source_target_pairs={{0,8},{1,25},{8,16},{9,1},{16,24},{17,9},{24,0},{25,17},{2,10},{3,... | collective-permute-start | bytes 1769480 | tf_op jit(solution)/shard_map/ppermute | solution.py:579
  9.3 14.6 %collective-permute-start.3 = (bf16[384,768]{1,0:T(8,128)(2,1)}, bf16[384,768]{1,0:T(8,128)(2,1)S(1)}, u32[]{:S(2)}, u32[]{:S(2)}) collective-permute-start(bf16[384,768]{1,0:T(8,128)(2,1)} %own), channel_id=1, source_target_pairs={{0,6},{1,3},{2,0},{3,5},{4,2},{5,7},{6,4},{7,1},{8,14},{9,11},{10,... | collective-permute-start | bytes 1769480 | tf_op jit(solution)/shard_map/ppermute | solution.py:579
  14.7 9.2 %collective-permute-start.5 = (f32[72,768]{1,0:T(8,128)S(1)}, f32[72,768]{1,0:T(8,128)S(1)}, u32[]{:S(2)}, u32[]{:S(2)}) collective-permute-start(f32[72,768]{1,0:T(8,128)S(1)} %get-tuple-element.57), channel_id=1, source_target_pairs={{0,96},{32,64},{64,32},{96,0},{1,97},{33,65},{65,33},{97,1},{2,98}... | collective-permute-start | bytes 663560 | tf_op jit(solution)/shard_map/ppermute | solution.py:574
  23.9 13.0 %collective-permute-start.6 = (bf16[384,768]{1,0:T(8,128)(2,1)S(1)}, bf16[384,768]{1,0:T(8,128)(2,1)S(1)}, u32[]{:S(2)}, u32[]{:S(2)}) collective-permute-start(bf16[384,768]{1,0:T(8,128)(2,1)S(1)} %collective-permute-done.x1), channel_id=1, source_target_pairs={{0,8},{1,25},{8,16},{9,1},{16,24},{17,9},{24,0},{25,17},{2,10},{3,... | collective-permute-start | bytes 1769480 | tf_op jit(solution)/shard_map/ppermute | solution.py:579
  24.6 12.3 %collective-permute-start.7 = (bf16[384,768]{1,0:T(8,128)(2,1)S(1)}, bf16[384,768]{1,0:T(8,128)(2,1)S(1)}, u32[]{:S(2)}, u32[]{:S(2)}) collective-permute-start(bf16[384,768]{1,0:T(8,128)(2,1)S(1)} %collective-permute-done.2.y1), channel_id=1, source_target_pairs={{0,2},{1,7},{2,4},{3,1},{4,6},{5,3},{6,0},{7,5},{8,10},{9,15},{10,... | collective-permute-start | bytes 1769480 | tf_op jit(solution)/shard_map/ppermute | solution.py:579
  26.4 8.3 %collective-permute-start.10 = (bf16[64,896]{1,0:T(8,128)(2,1)S(1)}, bf16[64,896]{1,0:T(8,128)(2,1)S(1)}, u32[]{:S(2)}, u32[]{:S(2)}) collective-permute-start(bf16[64,896]{1,0:T(8,128)(2,1)S(1)} %means.1.p0), channel_id=1, source_target_pairs={{0,96},{32,64},{64,32},{96,0},{1,97},{33,65},{65,33},{97,1},{2,98}... | collective-permute-start | bytes 344072 | tf_op jit(solution)/shard_map/ppermute | solution.py:574
  29.4 7.5 %collective-permute-start.9 = (bf16[64,896]{1,0:T(8,128)(2,1)S(1)}, bf16[64,896]{1,0:T(8,128)(2,1)S(1)}, u32[]{:S(2)}, u32[]{:S(2)}) collective-permute-start(bf16[64,896]{1,0:T(8,128)(2,1)S(1)} %means.1.p0), channel_id=1, source_target_pairs={{0,64},{32,96},{64,0},{96,32},{1,65},{33,97},{65,1},{97,33},{2,66}... | collective-permute-start | bytes 344072 | tf_op jit(solution)/shard_map/ppermute | solution.py:574
  29.4 7.5 %collective-permute-start.8 = (bf16[64,896]{1,0:T(8,128)(2,1)S(1)}, bf16[64,896]{1,0:T(8,128)(2,1)S(1)}, u32[]{:S(2)}, u32[]{:S(2)}) collective-permute-start(bf16[64,896]{1,0:T(8,128)(2,1)S(1)} %means.1.p0), channel_id=1, source_target_pairs={{0,32},{32,0},{64,96},{96,64},{1,33},{33,1},{65,97},{97,65},{2,34}... | collective-permute-start | bytes 344072 | tf_op jit(solution)/shard_map/ppermute | solution.py:574
  37.0 2.3 %collective-permute-start.11 = (bf16[384,768]{1,0:T(8,128)(2,1)}, bf16[384,768]{1,0:T(8,128)(2,1)S(1)}, u32[]{:S(2)}, u32[]{:S(2)}) collective-permute-start(bf16[384,768]{1,0:T(8,128)(2,1)} %own), channel_id=1, source_target_pairs={{0,1},{1,0},{2,3},{3,2},{4,5},{5,4},{6,7},{7,6},{8,9},{9,8},{10,11... | collective-permute-start | bytes 1769480 | tf_op jit(solution)/shard_map/ppermute | solution.py:574
  37.1 3.8 %collective-permute-start.12 = (bf16[384,768]{1,0:T(8,128)(2,1)S(1)}, bf16[384,768]{1,0:T(8,128)(2,1)S(1)}, u32[]{:S(2)}, u32[]{:S(2)}) collective-permute-start(bf16[384,768]{1,0:T(8,128)(2,1)S(1)} %collective-permute-done.2.y1), channel_id=1, source_target_pairs={{0,1},{1,0},{2,3},{3,2},{4,5},{5,4},{6,7},{7,6},{8,9},{9,8},{10,11... | collective-permute-start | bytes 1769480 | tf_op jit(solution)/shard_map/ppermute | solution.py:574
  37.5 4.0 %collective-permute-start.13 = (bf16[384,768]{1,0:T(8,128)(2,1)S(1)}, bf16[384,768]{1,0:T(8,128)(2,1)S(1)}, u32[]{:S(2)}, u32[]{:S(2)}) collective-permute-start(bf16[384,768]{1,0:T(8,128)(2,1)S(1)} %collective-permute-done.7.y2), channel_id=1, source_target_pairs={{0,1},{1,0},{2,3},{3,2},{4,5},{5,4},{6,7},{7,6},{8,9},{9,8},{10,11... | collective-permute-start | bytes 1769480 | tf_op jit(solution)/shard_map/ppermute | solution.py:574
  37.6 5.2 %collective-permute-start.14 = (bf16[384,768]{1,0:T(8,128)(2,1)S(1)}, bf16[384,768]{1,0:T(8,128)(2,1)S(1)}, u32[]{:S(2)}, u32[]{:S(2)}) collective-permute-start(bf16[384,768]{1,0:T(8,128)(2,1)S(1)} %collective-permute-done.3.y3), channel_id=1, source_target_pairs={{0,1},{1,0},{2,3},{3,2},{4,5},{5,4},{6,7},{7,6},{8,9},{9,8},{10,11... | collective-permute-start | bytes 1769480 | tf_op jit(solution)/shard_map/ppermute | solution.py:574
  38.2 15.4 %collective-permute-start.18 = (bf16[256,768]{1,0:T(8,128)(2,1)S(1)}, bf16[256,768]{1,0:T(8,128)(2,1)S(1)}, u32[]{:S(2)}, u32[]{:S(2)}) collective-permute-start(bf16[256,768]{1,0:T(8,128)(2,1)S(1)} %get-tuple-element.75.own), channel_id=1, source_target_pairs={{0,6},{1,3},{2,0},{3,5},{4,2},{5,7},{6,4},{7,1},{8,14},{9,11},{10,... | collective-permute-start | bytes 1179656 | tf_op jit(solution)/shard_map/ppermute | solution.py:579
  39.3 14.4 %collective-permute-start.17 = (bf16[256,768]{1,0:T(8,128)(2,1)S(1)}, bf16[256,768]{1,0:T(8,128)(2,1)S(1)}, u32[]{:S(2)}, u32[]{:S(2)}) collective-permute-start(bf16[256,768]{1,0:T(8,128)(2,1)S(1)} %get-tuple-element.75.own), channel_id=1, source_target_pairs={{0,2},{1,7},{2,4},{3,1},{4,6},{5,3},{6,0},{7,5},{8,10},{9,15},{10,... | collective-permute-start | bytes 1179656 | tf_op jit(solution)/shard_map/ppermute | solution.py:579
  40.8 12.8 %collective-permute-start.16 = (bf16[256,768]{1,0:T(8,128)(2,1)S(1)}, bf16[256,768]{1,0:T(8,128)(2,1)S(1)}, u32[]{:S(2)}, u32[]{:S(2)}) collective-permute-start(bf16[256,768]{1,0:T(8,128)(2,1)S(1)} %get-tuple-element.75.own), channel_id=1, source_target_pairs={{0,24},{1,9},{8,0},{9,17},{16,8},{17,25},{24,16},{25,1},{2,26},{3,... | collective-permute-start | bytes 1179656 | tf_op jit(solution)/shard_map/ppermute | solution.py:579
  41.6 12.1 %collective-permute-start.15 = (bf16[256,768]{1,0:T(8,128)(2,1)S(1)}, bf16[256,768]{1,0:T(8,128)(2,1)S(1)}, u32[]{:S(2)}, u32[]{:S(2)}) collective-permute-start(bf16[256,768]{1,0:T(8,128)(2,1)S(1)} %get-tuple-element.75.own), channel_id=1, source_target_pairs={{0,8},{1,25},{8,16},{9,1},{16,24},{17,9},{24,0},{25,17},{2,10},{3,... | collective-permute-start | bytes 1179656 | tf_op jit(solution)/shard_map/ppermute | solution.py:579
  53.7 9.1 %collective-permute-start.20 = (bf16[256,768]{1,0:T(8,128)(2,1)S(1)}, bf16[256,768]{1,0:T(8,128)(2,1)S(1)}, u32[]{:S(2)}, u32[]{:S(2)}) collective-permute-start(bf16[256,768]{1,0:T(8,128)(2,1)S(1)} %collective-permute-done.17.y1), channel_id=1, source_target_pairs={{0,2},{1,7},{2,4},{3,1},{4,6},{5,3},{6,0},{7,5},{8,10},{9,15},{10,... | collective-permute-start | bytes 1179656 | tf_op jit(solution)/shard_map/ppermute | solution.py:579
  54.9 9.5 %collective-permute-start.22 = (bf16[256,768]{1,0:T(8,128)(2,1)S(1)}, bf16[256,768]{1,0:T(8,128)(2,1)S(1)}, u32[]{:S(2)}, u32[]{:S(2)}) collective-permute-start(bf16[256,768]{1,0:T(8,128)(2,1)S(1)} %collective-permute-done.17.y1), channel_id=1, source_target_pairs={{0,1},{1,0},{2,3},{3,2},{4,5},{5,4},{6,7},{7,6},{8,9},{9,8},{10,11... | collective-permute-start | bytes 1179656 | tf_op jit(solution)/shard_map/ppermute | solution.py:574
  54.9 7.9 %collective-permute-start.21 = (bf16[256,768]{1,0:T(8,128)(2,1)S(1)}, bf16[256,768]{1,0:T(8,128)(2,1)S(1)}, u32[]{:S(2)}, u32[]{:S(2)}) collective-permute-start(bf16[256,768]{1,0:T(8,128)(2,1)S(1)} %get-tuple-element.75.own), channel_id=1, source_target_pairs={{0,1},{1,0},{2,3},{3,2},{4,5},{5,4},{6,7},{7,6},{8,9},{9,8},{10,11... | collective-permute-start | bytes 1179656 | tf_op jit(solution)/shard_map/ppermute | solution.py:574
  55.4 9.0 %collective-permute-start.19 = (bf16[256,768]{1,0:T(8,128)(2,1)S(1)}, bf16[256,768]{1,0:T(8,128)(2,1)S(1)}, u32[]{:S(2)}, u32[]{:S(2)}) collective-permute-start(bf16[256,768]{1,0:T(8,128)(2,1)S(1)} %collective-permute-done.15.x1), channel_id=1, source_target_pairs={{0,8},{1,25},{8,16},{9,1},{16,24},{17,9},{24,0},{25,17},{2,10},{3,... | collective-permute-start | bytes 1179656 | tf_op jit(solution)/shard_map/ppermute | solution.py:579
  55.8 8.6 %collective-permute-start.24 = (bf16[256,768]{1,0:T(8,128)(2,1)S(1)}, bf16[256,768]{1,0:T(8,128)(2,1)S(1)}, u32[]{:S(2)}, u32[]{:S(2)}) collective-permute-start(bf16[256,768]{1,0:T(8,128)(2,1)S(1)} %collective-permute-done.18.y3), channel_id=1, source_target_pairs={{0,1},{1,0},{2,3},{3,2},{4,5},{5,4},{6,7},{7,6},{8,9},{9,8},{10,11... | collective-permute-start | bytes 1179656 | tf_op jit(solution)/shard_map/ppermute | solution.py:574
  62.7 1.7 %collective-permute-start.23 = (bf16[256,768]{1,0:T(8,128)(2,1)S(1)}, bf16[256,768]{1,0:T(8,128)(2,1)S(1)}, u32[]{:S(2)}, u32[]{:S(2)}) collective-permute-start(bf16[256,768]{1,0:T(8,128)(2,1)S(1)} %collective-permute-done.20.y2), channel_id=1, source_target_pairs={{0,1},{1,0},{2,3},{3,2},{4,5},{5,4},{6,7},{7,6},{8,9},{9,8},{10,11... | collective-permute-start | bytes 1179656 | tf_op jit(solution)/shard_map/ppermute | solution.py:574
  71.7 3.8 %collective-permute-start.27 = (f32[24,128]{1,0:T(8,128)S(1)}, f32[24,128]{1,0:T(8,128)S(1)}, u32[]{:S(2)}, u32[]{:S(2)}) collective-permute-start(f32[24,128]{1,0:T(8,128)S(1)} %get-tuple-element.81.r_0_), channel_id=1, source_target_pairs={{0,6},{1,3},{2,0},{3,5},{4,2},{5,7},{6,4},{7,1},{8,14},{9,11},{10,... | collective-permute-start | bytes 36872 | tf_op jit(solution)/shard_map/ppermute | solution.py:579
  73.8 5.2 %collective-permute-start.26 = (f32[24,128]{1,0:T(8,128)S(1)}, f32[24,128]{1,0:T(8,128)S(1)}, u32[]{:S(2)}, u32[]{:S(2)}) collective-permute-start(f32[24,128]{1,0:T(8,128)S(1)} %get-tuple-element.81.r_0_), channel_id=1, source_target_pairs={{0,4},{1,5},{2,6},{3,7},{4,0},{5,1},{6,2},{7,3},{8,12},{9,13},{10,... | collective-permute-start | bytes 36872 | tf_op jit(solution)/shard_map/ppermute | solution.py:579
  74.8 4.9 %collective-permute-start.25 = (f32[24,128]{1,0:T(8,128)S(1)}, f32[24,128]{1,0:T(8,128)S(1)}, u32[]{:S(2)}, u32[]{:S(2)}) collective-permute-start(f32[24,128]{1,0:T(8,128)S(1)} %get-tuple-element.81.r_0_), channel_id=1, source_target_pairs={{0,2},{1,7},{2,4},{3,1},{4,6},{5,3},{6,0},{7,5},{8,10},{9,15},{10,... | collective-permute-start | bytes 36872 | tf_op jit(solution)/shard_map/ppermute | solution.py:579
  79.8 1.3 collective-permute-start.28
  82.4 3.8 %collective-permute-start.31 = (f32[32,128]{1,0:T(8,128)S(1)}, f32[32,128]{1,0:T(8,128)S(1)}, u32[]{:S(2)}, u32[]{:S(2)}) collective-permute-start(f32[32,128]{1,0:T(8,128)S(1)} %get-tuple-element.88.p0), channel_id=1, source_target_pairs={{0,24},{1,9},{8,0},{9,17},{16,8},{17,25},{24,16},{25,1},{2,26},{3,... | collective-permute-start | bytes 49160 | tf_op jit(solution)/shard_map/ppermute | solution.py:579
  83.6 5.2 %collective-permute-start.30 = (f32[32,128]{1,0:T(8,128)S(1)}, f32[32,128]{1,0:T(8,128)S(1)}, u32[]{:S(2)}, u32[]{:S(2)}) collective-permute-start(f32[32,128]{1,0:T(8,128)S(1)} %get-tuple-element.88.p0), channel_id=1, source_target_pairs={{0,16},{1,17},{8,24},{9,25},{16,0},{17,1},{24,8},{25,9},{2,18},{3,... | collective-permute-start | bytes 49160 | tf_op jit(solution)/shard_map/ppermute | solution.py:579
  83.9 5.1 %collective-permute-start.29 = (f32[32,128]{1,0:T(8,128)S(1)}, f32[32,128]{1,0:T(8,128)S(1)}, u32[]{:S(2)}, u32[]{:S(2)}) collective-permute-start(f32[32,128]{1,0:T(8,128)S(1)} %get-tuple-element.88.p0), channel_id=1, source_target_pairs={{0,8},{1,25},{8,16},{9,1},{16,24},{17,9},{24,0},{25,17},{2,10},{3,... | collective-permute-start | bytes 49160 | tf_op jit(solution)/shard_map/ppermute | solution.py:579
  92.2 3.9 %collective-permute-start.34 = (f32[40,128]{1,0:T(8,128)S(1)}, f32[40,128]{1,0:T(8,128)S(1)}, u32[]{:S(2)}, u32[]{:S(2)}) collective-permute-start(f32[40,128]{1,0:T(8,128)S(1)} %get-tuple-element.93.r_0_), channel_id=1, source_target_pairs={{0,6},{1,3},{2,0},{3,5},{4,2},{5,7},{6,4},{7,1},{8,14},{9,11},{10,... | collective-permute-start | bytes 61448 | tf_op jit(solution)/shard_map/ppermute | solution.py:579
  93.6 5.3 %collective-permute-start.33 = (f32[40,128]{1,0:T(8,128)S(1)}, f32[40,128]{1,0:T(8,128)S(1)}, u32[]{:S(2)}, u32[]{:S(2)}) collective-permute-start(f32[40,128]{1,0:T(8,128)S(1)} %get-tuple-element.93.r_0_), channel_id=1, source_target_pairs={{0,4},{1,5},{2,6},{3,7},{4,0},{5,1},{6,2},{7,3},{8,12},{9,13},{10,... | collective-permute-start | bytes 61448 | tf_op jit(solution)/shard_map/ppermute | solution.py:579
  94.5 5.0 %collective-permute-start.32 = (f32[40,128]{1,0:T(8,128)S(1)}, f32[40,128]{1,0:T(8,128)S(1)}, u32[]{:S(2)}, u32[]{:S(2)}) collective-permute-start(f32[40,128]{1,0:T(8,128)S(1)} %get-tuple-element.93.r_0_), channel_id=1, source_target_pairs={{0,2},{1,7},{2,4},{3,1},{4,6},{5,3},{6,0},{7,5},{8,10},{9,15},{10,... | collective-permute-start | bytes 61448 | tf_op jit(solution)/shard_map/ppermute | solution.py:579
  99.6 1.3 collective-permute-start.35
  104.5 3.8 %collective-permute-start.38 = (f32[24,128]{1,0:T(8,128)S(1)}, f32[24,128]{1,0:T(8,128)S(1)}, u32[]{:S(2)}, u32[]{:S(2)}) collective-permute-start(f32[24,128]{1,0:T(8,128)S(1)} %step4.1.p0), channel_id=1, source_target_pairs={{0,24},{1,9},{8,0},{9,17},{16,8},{17,25},{24,16},{25,1},{2,26},{3,... | collective-permute-start | bytes 36872 | tf_op jit(solution)/shard_map/ppermute | solution.py:579
  105.7 5.2 %collective-permute-start.37 = (f32[24,128]{1,0:T(8,128)S(1)}, f32[24,128]{1,0:T(8,128)S(1)}, u32[]{:S(2)}, u32[]{:S(2)}) collective-permute-start(f32[24,128]{1,0:T(8,128)S(1)} %step4.1.p0), channel_id=1, source_target_pairs={{0,16},{1,17},{8,24},{9,25},{16,0},{17,1},{24,8},{25,9},{2,18},{3,... | collective-permute-start | bytes 36872 | tf_op jit(solution)/shard_map/ppermute | solution.py:579
  106.7 4.9 %collective-permute-start.36 = (f32[24,128]{1,0:T(8,128)S(1)}, f32[24,128]{1,0:T(8,128)S(1)}, u32[]{:S(2)}, u32[]{:S(2)}) collective-permute-start(f32[24,128]{1,0:T(8,128)S(1)} %step4.1.p0), channel_id=1, source_target_pairs={{0,8},{1,25},{8,16},{9,1},{16,24},{17,9},{24,0},{25,17},{2,10},{3,... | collective-permute-start | bytes 36872 | tf_op jit(solution)/shard_map/ppermute | solution.py:579
  114.0 3.8 %collective-permute-start.41 = (f32[24,128]{1,0:T(8,128)S(1)}, f32[24,128]{1,0:T(8,128)S(1)}, u32[]{:S(2)}, u32[]{:S(2)}) collective-permute-start(f32[24,128]{1,0:T(8,128)S(1)} %get-tuple-element.97.r_0_), channel_id=1, source_target_pairs={{0,6},{1,3},{2,0},{3,5},{4,2},{5,7},{6,4},{7,1},{8,14},{9,11},{10,... | collective-permute-start | bytes 36872 | tf_op jit(solution)/shard_map/ppermute | solution.py:579
  116.1 5.2 %collective-permute-start.40 = (f32[24,128]{1,0:T(8,128)S(1)}, f32[24,128]{1,0:T(8,128)S(1)}, u32[]{:S(2)}, u32[]{:S(2)}) collective-permute-start(f32[24,128]{1,0:T(8,128)S(1)} %get-tuple-element.97.r_0_), channel_id=1, source_target_pairs={{0,4},{1,5},{2,6},{3,7},{4,0},{5,1},{6,2},{7,3},{8,12},{9,13},{10,... | collective-permute-start | bytes 36872 | tf_op jit(solution)/shard_map/ppermute | solution.py:579
  117.0 4.9 %collective-permute-start.39 = (f32[24,128]{1,0:T(8,128)S(1)}, f32[24,128]{1,0:T(8,128)S(1)}, u32[]{:S(2)}, u32[]{:S(2)}) collective-permute-start(f32[24,128]{1,0:T(8,128)S(1)} %get-tuple-element.97.r_0_), channel_id=1, source_target_pairs={{0,2},{1,7},{2,4},{3,1},{4,6},{5,3},{6,0},{7,5},{8,10},{9,15},{10,... | collective-permute-start | bytes 36872 | tf_op jit(solution)/shard_map/ppermute | solution.py:579
  121.9 1.3 collective-permute-start.42
  126.0 3.7 %collective-permute-start.45 = (f32[16,128]{1,0:T(8,128)S(1)}, f32[16,128]{1,0:T(8,128)S(1)}, u32[]{:S(2)}, u32[]{:S(2)}) collective-permute-start(f32[16,128]{1,0:T(8,128)S(1)} %get-tuple-element.98.p0), channel_id=1, source_target_pairs={{0,24},{1,9},{8,0},{9,17},{16,8},{17,25},{24,16},{25,1},{2,26},{3,... | collective-permute-start | bytes 24584 | tf_op jit(solution)/shard_map/ppermute | solution.py:579
  126.7 5.2 %collective-permute-start.44 = (f32[16,128]{1,0:T(8,128)S(1)}, f32[16,128]{1,0:T(8,128)S(1)}, u32[]{:S(2)}, u32[]{:S(2)}) collective-permute-start(f32[16,128]{1,0:T(8,128)S(1)} %get-tuple-element.98.p0), channel_id=1, source_target_pairs={{0,16},{1,17},{8,24},{9,25},{16,0},{17,1},{24,8},{25,9},{2,18},{3,... | collective-permute-start | bytes 24584 | tf_op jit(solution)/shard_map/ppermute | solution.py:579
  127.6 4.9 %collective-permute-start.43 = (f32[16,128]{1,0:T(8,128)S(1)}, f32[16,128]{1,0:T(8,128)S(1)}, u32[]{:S(2)}, u32[]{:S(2)}) collective-permute-start(f32[16,128]{1,0:T(8,128)S(1)} %get-tuple-element.98.p0), channel_id=1, source_target_pairs={{0,8},{1,25},{8,16},{9,1},{16,24},{17,9},{24,0},{25,17},{2,10},{3,... | collective-permute-start | bytes 24584 | tf_op jit(solution)/shard_map/ppermute | solution.py:579
